TPU v7x, 32 devices: a whole 2x2x4 slice. The times are simulated.
32 devices in a mesh: groups: 2 (over y), batch: 4 (over z), tensor: 4 (over x, core).
Axes of the slice: x: 2, y: 2, z: 4, core: 2. Of those that a mesh axis runs over, the one named last changes fastest.
Arguments:
- session_head_state: bfloat16 [128, 64, 64, 128], P(('groups', 'batch'), 'tensor'), parts along dimension 0, may hold values from -4 to 4
- convolved_activation: bfloat16 [2, 128, 4096], P(None, ('groups', 'batch'), 'tensor'), parts along dimension 1, may hold values from -6 to 6
- gate_activations: bfloat16 [2, 128, 4096], P(None, ('groups', 'batch'), 'tensor'), parts along dimension 1, may hold values from -6 to 6
- state_input_projection: bfloat16 [2, 128, 4, 128], P(None, ('groups', 'batch')), parts along dimension 1, may hold values from -6 to 6
- state_output_projection: bfloat16 [2, 128, 4, 128], P(None, ('groups', 'batch')), parts along dimension 1, may hold values from -6 to 6
- raw_step_sizes: float32 [2, 128, 64], P(None, ('groups', 'batch'), 'tensor'), parts along dimension 1, may hold values from -3 to 3
- step_size_bias: float32 [64], P('tensor'), may hold values from -4 to -1
- log_decay_rate: float32 [64], P('tensor'), may hold values from 0 to 3
- skip_coefficient: float32 [64], P('tensor'), may hold values from 0.5 to 2
- group_norm_gain: bfloat16 [4096], P('tensor'), may hold values from 0.5 to 1.5
- adapter_down_weight: bfloat16 [16, 64, 4096], P(('groups', 'batch'), None, 'tensor'), parts along dimension 0, may hold values from -0.09375 to 0.09375
- adapter_up_weight: bfloat16 [16, 64, 4096], P(('groups', 'batch'), None, 'tensor'), parts along dimension 0, may hold values from -0.75 to 0.75
- adapter_per_session: int32 [128], P(('groups', 'batch')), parts along dimension 0, may hold values from 0 to 7, as said below
- adapter_storage_slot: int32 [16], P('groups'), parts along dimension 0, may hold values from 0 to 7, as said below
Outputs:
- updated_state: bfloat16 [128, 64, 64, 128], P(('groups', 'batch'), 'tensor'), parts along dimension 0
- normed: bfloat16 [2, 128, 4096], P(None, ('groups', 'batch'), 'tensor'), parts along dimension 1
- adapter_output_term: float32 [2, 128, 4096], P(None, ('groups', 'batch'), 'tensor'), parts along dimension 1
There are 2 independent parts, one for each index of `groups`. A program takes and returns all parts, laid end to end along the dimension named above; an argument that names none is the same for every part. Nothing has to cross between parts.
Inputs may be any that keep to these rules, and one draw needn't show every extreme that they name: A permutation: adapter a is stored in slot adapter_storage_slot[a] of adapter_down_weight and adapter_up_weight, held by batch index adapter_storage_slot[a] // 2. `adapter_per_session`: the sessions of one batch index use adapters of one owner at most 4 times; in every draw one owner is used exactly 4 times by the sessions of every batch index.
All inputs are finite; a program needn't handle non-finite values.
Results may differ from a plain program's by a relative error of at most 0.0053.
Values may be sent and summed in bfloat16 or wider, within the bound.
No kernel may reach another device: no remote copies, remote signals or barrier semaphores. Data moves between devices by JAX's collectives and lax.ppermute only.
A program may use at most 64 MiB of HBM per device.

v0:
```python
import jax
import jax.numpy as jnp
from jax import lax
from jax.sharding import PartitionSpec as P

HEAD_COUNT = 64
HEAD_CHANNELS = 64
GROUPS = 4
DECODE_STEPS = 2
ADP_DEV = 2


adapter_scale = 2.0
norm_eps = 1e-05


def per_device(
    session_head_state,
    convolved_activation,
    gate_activations,
    state_input_projection,
    state_output_projection,
    raw_step_sizes,
    step_size_bias,
    log_decay_rate,
    skip_coefficient,
    group_norm_gain,
    adapter_down_weight,
    adapter_up_weight,
    adapter_per_session,
    adapter_storage_slot,
):
    highest_precision = lax.Precision.HIGHEST
    sessions = session_head_state.shape[0]
    local_heads = session_head_state.shape[1]
    channels = local_heads * HEAD_CHANNELS
    head_ids = lax.axis_index("tensor") * local_heads + jnp.arange(local_heads, dtype=jnp.int32)
    group_lookup = (
        (head_ids // (HEAD_COUNT // GROUPS))[:, None]
        == jnp.arange(GROUPS, dtype=jnp.int32)[None, :]
    ).astype(jnp.float32)
    gain = group_norm_gain.astype(jnp.float32).reshape(local_heads, HEAD_CHANNELS)
    carried = session_head_state.astype(jnp.float32)
    batch_count = lax.axis_size("batch")
    capacity = max(2, (sessions + batch_count - 1) // batch_count)
    adapter_count = adapter_storage_slot.shape[0]
    slots = jnp.sum(
        jnp.where(
            adapter_per_session[:, None] == jnp.arange(adapter_count, dtype=jnp.int32)[None, :],
            adapter_storage_slot[None, :],
            0,
        ),
        axis=1,
    )
    owners = slots // ADP_DEV
    position = jnp.arange(sessions, dtype=jnp.int32)
    earlier = jnp.sum(
        ((owners[:, None] == owners[None, :]) & (position[None, :] < position[:, None])).astype(
            jnp.int32
        ),
        axis=1,
    )
    adapter_pick = (
        (slots % ADP_DEV)[:, None] == jnp.arange(ADP_DEV, dtype=jnp.int32)[None, :]
    ).astype(jnp.bfloat16)
    normed_steps = []
    delta_steps = []
    rounded = session_head_state
    for step_index in range(DECODE_STEPS):
        step_size = jax.nn.softplus(raw_step_sizes[step_index] + step_size_bias)
        decays = jnp.exp(-jnp.exp(log_decay_rate) * step_size)
        b_heads = jnp.einsum(
            "sgn,hg->shn",
            state_input_projection[step_index].astype(jnp.float32),
            group_lookup,
            precision=highest_precision,
        )
        c_heads = jnp.einsum(
            "sgn,hg->shn",
            state_output_projection[step_index].astype(jnp.float32),
            group_lookup,
            precision=highest_precision,
        )
        inputs = (
            convolved_activation[step_index]
            .astype(jnp.float32)
            .reshape(sessions, local_heads, HEAD_CHANNELS)
        )
        carried = (
            decays[:, :, None, None] * carried
            + (step_size[:, :, None] * inputs)[:, :, :, None] * b_heads[:, :, None, :]
        )
        outputs = (
            jnp.einsum("shpn,shn->shp", carried, c_heads, precision=highest_precision)
            + skip_coefficient[None, :, None] * inputs
        )
        gated_out = outputs * jax.nn.silu(
            gate_activations[step_index]
            .astype(jnp.float32)
            .reshape(sessions, local_heads, HEAD_CHANNELS)
        )
        squares = jnp.sum(gated_out * gated_out, axis=(1, 2))
        totals = lax.psum(squares, "tensor")
        inverse = lax.rsqrt(totals / (HEAD_COUNT * HEAD_CHANNELS) + norm_eps)
        normalized_rows = (
            (gated_out * inverse[:, None, None] * gain)
            .reshape(sessions, channels)
            .astype(jnp.bfloat16)
        )
        normed_steps.append(normalized_rows)
        target = owners * capacity + 0 + earlier
        lookup = (
            target[:, None] == jnp.arange(batch_count * capacity, dtype=jnp.int32)[None, :]
        ).astype(jnp.float32)
        lookups = [lookup]
        normed_list = [normalized_rows]
        row_sum = jnp.zeros((lookups[0].shape[1], channels), jnp.float32)
        pick_sum = jnp.zeros((lookups[0].shape[1], ADP_DEV), jnp.float32)
        for pack_lookup, pack_normalized_rows in zip(lookups, normed_list):
            spread = pack_lookup.T.astype(jnp.bfloat16)
            row_sum = jnp.dot(spread, pack_normalized_rows, preferred_element_type=jnp.float32)
            pick_sum = jnp.dot(spread, adapter_pick, preferred_element_type=jnp.float32)
        row_pack = row_sum.astype(jnp.bfloat16).reshape(batch_count, -1, channels)
        pick_pack = pick_sum.astype(jnp.bfloat16).reshape(batch_count, -1, ADP_DEV)
        session_row_block = lax.all_to_all(
            row_pack, "batch", split_axis=0, concat_axis=0, tiled=True
        )
        pick_block = lax.all_to_all(pick_pack, "batch", split_axis=0, concat_axis=0, tiled=True)
        selected_adapters = pick_block.astype(jnp.float32)
        projected = jnp.einsum(
            "uyl,nil->uyni",
            session_row_block,
            adapter_down_weight,
            preferred_element_type=jnp.float32,
        )
        partial_rank = jnp.einsum(
            "skaq,ska->skq", projected, selected_adapters, precision=highest_precision
        )
        rank_projected_rows = lax.psum(partial_rank, "tensor").astype(jnp.bfloat16)
        broadcast_rows = jnp.einsum(
            "cyg,hgf->cyhf",
            rank_projected_rows,
            adapter_up_weight,
            preferred_element_type=jnp.float32,
        )
        step_deltas = adapter_scale * jnp.einsum(
            "wfor,wfo->wfr", broadcast_rows, selected_adapters, precision=highest_precision
        )
        returned = lax.all_to_all(step_deltas, "batch", split_axis=0, concat_axis=0, tiled=True)
        flat = returned.reshape(-1, returned.shape[2])
        delta_steps.append(jnp.dot(lookup, flat, precision=highest_precision))
        rounded = lax.optimization_barrier(carried.astype(jnp.bfloat16))
        carried = rounded.astype(jnp.float32)
    return (rounded, jnp.stack(normed_steps), jnp.stack(delta_steps))


def solution(mesh):
    placed = (
        P(("groups", "batch"), "tensor", None, None),
        P(None, ("groups", "batch"), "tensor"),
        P(None, ("groups", "batch"), "tensor"),
        P(None, ("groups", "batch"), None, None),
        P(None, ("groups", "batch"), None, None),
        P(None, ("groups", "batch"), "tensor"),
        P("tensor"),
        P("tensor"),
        P("tensor"),
        P("tensor"),
        P(("groups", "batch"), None, "tensor"),
        P(("groups", "batch"), None, "tensor"),
        P(("groups", "batch")),
        P("groups"),
    )
    return jax.shard_map(
        per_device,
        mesh=mesh,
        in_specs=placed,
        out_specs=(
            P(("groups", "batch"), "tensor", None, None),
            P(None, ("groups", "batch"), "tensor"),
            P(None, ("groups", "batch"), "tensor"),
        ),
        check_vma=False,
    )
```

profile of v0, /device:TPU:0, one launch (start us, length us, event | category | flops | bytes accessed | tf_op | source)
XLA Modules:
  0.0 115.5 jit_solution(5158110393477439590)
XLA Ops:
  0.6 0.8 select_reduce_fusion
  2.6 6.3 %all-to-all-start.1 = ((bf16[4,4,2]{1,2,0:T(2,128)(2,1)}), bf16[4,4,2]{1,2,0:T(2,128)(2,1)S(1)}, u32[]{:S(2)}, u32[]{:S(2)}) async-start(bf16[4,4,2]{1,2,0:T(2,128)(2,1)} %copy.18), calls=%async_computation.1 | async-start | bytes 4096 | tf_op jit(solution)/shard_map/all_to_all | solution.py:128
  8.9 0.9 convolution_bitcast_fusion.1
  9.8 0.9 convolution_bitcast_fusion
  10.8 0.9 fusion.24
  11.7 0.9 fusion.26
  12.6 0.7 exponential_negate_fusion
  13.3 0.8 slice_convert_fusion.2
  14.3 0.8 multiply_exponential_fusion.1
  15.2 6.3 %fusion.3 = bf16[16,16,64,128]{3,2,1,0:T(8,128)(2,1)} fusion(bf16[16,16,64,128]{3,2,1,0:T(8,128)(2,1)} %param.14, f32[16,16,128]{2,1,0:T(8,128)S(1)} %convolution_bitcast_fusion.1, f32[16,16,64]{2,1,0:T(8,128)S(1)} %get-tuple-element.28, f32[16,16]{1,0:T(8,128)S(1)} %get-tuple-element.19), kind=kLoop, calls=%fused_computation.5 | loop fusion | flops 10485760 | bytes 8586240 | tf_op jit(solution)/shard_map/convert_element_type | solution.py:152
  21.5 13.7 %fusion.2 = f32[16,16,1,64]{3,2,1,0:T(1,128)S(1)} fusion(f32[16,16,128,1]{2,3,1,0:T(1,128)S(1)} %bitcast.104, bf16[16,16,64,128]{3,2,1,0:T(8,128)(2,1)S(1)} %copy-done.1, f32[16,16,128]{2,1,0:T(8,128)S(1)} %convolution_bitcast_fusion.1, f32[16,16,64]{2,1,0:T(8,128)S(1)} %get-tuple-element.28, f32[16,16]{1,0:T(8,128)S(1)} %get-tuple-element.19), kind=kOutput, calls=%fused_computation.4 | convolution fusion | flops 33554432 | bytes 4588544 | tf_op jit(solution)/shard_map/shpn,shn->shp/dot_general | solution.py:94
  35.4 15.7 %fusion = f32[16,16,1,64]{3,2,1,0:T(1,128)S(1)} fusion(f32[16,16,128,1]{2,3,1,0:T(1,128)S(1)} %bitcast.103, bf16[16,16,64,128]{3,2,1,0:T(8,128)(2,1)} %fusion.3, f32[16,16,128]{2,1,0:T(8,128)S(1)} %convolution_bitcast_fusion, f32[16,16,64]{2,1,0:T(8,128)S(1)} %get-tuple-element.27, f32[16,16]{1,0:T(8,128)S(1)} %get-tuple-element.11), kind=kOutput, calls=%fused_computation.1 | convolution fusion | flops 33554432 | bytes 4588544 | tf_op jit(solution)/shard_map/shpn,shn->shp/dot_general | solution.py:94
  51.4 6.3 %all-reduce.1 = (f32[16]{0:T(128)S(1)}, f32[16]{0:T(128)S(1)}) all-reduce(f32[16]{0:T(128)S(1)} %get-tuple-element.25, f32[16]{0:T(128)S(1)} %get-tuple-element.7), channel_id=1, replica_groups=mesh['groups'=2,'batch'=4,'tensor'=4] {'tensor'}, use_global_device_ids=true, to_apply=%region_3.4 | all-reduce | flops 32 | bytes 256 | tf_op jit(solution)/shard_map/psum | solution.py:103
  58.4 6.1 %fusion.1 = bf16[16,16,64,128]{3,2,1,0:T(8,128)(2,1)} fusion(bf16[16,16,64,128]{3,2,1,0:T(8,128)(2,1)} %fusion.3, f32[16,16,128]{2,1,0:T(8,128)S(1)} %convolution_bitcast_fusion, f32[16,16,64]{2,1,0:T(8,128)S(1)} %get-tuple-element.27, f32[16,16]{1,0:T(8,128)S(1)} %get-tuple-element.11), kind=kLoop, calls=%fused_computation.2 | loop fusion | flops 10485760 | bytes 8586240 | tf_op jit(solution)/shard_map/convert_element_type | solution.py:152
  65.4 4.8 %all-to-all-start = ((bf16[4,4,1024]{2,1,0:T(4,128)(2,1)}), bf16[4,4,1024]{2,1,0:T(4,128)(2,1)S(1)}, u32[]{:S(2)}, u32[]{:S(2)}) async-start(bf16[4,4,1024]{2,1,0:T(4,128)(2,1)} %reshape.270), calls=%async_computation | async-start | bytes 65536 | tf_op jit(solution)/shard_map/all_to_all | solution.py:125
  71.6 4.2 %all-to-all-done = bf16[4,4,1024]{2,1,0:T(4,128)(2,1)S(1)} async-done(((bf16[4,4,1024]{2,1,0:T(4,128)(2,1)}), bf16[4,4,1024]{2,1,0:T(4,128)(2,1)S(1)}, u32[]{:S(2)}, u32[]{:S(2)}) %all-to-all-start) | async-done | bytes 32800 | tf_op jit(solution)/shard_map/all_to_all | solution.py:125
  75.8 3.3 %all-to-all-start.3 = ((bf16[4,4,1024]{2,1,0:T(4,128)(2,1)}), bf16[4,4,1024]{2,1,0:T(4,128)(2,1)S(1)}, u32[]{:S(2)}, u32[]{:S(2)}) async-start(bf16[4,4,1024]{2,1,0:T(4,128)(2,1)} %reshape.273), calls=%async_computation.3 | async-start | bytes 65536 | tf_op jit(solution)/shard_map/all_to_all | solution.py:125
  79.5 5.2 %all-to-all-done.3 = bf16[4,4,1024]{2,1,0:T(4,128)(2,1)S(1)} async-done(((bf16[4,4,1024]{2,1,0:T(4,128)(2,1)}), bf16[4,4,1024]{2,1,0:T(4,128)(2,1)S(1)}, u32[]{:S(2)}, u32[]{:S(2)}) %all-to-all-start.3) | async-done | bytes 32800 | tf_op jit(solution)/shard_map/all_to_all | solution.py:125
  85.1 10.2 %all-reduce = (bf16[4,4,64]{2,1,0:T(4,128)(2,1)S(1)}, bf16[4,4,64]{2,1,0:T(4,128)(2,1)S(1)}) all-reduce(f32[4,4,64]{2,1,0:T(4,128)S(1)} %bitcast.107, f32[4,4,64]{2,1,0:T(4,128)S(1)} %bitcast.106), channel_id=1, replica_groups=mesh['groups'=2,'batch'=4,'tensor'=4] {'tensor'}, use_global_device_ids=true, to_apply=%region_7.8 | all-reduce | flops 2048 | bytes 12288 | tf_op jit(solution)/shard_map/psum | solution.py:139
  96.5 3.3 %all-to-all-start.2 = ((f32[4,4,1024]{2,1,0:T(4,128)}), f32[4,4,1024]{2,1,0:T(4,128)S(1)}, u32[]{:S(2)}, u32[]{:S(2)}) async-start(f32[4,4,1024]{2,1,0:T(4,128)} %bitcast_multiply_fusion.1), calls=%async_computation.2 | async-start | bytes 131072 | tf_op jit(solution)/shard_map/all_to_all | solution.py:149
  101.1 4.5 %all-to-all-done.2 = f32[4,4,1024]{2,1,0:T(4,128)S(1)} async-done(((f32[4,4,1024]{2,1,0:T(4,128)}), f32[4,4,1024]{2,1,0:T(4,128)S(1)}, u32[]{:S(2)}, u32[]{:S(2)}) %all-to-all-start.2) | async-done | bytes 65568 | tf_op jit(solution)/shard_map/all_to_all | solution.py:149
  105.5 3.3 %all-to-all-start.4 = ((f32[4,4,1024]{2,1,0:T(4,128)}), f32[4,4,1024]{2,1,0:T(4,128)S(1)}, u32[]{:S(2)}, u32[]{:S(2)}) async-start(f32[4,4,1024]{2,1,0:T(4,128)} %bitcast_multiply_fusion), calls=%async_computation.4 | async-start | bytes 131072 | tf_op jit(solution)/shard_map/all_to_all | solution.py:149
  109.1 5.5 %all-to-all-done.4 = f32[4,4,1024]{2,1,0:T(4,128)S(1)} async-done(((f32[4,4,1024]{2,1,0:T(4,128)}), f32[4,4,1024]{2,1,0:T(4,128)S(1)}, u32[]{:S(2)}, u32[]{:S(2)}) %all-to-all-start.4) | async-done | bytes 65568 | tf_op jit(solution)/shard_map/all_to_all | solution.py:149
  114.8 0.7 pad_maximum_fusion
  (55 shorter events, 8.6 us)
Async XLA Ops:
  0.6 94.7 %copy-start = (bf16[2,64,1024]{2,1,0:T(8,128)(2,1)S(1)}, bf16[2,64,1024]{2,1,0:T(8,128)(2,1)}, u32[]{:S(2)}) copy-start(bf16[2,64,1024]{2,1,0:T(8,128)(2,1)} %param.25) | copy-start | bytes 786436
  2.6 62.8 %all-to-all-start.1 = ((bf16[4,4,2]{1,2,0:T(2,128)(2,1)}), bf16[4,4,2]{1,2,0:T(2,128)(2,1)S(1)}, u32[]{:S(2)}, u32[]{:S(2)}) async-start(bf16[4,4,2]{1,2,0:T(2,128)(2,1)} %copy.18), calls=%async_computation.1 | async-start | bytes 4096 | tf_op jit(solution)/shard_map/all_to_all | solution.py:128
  15.2 6.3 %copy-start.1 = (bf16[16,16,64,128]{3,2,1,0:T(8,128)(2,1)S(1)}, bf16[16,16,64,128]{3,2,1,0:T(8,128)(2,1)}, u32[]{:S(2)}) copy-start(bf16[16,16,64,128]{3,2,1,0:T(8,128)(2,1)} %param.14) | copy-start | bytes 12582916
  21.5 13.7 %copy-start.3 = (bf16[2,16,1024]{2,1,0:T(8,128)(2,1)S(1)}, bf16[2,16,1024]{2,1,0:T(8,128)(2,1)}, u32[]{:S(2)}) copy-start(bf16[2,16,1024]{2,1,0:T(8,128)(2,1)} %param.16) | copy-start | bytes 196612
  35.4 15.7 %copy-start.5 = (f32[16]{0:T(128)S(1)}, f32[16]{0:T(128)}, u32[]{:S(2)}) copy-start(f32[16]{0:T(128)} %param.22) | copy-start | bytes 196
  35.4 22.3 %copy-start.4 = (bf16[1024]{0:T(1024)(128)(2,1)S(1)}, bf16[1024]{0:T(1024)(128)(2,1)}, u32[]{:S(2)}) copy-start(bf16[1024]{0:T(1024)(128)(2,1)} %param.23) | copy-start | bytes 6148
  58.3 20.8 %copy-start.2 = (bf16[2,64,1024]{2,1,0:T(8,128)(2,1)S(1)}, bf16[2,64,1024]{2,1,0:T(8,128)(2,1)}, u32[]{:S(2)}) copy-start(bf16[2,64,1024]{2,1,0:T(8,128)(2,1)} %param.24) | copy-start | bytes 786436
  65.4 10.5 %all-to-all-start = ((bf16[4,4,1024]{2,1,0:T(4,128)(2,1)}), bf16[4,4,1024]{2,1,0:T(4,128)(2,1)S(1)}, u32[]{:S(2)}, u32[]{:S(2)}) async-start(bf16[4,4,1024]{2,1,0:T(4,128)(2,1)} %reshape.270), calls=%async_computation | async-start | bytes 65536 | tf_op jit(solution)/shard_map/all_to_all | solution.py:125
  75.8 8.9 %all-to-all-start.3 = ((bf16[4,4,1024]{2,1,0:T(4,128)(2,1)}), bf16[4,4,1024]{2,1,0:T(4,128)(2,1)S(1)}, u32[]{:S(2)}, u32[]{:S(2)}) async-start(bf16[4,4,1024]{2,1,0:T(4,128)(2,1)} %reshape.273), calls=%async_computation.3 | async-start | bytes 65536 | tf_op jit(solution)/shard_map/all_to_all | solution.py:125
  96.5 9.0 %all-to-all-start.2 = ((f32[4,4,1024]{2,1,0:T(4,128)}), f32[4,4,1024]{2,1,0:T(4,128)S(1)}, u32[]{:S(2)}, u32[]{:S(2)}) async-start(f32[4,4,1024]{2,1,0:T(4,128)} %bitcast_multiply_fusion.1), calls=%async_computation.2 | async-start | bytes 131072 | tf_op jit(solution)/shard_map/all_to_all | solution.py:149
  105.5 9.0 %all-to-all-start.4 = ((f32[4,4,1024]{2,1,0:T(4,128)}), f32[4,4,1024]{2,1,0:T(4,128)S(1)}, u32[]{:S(2)}, u32[]{:S(2)}) async-start(f32[4,4,1024]{2,1,0:T(4,128)} %bitcast_multiply_fusion), calls=%async_computation.4 | async-start | bytes 131072 | tf_op jit(solution)/shard_map/all_to_all | solution.py:149
where the time goes:
time: 117 us; the launch traced here: 115 us
  matrix products  36 us (31%)
  starting transfers between devices  21 us (18%)
  waiting for transfers between devices  19.4 us (17%)
  other arithmetic  18.8 us (16%)
  blocking collectives  16.5 us (14%)
  local copies, waits for them, and re-layouts  3.02 us (3%)
    dot_general x2, matrix products, per_device(): jnp.einsum('shpn,shn->shp', carried, c_heads, precision=highest_precision)  29.4 us
    convert_element_type x2, other arithmetic, per_device(): rounded = lax.optimization_barrier(carried.astype(jnp.bfloat16))  12.4 us
    psum x1, blocking collectives, per_device(): rank_projected_rows = lax.psum(partial_rank, 'tensor').astype(jnp.bfloat16)  10.2 us
    all_to_all x2, waiting for transfers between devices, per_device(): lax.all_to_all(step_deltas, 'batch', split_axis=0, concat_axis=0, tiled=T...  9.93 us
    all_to_all x2, waiting for transfers between devices, per_device(): lax.all_to_all(row_pack, 'batch', split_axis=0, concat_axis=0, tiled=True)  9.43 us
    all_to_all x2, starting transfers between devices, per_device(): lax.all_to_all(row_pack, 'batch', split_axis=0, concat_axis=0, tiled=True)  8.08 us
    all_to_all x2, starting transfers between devices, per_device(): lax.all_to_all(step_deltas, 'batch', split_axis=0, concat_axis=0, tiled=T...  6.57 us
    all_to_all x1, starting transfers between devices, per_device(): lax.all_to_all(pick_pack, 'batch', split_axis=0, concat_axis=0, tiled=True)  6.32 us
  transfers between devices with their start and end apart: 5, of which 4 were waited for; matrix products, arithmetic and copies ran while one was open for 46% of the time, Pallas kernels for 0%

commit v1 on v0

v1 whole, which is shorter than its diff:
```python
import functools

import jax
import jax.numpy as jnp
from jax import lax
from jax.experimental import pallas as pl
from jax.experimental.pallas import tpu as pltpu
from jax.sharding import PartitionSpec as P

HEAD_COUNT = 64
HEAD_CHANNELS = 64
GROUPS = 4
DECODE_STEPS = 2
RANK = 64
LANES = 128

adapter_scale = 2.0
norm_eps = 1e-05

F32 = jnp.float32
BF16 = jnp.bfloat16
HIGHEST = lax.Precision.HIGHEST
NT = (((1,), (1,)), ((), ()))


def iota(shape, axis):
    return lax.broadcasted_iota(jnp.int32, shape, axis)


def front_kernel(dims, *refs):
    sessions, heads, batch_count, capacity, adapters_held, chunks, split = dims
    (ids, adapter, slot_of, state, x, z, b, c, raw, bias, rate, skip, gain) = refs[:13]
    n_msg = batch_count if split else 1
    msgs = refs[13 : 13 + n_msg]
    gated_ref, square_ref, drive_ref, b_ref, keep_ref, place_ref = refs[13 + n_msg : 19 + n_msg]
    held, sems, counts = refs[19 + n_msg :]
    channels = heads * HEAD_CHANNELS
    rows = DECODE_STEPS * sessions
    part = heads // chunks
    width = part * HEAD_CHANNELS

    copies = []
    for i in range(chunks):
        window = pl.ds(i * part, part)
        copy = pltpu.make_async_copy(state.at[:, window], held.at[:, window], sems.at[i])
        copy.start()
        copies.append(copy)

    me = ids[0]
    group = ids[1]
    for i in range(batch_count):
        counts[i] = 0
    per_owner = DECODE_STEPS * capacity
    targets = batch_count * per_owner
    to = iota((targets, rows), 0)
    source = iota((targets, rows), 1)
    lane_to = iota((targets, LANES), 0)
    place = jnp.zeros((targets, rows), F32)
    pick = jnp.zeros((targets, LANES), F32)
    for s in range(sessions):
        slot = slot_of[adapter[s]]
        owner = slot // adapters_held
        which = (slot - owner * adapters_held).astype(F32)
        earlier = counts[owner]
        counts[owner] = earlier + 1
        relative = (owner ^ me) if split else owner
        first = relative * per_owner + earlier * DECODE_STEPS
        hit = (to - first == source // sessions) & (source % sessions == s)
        place = jnp.where(hit, 1.0, place)
        mine = (lane_to >= first) & (lane_to < first + DECODE_STEPS)
        pick = jnp.where(mine, which, pick)
    place_ref[...] = place
    place_bf = place.astype(BF16)

    def pick_group(ref):
        values = ref[...].astype(F32).reshape(rows, GROUPS, LANES)
        return jnp.sum(jnp.where(iota(values.shape, 1) == group, values, 0.0), axis=1)

    b_rows = pick_group(b)
    c_rows = pick_group(c)
    b_ref[...] = b_rows
    b1, b2 = b_rows[:sessions], b_rows[sessions:]
    c1, c2 = c_rows[:sessions], c_rows[sessions:]
    bc11 = jnp.sum(b1 * c1, axis=1, keepdims=True)
    bc12 = jnp.sum(b1 * c2, axis=1, keepdims=True)
    bc22 = jnp.sum(b2 * c2, axis=1, keepdims=True)

    def softplus(v):
        return jnp.maximum(v, 0.0) + jnp.log1p(jnp.exp(-jnp.abs(v)))

    step1 = softplus(raw[0] + bias[...])
    step2 = softplus(raw[1] + bias[...])
    speed = -jnp.exp(rate[...])
    decay1 = jnp.exp(speed * step1)
    decay2 = jnp.exp(speed * step2)
    keep = decay1 * decay2
    keep_ref[...] = keep
    factors = jnp.concatenate(
        [
            decay1,
            step1 * bc11 + skip[...],
            keep,
            decay2 * step1 * bc12,
            step2 * bc22 + skip[...],
            decay2 * step1,
            step2,
        ],
        axis=0,
    )
    spread = (iota((heads, channels), 1) // HEAD_CHANNELS == iota((heads, channels), 0)).astype(F32)
    wide = jnp.dot(factors, spread, precision=HIGHEST, preferred_element_type=F32)
    wide = [wide[i * sessions : (i + 1) * sessions] for i in range(7)]
    x1 = x[0].astype(F32)
    x2 = x[1].astype(F32)
    drive_ref[...] = jnp.concatenate([wide[5] * x1, wide[6] * x2], axis=0)
    base1 = x1 * wide[1]
    base2 = x1 * wide[3] + x2 * wide[4]
    gates = jnp.concatenate([z[0].astype(F32), z[1].astype(F32)], axis=0)
    gates = gates / (1.0 + jnp.exp(-gates))
    base = jnp.concatenate([base1, base2], axis=0)
    scale = jnp.concatenate([wide[0], wide[2]], axis=0)
    row_session = iota((rows, LANES), 0) % sessions
    c_blocks = jnp.concatenate(
        [jnp.where(row_session == s, c_rows, 0.0).astype(BF16) for s in range(sessions)], axis=1
    )
    squares = jnp.zeros((rows, LANES), F32)
    for i in range(chunks):
        copies[i].wait()
        lanes = slice(i * width, (i + 1) * width)
        block = jnp.concatenate(
            [
                held[s, i * part : (i + 1) * part].reshape(width, LANES)
                for s in range(sessions)
            ],
            axis=1,
        )
        reads = lax.dot_general(c_blocks, block, NT, preferred_element_type=F32)
        gated = (scale[:, lanes] * reads + base[:, lanes]) * gates[:, lanes]
        gated_ref[:, lanes] = gated
        for j in range(width // LANES):
            piece = gated[:, j * LANES : (j + 1) * LANES]
            squares = squares + piece * piece
        weighted = (gated * gain[:, lanes].astype(F32)).astype(BF16)
        packed = jnp.dot(place_bf, weighted, preferred_element_type=F32)
        for k in range(n_msg):
            n = targets // n_msg
            msgs[k][:, lanes] = packed[k * n : (k + 1) * n].astype(BF16)
    for k in range(n_msg):
        n = targets // n_msg
        msgs[k][:, channels:] = pick[k * n : (k + 1) * n].astype(BF16)
    square_ref[...] = squares[:, :RANK] + squares[:, RANK:]


def state_kernel(sessions, heads, pair, drive, b, keep, state, out, drive_t):
    i = pl.program_id(0)
    channels = heads * HEAD_CHANNELS
    rows = DECODE_STEPS * sessions

    @pl.when(i == 0)
    def _():
        turned = drive[...].T
        high = turned.astype(BF16)
        low = (turned - high.astype(F32)).astype(BF16)
        drive_t[...] = jnp.concatenate([high, low], axis=1)

    row_session = iota((rows, LANES), 0) % sessions
    b_rows = b[...]
    right = jnp.concatenate(
        [jnp.where(row_session == i * pair + q, b_rows, 0.0) for q in range(pair)], axis=1
    )
    right = jnp.concatenate([right, right], axis=0).astype(BF16)
    for h in range(heads):
        piece = slice(h * HEAD_CHANNELS, (h + 1) * HEAD_CHANNELS)
        added = jnp.dot(drive_t[piece], right, preferred_element_type=F32)
        for q in range(pair):
            kept = state[q, h].astype(F32) * keep[i * pair + q, h]
            out[q, h] = (kept + added[:, q * LANES : (q + 1) * LANES]).astype(BF16)


def down_kernel(n_msg, *refs):
    msgs = refs[:n_msg]
    down, squares, out, pick_ref = refs[n_msg:]
    held, rank, channels = down.shape
    rows = jnp.concatenate([m[...].astype(F32) for m in msgs], axis=0)
    pick = rows[:, channels:]
    weights = down[...].reshape(held * rank, channels)
    ranks = lax.dot_general(
        rows[:, :channels].astype(BF16), weights, NT, preferred_element_type=F32
    )
    chosen = jnp.zeros((rows.shape[0], rank), F32)
    for j in range(held):
        chosen = jnp.where(pick[:, :rank] == j, ranks[:, j * rank : (j + 1) * rank], chosen)
    pick_ref[...] = pick
    n_squares = squares.shape[0]
    if n_squares < chosen.shape[0]:
        filled = jnp.concatenate(
            [squares[...], jnp.zeros((chosen.shape[0] - n_squares, rank), F32)], axis=0
        )
    else:
        filled = squares[...]
    out[...] = jnp.concatenate([chosen, filled], axis=1)


def up_kernel(n_sum, n_msg, sessions, *refs):
    parts = refs[:n_sum]
    pick, up = refs[n_sum : n_sum + 2]
    outs = refs[n_sum + 2 : n_sum + 2 + n_msg]
    inverse = refs[n_sum + 2 + n_msg]
    held, rank, channels = up.shape
    total = parts[0][...]
    for p in parts[1:]:
        total = total + p[...]
    ranks = total[:, :rank]
    left = jnp.concatenate(
        [jnp.where(pick[:, :rank] == j, ranks, 0.0) for j in range(held)], axis=1
    ).astype(BF16)
    terms = adapter_scale * jnp.dot(
        left, up[...].reshape(held * rank, channels), preferred_element_type=F32
    )
    n = terms.shape[0] // n_msg
    for k in range(n_msg):
        outs[k][...] = terms[k * n : (k + 1) * n]
    rows = DECODE_STEPS * sessions
    sums = jnp.sum(total[:rows, rank:], axis=1, keepdims=True)
    factor = lax.rsqrt(sums / (HEAD_COUNT * HEAD_CHANNELS) + norm_eps)
    inverse[...] = jnp.broadcast_to(factor, inverse.shape)


def norm_kernel(gated, inverse, gain, out):
    rows, channels = gated.shape
    normed = gated[...] * inverse[:, :1] * gain[...].astype(F32)
    out[...] = normed.astype(BF16).reshape(out.shape)


def final_kernel(n_msg, *refs):
    msgs = refs[:n_msg]
    place, inverse, out = refs[n_msg:]
    terms = jnp.concatenate([m[...].astype(F32) for m in msgs], axis=0)
    mine = lax.dot_general(
        place[...], terms, (((0,), (0,)), ((), ())), precision=HIGHEST, preferred_element_type=F32
    )
    out[...] = (mine * inverse[:, :1]).reshape(out.shape)


def vmem():
    return pl.BlockSpec(memory_space=pltpu.VMEM)


def smem():
    return pl.BlockSpec(memory_space=pltpu.SMEM)


def shape(dims, dtype):
    return jax.ShapeDtypeStruct(dims, dtype)


def per_device(
    session_head_state,
    convolved_activation,
    gate_activations,
    state_input_projection,
    state_output_projection,
    raw_step_sizes,
    step_size_bias,
    log_decay_rate,
    skip_coefficient,
    group_norm_gain,
    adapter_down_weight,
    adapter_up_weight,
    adapter_per_session,
    adapter_storage_slot,
):
    sessions, heads, _, state_size = session_head_state.shape
    channels = heads * HEAD_CHANNELS
    rows = DECODE_STEPS * sessions
    batch_count = lax.axis_size("batch")
    tensor_count = lax.axis_size("tensor")
    capacity = max(2, (sessions + batch_count - 1) // batch_count)
    held = adapter_down_weight.shape[0]
    split = batch_count in (2, 4)
    per_owner = DECODE_STEPS * capacity
    targets = batch_count * per_owner
    n_msg = batch_count if split else 1
    chunks = 4
    me = lax.axis_index("batch")
    group = lax.axis_index("tensor") * heads // (HEAD_COUNT // GROUPS)
    ids = jnp.stack([me, group]).astype(jnp.int32)
    gain = group_norm_gain.reshape(1, channels)

    msg_rows = targets // n_msg
    dims = (sessions, heads, batch_count, capacity, held, chunks, split)
    out = pl.pallas_call(
        functools.partial(front_kernel, dims),
        out_shape=[shape((msg_rows, channels + LANES), BF16)] * n_msg
        + [
            shape((rows, channels), F32),
            shape((rows, RANK), F32),
            shape((rows, channels), F32),
            shape((rows, LANES), F32),
            shape((sessions, heads), F32),
            shape((targets, rows), F32),
        ],
        in_specs=[smem()] * 3 + [pl.BlockSpec(memory_space=pl.ANY)] + [vmem()] * 9,
        out_specs=[vmem()] * (n_msg + 6),
        scratch_shapes=[
            pltpu.VMEM(session_head_state.shape, BF16),
            pltpu.SemaphoreType.DMA((chunks,)),
            pltpu.SMEM((batch_count,), jnp.int32),
        ],
        compiler_params=pltpu.CompilerParams(vmem_limit_bytes=24 << 20),
        cost_estimate=pl.CostEstimate(
            flops=2 * 32 * session_head_state.size,
            bytes_accessed=2 * session_head_state.size,
            transcendentals=0,
        ),
        name="front",
    )(
        ids,
        adapter_per_session,
        adapter_storage_slot,
        session_head_state,
        convolved_activation,
        gate_activations,
        state_input_projection,
        state_output_projection,
        raw_step_sizes,
        step_size_bias.reshape(1, heads),
        log_decay_rate.reshape(1, heads),
        skip_coefficient.reshape(1, heads),
        gain,
    )
    msgs = out[:n_msg]
    gated, squares, drive, b_rows, keep, place = out[n_msg:]

    def exchange(blocks):
        if split:
            return [blocks[0]] + [
                lax.ppermute(
                    blocks[k], "batch", [(i, i ^ k) for i in range(batch_count)]
                )
                for k in range(1, batch_count)
            ]
        block = blocks[0].reshape(batch_count, per_owner, -1)
        block = lax.all_to_all(block, "batch", split_axis=0, concat_axis=0, tiled=True)
        return [block.reshape(targets, -1)]

    arrived = exchange(msgs)

    pair = 2
    updated = pl.pallas_call(
        functools.partial(state_kernel, sessions, heads, pair),
        grid=(sessions // pair,),
        out_shape=shape(session_head_state.shape, BF16),
        in_specs=[
            pl.BlockSpec((rows, channels), lambda i: (0, 0)),
            pl.BlockSpec((rows, LANES), lambda i: (0, 0)),
            smem(),
            pl.BlockSpec((pair, heads, HEAD_CHANNELS, state_size), lambda i: (i, 0, 0, 0)),
        ],
        out_specs=pl.BlockSpec((pair, heads, HEAD_CHANNELS, state_size), lambda i: (i, 0, 0, 0)),
        scratch_shapes=[pltpu.VMEM((channels, 2 * rows), BF16)],
        compiler_params=pltpu.CompilerParams(vmem_limit_bytes=16 << 20),
        cost_estimate=pl.CostEstimate(
            flops=8 * session_head_state.size,
            bytes_accessed=4 * session_head_state.size,
            transcendentals=0,
        ),
        name="state",
    )(drive, b_rows, keep, session_head_state)

    partial, pick = pl.pallas_call(
        functools.partial(down_kernel, n_msg),
        out_shape=[shape((targets, 2 * RANK), F32), shape((targets, LANES), F32)],
        in_specs=[vmem()] * (n_msg + 2),
        out_specs=[vmem()] * 2,
        name="down",
    )(*arrived, adapter_down_weight, squares)

    if tensor_count in (2, 4):
        parts = [partial] + [
            lax.ppermute(partial, "tensor", [(i, i ^ k) for i in range(tensor_count)])
            for k in range(1, tensor_count)
        ]
    else:
        parts = [lax.psum(partial, "tensor")]

    out = pl.pallas_call(
        functools.partial(up_kernel, len(parts), n_msg, sessions),
        out_shape=[shape((msg_rows, channels), F32)] * n_msg + [shape((rows, LANES), F32)],
        in_specs=[vmem()] * (len(parts) + 2),
        out_specs=[vmem()] * (n_msg + 1),
        name="up",
    )(*parts, pick, adapter_up_weight)
    terms, inverse = out[:n_msg], out[n_msg]
    returned = exchange(terms)

    normed = pl.pallas_call(
        norm_kernel,
        out_shape=shape((DECODE_STEPS, sessions, channels), BF16),
        in_specs=[vmem()] * 3,
        out_specs=vmem(),
        name="norm",
    )(gated, inverse, gain)

    delta = pl.pallas_call(
        functools.partial(final_kernel, n_msg),
        out_shape=shape((DECODE_STEPS, sessions, channels), F32),
        in_specs=[vmem()] * (n_msg + 2),
        out_specs=vmem(),
        name="final",
    )(*returned, place, inverse)
    return (updated, normed, delta)


def solution(mesh):
    placed = (
        P(("groups", "batch"), "tensor", None, None),
        P(None, ("groups", "batch"), "tensor"),
        P(None, ("groups", "batch"), "tensor"),
        P(None, ("groups", "batch"), None, None),
        P(None, ("groups", "batch"), None, None),
        P(None, ("groups", "batch"), "tensor"),
        P("tensor"),
        P("tensor"),
        P("tensor"),
        P("tensor"),
        P(("groups", "batch"), None, "tensor"),
        P(("groups", "batch"), None, "tensor"),
        P(("groups", "batch")),
        P("groups"),
    )
    return jax.shard_map(
        per_device,
        mesh=mesh,
        in_specs=placed,
        out_specs=(
            P(("groups", "batch"), "tensor", None, None),
            P(None, ("groups", "batch"), "tensor"),
            P(None, ("groups", "batch"), "tensor"),
        ),
        check_vma=False,
    )
```

time: 117 us -> 55 us (0.47)
  matrix products: 36 us -> 0 us
  other arithmetic: 18.8 us -> 0.07 us
  Pallas kernels: 0 us -> 17.5 us
  blocking collectives: 16.5 us -> 0 us
  local copies, waits for them, and re-layouts: 3.02 us -> 16.5 us
  waiting for transfers between devices: 19.4 us -> 7.68 us
  starting transfers between devices: 21 us -> 11.9 us
    dot_general x19 -> x0, matrix products: 36 us -> none  [the longest x2 29.4 us: per_device(): jnp.einsum('shpn,shn->shp', carried, c_heads, precision=highest_precision)]
    all_to_all x5 -> x0, starting transfers between devices: 21 us -> none  [the longest x2 8.08 us: per_device(): lax.all_to_all(row_pack, 'batch', split_axis=0, concat_axis=0, tiled=True)]
    all_to_all x5 -> x0, waiting for transfers between devices: 19.4 us -> none  [the longest x2 9.93 us: per_device(): lax.all_to_all(step_deltas, 'batch', split_axis=0, concat_axis=0, tiled=T...]
    pallas_call x0 -> x6, Pallas kernels: none -> 17.5 us  [the longest x1 5.6 us: per_device(): pl.pallas_call(functools.partial(state_kernel, sessions, heads, pair), gr...]
    psum x2 -> x0, blocking collectives: 16.5 us -> none  [the longest x1 10.2 us: per_device(): rank_projected_rows = lax.psum(partial_rank, 'tensor').astype(jnp.bfloat16)]
    unnamed x12 -> x52, local copies, waits for them, and re-layouts: 0.03 us -> 15.8 us
    convert_element_type x5 -> x0, other arithmetic: 13.3 us -> none  [the longest x2 12.4 us: per_device(): rounded = lax.optimization_barrier(carried.astype(jnp.bfloat16))]
    ppermute x0 -> x9, starting transfers between devices: none -> 11.9 us  [the longest x6 10 us: exchange(): lax.ppermute(blocks[k], 'batch', [(i, i ^ k) for i in range(batch_count)])]
  transfers between devices with their start and end apart: 5 -> 9, of which waited for: 4 -> 4; matrix products, arithmetic and copies ran while one was open for 46% -> 0% of each run, Pallas kernels for 0% -> 13%
where the time goes in v1:
time: 55 us; the launch traced here: 54.4 us
  Pallas kernels  17.5 us (32%)
  local copies, waits for them, and re-layouts  16.5 us (30%)
  starting transfers between devices  11.9 us (22%)
  waiting for transfers between devices  7.68 us (14%)
  between operations  0.72 us (1%)
    unnamed x52, local copies, waits for them, and re-layouts  15.8 us
    ppermute x6, starting transfers between devices, exchange(): lax.ppermute(blocks[k], 'batch', [(i, i ^ k) for i in range(batch_count)])  10 us
    pallas_call x1, Pallas kernels, per_device(): pl.pallas_call(functools.partial(state_kernel, sessions, heads, pair), gr...  5.6 us
    ppermute x6, waiting for transfers between devices, exchange(): lax.ppermute(blocks[k], 'batch', [(i, i ^ k) for i in range(batch_count)])  5.56 us
    pallas_call x1, Pallas kernels, per_device(): pl.pallas_call(functools.partial(front_kernel, dims), out_shape=[shape((m...  4.7 us
    ppermute x3, waiting for transfers between devices, per_device(): lax.ppermute(partial, 'tensor', [(i, i ^ k) for i in range(tensor_count)])  2.12 us
    pallas_call x1, Pallas kernels, per_device(): pl.pallas_call(functools.partial(up_kernel, len(parts), n_msg, sessions),...  1.91 us
    pallas_call x1, Pallas kernels, per_device(): pl.pallas_call(functools.partial(down_kernel, n_msg), out_shape=[shape((t...  1.89 us
  transfers between devices with their start and end apart: 9, of which 4 were waited for; matrix products, arithmetic and copies ran while one was open for 0% of the time, Pallas kernels for 13%

profile of v1, /device:TPU:0, one launch (start us, length us, event | category | flops | bytes accessed | tf_op | source)
XLA Modules:
  0.0 54.4 jit_solution(2133767395257300657)
XLA Ops:
  0.6 0.7 %reshape.21.refs_12_.gain = bf16[1,1024]{1,0:T(2,128)(2,1)S(1)} reshape(bf16[1024]{0:T(1024)(128)(2,1)} %param.23) | data formatting | bytes 4096 | tf_op jit(solution)/shard_map/reshape | solution.py:288
  1.4 2.2 %copy-done = bf16[16,16,64,128]{3,2,1,0:T(8,128)(2,1)S(1)} copy-done((bf16[16,16,64,128]{3,2,1,0:T(8,128)(2,1)S(1)}, bf16[16,16,64,128]{3,2,1,0:T(8,128)(2,1)}, u32[]{:S(2)}) %copy-start) | copy-done | bytes 4194328
  3.6 0.8 %copy-done.3 = bf16[2,16,1024]{2,1,0:T(8,128)(2,1)S(1)} copy-done((bf16[2,16,1024]{2,1,0:T(8,128)(2,1)S(1)}, bf16[2,16,1024]{2,1,0:T(8,128)(2,1)}, u32[]{:S(2)}) %copy-start.3) | copy-done | bytes 65560
  4.4 0.8 %copy-done.4 = bf16[2,16,1024]{2,1,0:T(8,128)(2,1)S(1)} copy-done((bf16[2,16,1024]{2,1,0:T(8,128)(2,1)S(1)}, bf16[2,16,1024]{2,1,0:T(8,128)(2,1)}, u32[]{:S(2)}) %copy-start.4) | copy-done | bytes 65560
  5.3 0.8 %copy-done.6 = bf16[2,16,4,128]{3,2,1,0:T(4,128)(2,1)S(1)} copy-done((bf16[2,16,4,128]{3,2,1,0:T(4,128)(2,1)S(1)}, bf16[2,16,4,128]{3,2,1,0:T(4,128)(2,1)}, u32[]{:S(2)}) %copy-start.6) | copy-done | bytes 32792
  6.0 0.8 %copy-done.7 = bf16[2,16,4,128]{3,2,1,0:T(4,128)(2,1)S(1)} copy-done((bf16[2,16,4,128]{3,2,1,0:T(4,128)(2,1)S(1)}, bf16[2,16,4,128]{3,2,1,0:T(4,128)(2,1)}, u32[]{:S(2)}) %copy-start.7) | copy-done | bytes 32792
  6.8 0.7 %copy-done.9 = f32[2,16,16]{2,1,0:T(8,128)S(1)} copy-done((f32[2,16,16]{2,1,0:T(8,128)S(1)}, f32[2,16,16]{2,1,0:T(8,128)}, u32[]{:S(2)}) %copy-start.9) | copy-done | bytes 2072
  7.5 0.7 %copy-done.12 = s32[16]{0:T(128)S(1)} copy-done((s32[16]{0:T(128)S(1)}, s32[16]{0:T(128)}, u32[]{:S(2)}) %copy-start.12) | copy-done | bytes 88
  8.2 0.7 %copy-done.13 = s32[8]{0:T(128)S(1)} copy-done((s32[8]{0:T(128)S(1)}, s32[8]{0:T(128)}, u32[]{:S(2)}) %copy-start.13) | copy-done | bytes 56
  10.8 4.7 %front.1 = (bf16[8,1152]{1,0:T(8,128)(2,1)S(1)}, bf16[8,1152]{1,0:T(8,128)(2,1)S(1)}, bf16[8,1152]{1,0:T(8,128)(2,1)S(1)}, bf16[8,1152]{1,0:T(8,128)(2,1)S(1)}, ...) custom-call(s32[2]{0:T(128)S(1)} %pad_add_fusion.refs_0_, ...), custom_call_target="tpu_custom_call" | custom-call | flops 134217728 | bytes 4194304 | tf_op jit(solution)/shard_map/front/pallas_call | solution.py:292
  18.0 3.0 %collective-permute-start = (bf16[8,1152]{1,0:T(8,128)(2,1)S(1)}, bf16[8,1152]{1,0:T(8,128)(2,1)S(1)}, u32[]{:S(2)}, u32[]{:S(2)}) collective-permute-start(bf16[8,1152]{1,0:T(8,128)(2,1)S(1)} %get-tuple-element.25), channel_id=1, source_target_pairs={{0,4},{4,0},{8,12},{12,8},{1,5},{5,1},{9,13},{13,9},{2,6},{6,2},{1... | collective-permute-start | bytes 55304 | tf_op jit(solution)/shard_map/ppermute | solution.py:338
  21.0 2.6 %collective-permute-start.1 = (bf16[8,1152]{1,0:T(8,128)(2,1)S(1)}, bf16[8,1152]{1,0:T(8,128)(2,1)S(1)}, u32[]{:S(2)}, u32[]{:S(2)}) collective-permute-start(bf16[8,1152]{1,0:T(8,128)(2,1)S(1)} %get-tuple-element.26), channel_id=1, source_target_pairs={{0,8},{4,12},{8,0},{12,4},{1,9},{5,13},{9,1},{13,5},{2,10},{6,14},... | collective-permute-start | bytes 55304 | tf_op jit(solution)/shard_map/ppermute | solution.py:338
  23.6 2.2 %collective-permute-done.1.refs_2_ = bf16[8,1152]{1,0:T(8,128)(2,1)S(1)} collective-permute-done((bf16[8,1152]{1,0:T(8,128)(2,1)S(1)}, bf16[8,1152]{1,0:T(8,128)(2,1)S(1)}, u32[]{:S(2)}, u32[]{:S(2)}) %collective-permute-start.1) | collective-permute-done | bytes 18464 | tf_op jit(solution)/shard_map/ppermute | solution.py:338
  25.8 3.3 %collective-permute-done.2.refs_3_ = bf16[8,1152]{1,0:T(8,128)(2,1)S(1)} collective-permute-done((bf16[8,1152]{1,0:T(8,128)(2,1)S(1)}, bf16[8,1152]{1,0:T(8,128)(2,1)S(1)}, u32[]{:S(2)}, u32[]{:S(2)}) %collective-permute-start.2) | collective-permute-done | bytes 18464 | tf_op jit(solution)/shard_map/ppermute | solution.py:338
  29.7 1.9 %down.1 = (f32[32,128]{1,0:T(8,128)}, f32[32,128]{1,0:T(8,128)}) custom-call(bf16[8,1152]{1,0:T(8,128)(2,1)} %copy-done.8, bf16[8,1152]{1,0:T(8,128)(2,1)} %copy-done.20, bf16[8,1152]{1,0:T(8,128)(2,1)} %copy-done.21, bf16[8,1152]{1,0:T(8,128)(2,1)} %copy-done.22, bf16[2,64,1024]{2,1,0:T(8,128)(2,1)} %refs_4_.3, f32[32,64]{1,0:T(8,128)} %copy-done.11), custom_call_target="tpu_custom_call" | custom-call | tf_op jit(solution)/shard_map/down/pallas_call | solution.py:371
  31.6 1.5 %collective-permute-start.4 = (f32[32,128]{1,0:T(8,128)}, f32[32,128]{1,0:T(8,128)S(1)}, u32[]{:S(2)}, u32[]{:S(2)}) collective-permute-start(f32[32,128]{1,0:T(8,128)} %get-tuple-element.29.refs_0_), channel_id=1, source_target_pairs={{0,2},{1,3},{2,0},{3,1},{4,6},{5,7},{6,4},{7,5},{8,10},{9,11},{10,... | collective-permute-start | bytes 49160 | tf_op jit(solution)/shard_map/ppermute | solution.py:381
  33.5 1.6 %collective-permute-done.5.refs_3_ = f32[32,128]{1,0:T(8,128)S(1)} collective-permute-done((f32[32,128]{1,0:T(8,128)}, f32[32,128]{1,0:T(8,128)S(1)}, u32[]{:S(2)}, u32[]{:S(2)}) %collective-permute-start.5) | collective-permute-done | bytes 16416 | tf_op jit(solution)/shard_map/ppermute | solution.py:381
  36.2 1.9 %up.1 = (f32[8,1024]{1,0:T(8,128)}, f32[8,1024]{1,0:T(8,128)}, f32[8,1024]{1,0:T(8,128)}, f32[8,1024]{1,0:T(8,128)}, f32[32,128]{1,0:T(8,128)}) custom-call(f32[32,128]{1,0:T(8,128)} %get-tuple-element.29.refs_0_, f32[32,128]{1,0:T(8,128)} %copy-done.25, f32[32,128]{1,0:T(8,128)} %copy-done.24, f32[32,128]{1,0:T(8,128)} %copy-done.23, ...), custom_call_target="tpu_custom_call" | custom-call | tf_op jit(solution)/shard_map/up/pallas_call | solution.py:387
  38.1 0.8 %collective-permute-start.7 = (f32[8,1024]{1,0:T(8,128)}, f32[8,1024]{1,0:T(8,128)S(1)}, u32[]{:S(2)}, u32[]{:S(2)}) collective-permute-start(f32[8,1024]{1,0:T(8,128)} %get-tuple-element.34), channel_id=1, source_target_pairs={{0,8},{4,12},{8,0},{12,4},{1,9},{5,13},{9,1},{13,5},{2,10},{6,14},... | collective-permute-start | bytes 98312 | tf_op jit(solution)/shard_map/ppermute | solution.py:338
  38.9 3.6 %collective-permute-start.8 = (f32[8,1024]{1,0:T(8,128)}, f32[8,1024]{1,0:T(8,128)S(1)}, u32[]{:S(2)}, u32[]{:S(2)}) collective-permute-start(f32[8,1024]{1,0:T(8,128)} %get-tuple-element.35), channel_id=1, source_target_pairs={{0,12},{4,8},{8,4},{12,0},{1,13},{5,9},{9,5},{13,1},{2,14},{6,10},... | collective-permute-start | bytes 98312 | tf_op jit(solution)/shard_map/ppermute | solution.py:338
  42.5 2.2 %copy-done.1 = bf16[16,16,64,128]{3,2,1,0:T(8,128)(2,1)S(1)} copy-done((bf16[16,16,64,128]{3,2,1,0:T(8,128)(2,1)S(1)}, bf16[16,16,64,128]{3,2,1,0:T(8,128)(2,1)}, u32[]{:S(2)}) %copy-start.1) | copy-done | bytes 4194328
  44.7 5.6 %state.2 = bf16[16,16,64,128]{3,2,1,0:T(8,128)(2,1)} custom-call(f32[32,1024]{1,0:T(8,128)S(1)} %get-tuple-element.20.drive, f32[32,128]{1,0:T(8,128)S(1)} %get-tuple-element.21.b, f32[16,16]{1,0:T(8,128)S(1)} %get-tuple-element.22.keep, bf16[16,16,64,128]{3,2,1,0:T(8,128)(2,1)S(1)} %copy-done.1), custom_call_target="tpu_custom_call" | custom-call | flops 16777216 | bytes 8388608 | tf_op jit(solution)/shard_map/state/pallas_call | solution.py:350
  50.3 1.6 %norm.1 = bf16[2,16,1024]{2,1,0:T(8,128)(2,1)} custom-call(f32[32,1024]{1,0:T(8,128)} %copy-done.2, f32[32,128]{1,0:T(8,128)} %get-tuple-element.31.inverse.refs_5_, bf16[1,1024]{1,0:T(2,128)(2,1)} %copy-done.5), custom_call_target="tpu_custom_call" | custom-call | tf_op jit(solution)/shard_map/norm/pallas_call | solution.py:397
  52.6 1.8 %final.1 = f32[2,16,1024]{2,1,0:T(8,128)} custom-call(f32[8,1024]{1,0:T(8,128)} %get-tuple-element.32.refs_0_, f32[8,1024]{1,0:T(8,128)} %copy-done.17, f32[8,1024]{1,0:T(8,128)} %copy-done.18, f32[8,1024]{1,0:T(8,128)} %copy-done.19, f32[32,32]{1,0:T(8,128)} %copy-done.10, f32[32,128]{1,0:T(8,128)} %get-tuple-element.31.inverse.refs_5_), custom_call_target="tpu_custom_call" | custom-call | tf_op jit(solution)/shard_map/final/pallas_call | solution.py:405
  (54 shorter events, 7.1 us)
Async XLA Ops:
  1.3 49.0 %copy-start.5 = (bf16[1,1024]{1,0:T(2,128)(2,1)}, bf16[1,1024]{1,0:T(2,128)(2,1)S(1)}, u32[]{:S(2)}) copy-start(bf16[1,1024]{1,0:T(2,128)(2,1)S(1)} %reshape.21.refs_12_.gain) | copy-start | bytes 6148
  1.4 2.2 %copy-start = (bf16[16,16,64,128]{3,2,1,0:T(8,128)(2,1)S(1)}, bf16[16,16,64,128]{3,2,1,0:T(8,128)(2,1)}, u32[]{:S(2)}) copy-start(bf16[16,16,64,128]{3,2,1,0:T(8,128)(2,1)} %state.3) | copy-start | bytes 12582916
  3.6 0.8 %copy-start.3 = (bf16[2,16,1024]{2,1,0:T(8,128)(2,1)S(1)}, bf16[2,16,1024]{2,1,0:T(8,128)(2,1)}, u32[]{:S(2)}) copy-start(bf16[2,16,1024]{2,1,0:T(8,128)(2,1)} %refs_4_.2) | copy-start | bytes 196612
  4.4 0.8 %copy-start.4 = (bf16[2,16,1024]{2,1,0:T(8,128)(2,1)S(1)}, bf16[2,16,1024]{2,1,0:T(8,128)(2,1)}, u32[]{:S(2)}) copy-start(bf16[2,16,1024]{2,1,0:T(8,128)(2,1)} %refs_5_.2) | copy-start | bytes 196612
  5.3 0.8 %copy-start.6 = (bf16[2,16,4,128]{3,2,1,0:T(4,128)(2,1)S(1)}, bf16[2,16,4,128]{3,2,1,0:T(4,128)(2,1)}, u32[]{:S(2)}) copy-start(bf16[2,16,4,128]{3,2,1,0:T(4,128)(2,1)} %refs_6_.1) | copy-start | bytes 98308
  6.0 0.8 %copy-start.7 = (bf16[2,16,4,128]{3,2,1,0:T(4,128)(2,1)S(1)}, bf16[2,16,4,128]{3,2,1,0:T(4,128)(2,1)}, u32[]{:S(2)}) copy-start(bf16[2,16,4,128]{3,2,1,0:T(4,128)(2,1)} %refs_7_.1) | copy-start | bytes 98308
  6.8 0.7 %copy-start.9 = (f32[2,16,16]{2,1,0:T(8,128)S(1)}, f32[2,16,16]{2,1,0:T(8,128)}, u32[]{:S(2)}) copy-start(f32[2,16,16]{2,1,0:T(8,128)} %refs_8_.1) | copy-start | bytes 6148
  7.5 0.7 %copy-start.12 = (s32[16]{0:T(128)S(1)}, s32[16]{0:T(128)}, u32[]{:S(2)}) copy-start(s32[16]{0:T(128)} %refs_1_.1) | copy-start | bytes 196
  8.2 0.7 %copy-start.13 = (s32[8]{0:T(128)S(1)}, s32[8]{0:T(128)}, u32[]{:S(2)}) copy-start(s32[8]{0:T(128)} %refs_2_.1) | copy-start | bytes 100
  8.8 0.7 %copy-start.14 = (f32[16]{0:T(128)S(1)}, f32[16]{0:T(128)}, u32[]{:S(2)}) copy-start(f32[16]{0:T(128)} %param.20) | copy-start | bytes 196
  9.5 0.7 %copy-start.15 = (f32[16]{0:T(128)S(1)}, f32[16]{0:T(128)}, u32[]{:S(2)}) copy-start(f32[16]{0:T(128)} %param.21) | copy-start | bytes 196
  15.5 0.7 %copy-start.2 = (f32[32,1024]{1,0:T(8,128)}, f32[32,1024]{1,0:T(8,128)S(1)}, u32[]{:S(2)}) copy-start(f32[32,1024]{1,0:T(8,128)S(1)} %get-tuple-element.23.gated) | copy-start | bytes 393220
  18.0 5.6 %collective-permute-start = (bf16[8,1152]{1,0:T(8,128)(2,1)S(1)}, bf16[8,1152]{1,0:T(8,128)(2,1)S(1)}, u32[]{:S(2)}, u32[]{:S(2)}) collective-permute-start(bf16[8,1152]{1,0:T(8,128)(2,1)S(1)} %get-tuple-element.25), channel_id=1, source_target_pairs={{0,4},{4,0},{8,12},{12,8},{1,5},{5,1},{9,13},{13,9},{2,6},{6,2},{1... | collective-permute-start | bytes 55304 | tf_op jit(solution)/shard_map/ppermute | solution.py:338
  21.0 4.8 %collective-permute-start.1 = (bf16[8,1152]{1,0:T(8,128)(2,1)S(1)}, bf16[8,1152]{1,0:T(8,128)(2,1)S(1)}, u32[]{:S(2)}, u32[]{:S(2)}) collective-permute-start(bf16[8,1152]{1,0:T(8,128)(2,1)S(1)} %get-tuple-element.26), channel_id=1, source_target_pairs={{0,8},{4,12},{8,0},{12,4},{1,9},{5,13},{9,1},{13,5},{2,10},{6,14},... | collective-permute-start | bytes 55304 | tf_op jit(solution)/shard_map/ppermute | solution.py:338
  23.6 5.6 %collective-permute-start.2 = (bf16[8,1152]{1,0:T(8,128)(2,1)S(1)}, bf16[8,1152]{1,0:T(8,128)(2,1)S(1)}, u32[]{:S(2)}, u32[]{:S(2)}) collective-permute-start(bf16[8,1152]{1,0:T(8,128)(2,1)S(1)} %get-tuple-element.27), channel_id=1, source_target_pairs={{0,12},{4,8},{8,4},{12,0},{1,13},{5,9},{9,5},{13,1},{2,14},{6,10},... | collective-permute-start | bytes 55304 | tf_op jit(solution)/shard_map/ppermute | solution.py:338
  23.6 5.6 %copy-start.20 = (bf16[8,1152]{1,0:T(8,128)(2,1)}, bf16[8,1152]{1,0:T(8,128)(2,1)S(1)}, u32[]{:S(2)}) copy-start(bf16[8,1152]{1,0:T(8,128)(2,1)S(1)} %collective-permute-done.refs_1_) | copy-start | bytes 55300
  25.8 3.4 %copy-start.21 = (bf16[8,1152]{1,0:T(8,128)(2,1)}, bf16[8,1152]{1,0:T(8,128)(2,1)S(1)}, u32[]{:S(2)}) copy-start(bf16[8,1152]{1,0:T(8,128)(2,1)S(1)} %collective-permute-done.1.refs_2_) | copy-start | bytes 55300
  31.6 3.5 %collective-permute-start.5 = (f32[32,128]{1,0:T(8,128)}, f32[32,128]{1,0:T(8,128)S(1)}, u32[]{:S(2)}, u32[]{:S(2)}) collective-permute-start(f32[32,128]{1,0:T(8,128)} %get-tuple-element.29.refs_0_), channel_id=1, source_target_pairs={{0,3},{1,2},{2,1},{3,0},{4,7},{5,6},{6,5},{7,4},{8,11},{9,10},{10,... | collective-permute-start | bytes 49160 | tf_op jit(solution)/shard_map/ppermute | solution.py:381
  31.6 4.0 %collective-permute-start.4 = (f32[32,128]{1,0:T(8,128)}, f32[32,128]{1,0:T(8,128)S(1)}, u32[]{:S(2)}, u32[]{:S(2)}) collective-permute-start(f32[32,128]{1,0:T(8,128)} %get-tuple-element.29.refs_0_), channel_id=1, source_target_pairs={{0,2},{1,3},{2,0},{3,1},{4,6},{5,7},{6,4},{7,5},{8,10},{9,11},{10,... | collective-permute-start | bytes 49160 | tf_op jit(solution)/shard_map/ppermute | solution.py:381
  33.1 2.5 %collective-permute-start.3 = (f32[32,128]{1,0:T(8,128)}, f32[32,128]{1,0:T(8,128)S(1)}, u32[]{:S(2)}, u32[]{:S(2)}) collective-permute-start(f32[32,128]{1,0:T(8,128)} %get-tuple-element.29.refs_0_), channel_id=1, source_target_pairs={{0,1},{1,0},{2,3},{3,2},{4,5},{5,4},{6,7},{7,6},{8,9},{9,8},{10,11... | collective-permute-start | bytes 49160 | tf_op jit(solution)/shard_map/ppermute | solution.py:381
  38.1 13.8 %collective-permute-start.6 = (f32[8,1024]{1,0:T(8,128)}, f32[8,1024]{1,0:T(8,128)S(1)}, u32[]{:S(2)}, u32[]{:S(2)}) collective-permute-start(f32[8,1024]{1,0:T(8,128)} %get-tuple-element.33), channel_id=1, source_target_pairs={{0,4},{4,0},{8,12},{12,8},{1,5},{5,1},{9,13},{13,9},{2,6},{6,2},{1... | collective-permute-start | bytes 98312 | tf_op jit(solution)/shard_map/ppermute | solution.py:338
  38.1 13.8 %collective-permute-start.7 = (f32[8,1024]{1,0:T(8,128)}, f32[8,1024]{1,0:T(8,128)S(1)}, u32[]{:S(2)}, u32[]{:S(2)}) collective-permute-start(f32[8,1024]{1,0:T(8,128)} %get-tuple-element.34), channel_id=1, source_target_pairs={{0,8},{4,12},{8,0},{12,4},{1,9},{5,13},{9,1},{13,5},{2,10},{6,14},... | collective-permute-start | bytes 98312 | tf_op jit(solution)/shard_map/ppermute | solution.py:338
  38.9 13.1 %collective-permute-start.8 = (f32[8,1024]{1,0:T(8,128)}, f32[8,1024]{1,0:T(8,128)S(1)}, u32[]{:S(2)}, u32[]{:S(2)}) collective-permute-start(f32[8,1024]{1,0:T(8,128)} %get-tuple-element.35), channel_id=1, source_target_pairs={{0,12},{4,8},{8,4},{12,0},{1,13},{5,9},{9,5},{13,1},{2,14},{6,10},... | collective-permute-start | bytes 98312 | tf_op jit(solution)/shard_map/ppermute | solution.py:338
  42.5 2.2 %copy-start.1 = (bf16[16,16,64,128]{3,2,1,0:T(8,128)(2,1)S(1)}, bf16[16,16,64,128]{3,2,1,0:T(8,128)(2,1)}, u32[]{:S(2)}) copy-start(bf16[16,16,64,128]{3,2,1,0:T(8,128)(2,1)} %state.3) | copy-start | bytes 12582916
  (11 other events, 6.7 us)

commit v2 on v1

--- a/solution.py
+++ b/solution.py
@@ -29,25 +29,45 @@
 
 def front_kernel(dims, *refs):
     sessions, heads, batch_count, capacity, adapters_held, chunks, split = dims
-    (ids, adapter, slot_of, state, x, z, b, c, raw, bias, rate, skip, gain) = refs[:13]
     n_msg = batch_count if split else 1
-    msgs = refs[13 : 13 + n_msg]
-    gated_ref, square_ref, drive_ref, b_ref, keep_ref, place_ref = refs[13 + n_msg : 19 + n_msg]
-    held, sems, counts = refs[19 + n_msg :]
+    inputs, refs = refs[:14], refs[14:]
+    msgs, refs = refs[:n_msg], refs[n_msg:]
+    gated_ref, square_ref, drive_ref, b_ref, keep_ref, place_ref, gain_ref = refs[:7]
+    held, down_out, up_out = refs[7:10]
+    local, (sems, small_sems, weight_sems, counts) = refs[10:21], refs[21:]
+    state, down, up = inputs[:3]
     channels = heads * HEAD_CHANNELS
     rows = DECODE_STEPS * sessions
     part = heads // chunks
     width = part * HEAD_CHANNELS
 
+    loads = [
+        pltpu.make_async_copy(source, target, small_sems.at[i])
+        for i, (source, target) in enumerate(zip(inputs[3:], local))
+    ]
+    for load in loads:
+        load.start()
     copies = []
     for i in range(chunks):
         window = pl.ds(i * part, part)
         copy = pltpu.make_async_copy(state.at[:, window], held.at[:, window], sems.at[i])
         copy.start()
         copies.append(copy)
-
-    me = ids[0]
-    group = ids[1]
+    weights = [
+        pltpu.make_async_copy(down, down_out, weight_sems.at[0]),
+        pltpu.make_async_copy(up, up_out, weight_sems.at[1]),
+    ]
+    for load in weights:
+        load.start()
+    adapter, slot_of, x, z, b, c, raw, bias, rate, skip, gain_rows = local
+    me = lax.axis_index("batch")
+    group = lax.axis_index("tensor") * heads // (HEAD_COUNT // GROUPS)
+    for load in loads:
+        load.wait()
+    gain = jnp.concatenate(
+        [gain_rows[i : i + 1].astype(F32) for i in range(channels // LANES)], axis=1
+    )
+    gain_ref[...] = gain
     for i in range(batch_count):
         counts[i] = 0
     per_owner = DECODE_STEPS * capacity
@@ -140,7 +160,7 @@
         for j in range(width // LANES):
             piece = gated[:, j * LANES : (j + 1) * LANES]
             squares = squares + piece * piece
-        weighted = (gated * gain[:, lanes].astype(F32)).astype(BF16)
+        weighted = (gated * gain[:, lanes]).astype(BF16)
         packed = jnp.dot(place_bf, weighted, preferred_element_type=F32)
         for k in range(n_msg):
             n = targets // n_msg
@@ -149,32 +169,38 @@
         n = targets // n_msg
         msgs[k][:, channels:] = pick[k * n : (k + 1) * n].astype(BF16)
     square_ref[...] = squares[:, :RANK] + squares[:, RANK:]
-
-
-def state_kernel(sessions, heads, pair, drive, b, keep, state, out, drive_t):
-    i = pl.program_id(0)
-    channels = heads * HEAD_CHANNELS
+    for load in weights:
+        load.wait()
+
+
+def state_kernel(pair, drive, b, keep, state, out, made, sems):
+    sessions, heads, _, _ = state.shape
     rows = DECODE_STEPS * sessions
-
-    @pl.when(i == 0)
-    def _():
-        turned = drive[...].T
-        high = turned.astype(BF16)
-        low = (turned - high.astype(F32)).astype(BF16)
-        drive_t[...] = jnp.concatenate([high, low], axis=1)
-
+    turned = drive[...].T
+    high = turned.astype(BF16)
+    low = (turned - high.astype(F32)).astype(BF16)
+    left = jnp.concatenate([high, low], axis=1)
     row_session = iota((rows, LANES), 0) % sessions
     b_rows = b[...]
-    right = jnp.concatenate(
-        [jnp.where(row_session == i * pair + q, b_rows, 0.0) for q in range(pair)], axis=1
-    )
-    right = jnp.concatenate([right, right], axis=0).astype(BF16)
-    for h in range(heads):
-        piece = slice(h * HEAD_CHANNELS, (h + 1) * HEAD_CHANNELS)
-        added = jnp.dot(drive_t[piece], right, preferred_element_type=F32)
-        for q in range(pair):
-            kept = state[q, h].astype(F32) * keep[i * pair + q, h]
-            out[q, h] = (kept + added[:, q * LANES : (q + 1) * LANES]).astype(BF16)
+    copies = []
+    for i in range(sessions // pair):
+        right = jnp.concatenate(
+            [jnp.where(row_session == i * pair + q, b_rows, 0.0) for q in range(pair)], axis=1
+        )
+        right = jnp.concatenate([right, right], axis=0).astype(BF16)
+        for h in range(heads):
+            piece = slice(h * HEAD_CHANNELS, (h + 1) * HEAD_CHANNELS)
+            added = jnp.dot(left[piece], right, preferred_element_type=F32)
+            for q in range(pair):
+                s = i * pair + q
+                kept = state[s, h].astype(F32) * keep[s, h]
+                made[s, h] = (kept + added[:, q * LANES : (q + 1) * LANES]).astype(BF16)
+        window = pl.ds(i * pair, pair)
+        copy = pltpu.make_async_copy(made.at[window], out.at[window], sems.at[i])
+        copy.start()
+        copies.append(copy)
+    for copy in copies:
+        copy.wait()
 
 
 def down_kernel(n_msg, *refs):
@@ -228,7 +254,7 @@
 
 def norm_kernel(gated, inverse, gain, out):
     rows, channels = gated.shape
-    normed = gated[...] * inverse[:, :1] * gain[...].astype(F32)
+    normed = gated[...] * inverse[:, :1] * gain[...]
     out[...] = normed.astype(BF16).reshape(out.shape)
 
 
@@ -276,19 +302,27 @@
     batch_count = lax.axis_size("batch")
     tensor_count = lax.axis_size("tensor")
     capacity = max(2, (sessions + batch_count - 1) // batch_count)
-    held = adapter_down_weight.shape[0]
+    adapters_held = adapter_down_weight.shape[0]
     split = batch_count in (2, 4)
     per_owner = DECODE_STEPS * capacity
     targets = batch_count * per_owner
     n_msg = batch_count if split else 1
     chunks = 4
-    me = lax.axis_index("batch")
-    group = lax.axis_index("tensor") * heads // (HEAD_COUNT // GROUPS)
-    ids = jnp.stack([me, group]).astype(jnp.int32)
-    gain = group_norm_gain.reshape(1, channels)
-
     msg_rows = targets // n_msg
-    dims = (sessions, heads, batch_count, capacity, held, chunks, split)
+    dims = (sessions, heads, batch_count, capacity, adapters_held, chunks, split)
+    smalls = (
+        adapter_per_session,
+        adapter_storage_slot,
+        convolved_activation,
+        gate_activations,
+        state_input_projection,
+        state_output_projection,
+        raw_step_sizes,
+        step_size_bias.reshape(1, heads),
+        log_decay_rate.reshape(1, heads),
+        skip_coefficient.reshape(1, heads),
+        group_norm_gain.reshape(channels // LANES, LANES),
+    )
     out = pl.pallas_call(
         functools.partial(front_kernel, dims),
         out_shape=[shape((msg_rows, channels + LANES), BF16)] * n_msg
@@ -299,38 +333,31 @@
             shape((rows, LANES), F32),
             shape((sessions, heads), F32),
             shape((targets, rows), F32),
+            shape((1, channels), F32),
+            shape(session_head_state.shape, BF16),
+            shape(adapter_down_weight.shape, BF16),
+            shape(adapter_up_weight.shape, BF16),
         ],
-        in_specs=[smem()] * 3 + [pl.BlockSpec(memory_space=pl.ANY)] + [vmem()] * 9,
-        out_specs=[vmem()] * (n_msg + 6),
-        scratch_shapes=[
-            pltpu.VMEM(session_head_state.shape, BF16),
+        in_specs=[pl.BlockSpec(memory_space=pltpu.HBM)] * 14,
+        out_specs=[vmem()] * (n_msg + 10),
+        scratch_shapes=[pltpu.SMEM(v.shape, v.dtype) for v in smalls[:2]]
+        + [pltpu.VMEM(v.shape, v.dtype) for v in smalls[2:]]
+        + [
             pltpu.SemaphoreType.DMA((chunks,)),
+            pltpu.SemaphoreType.DMA((len(smalls),)),
+            pltpu.SemaphoreType.DMA((2,)),
             pltpu.SMEM((batch_count,), jnp.int32),
         ],
-        compiler_params=pltpu.CompilerParams(vmem_limit_bytes=24 << 20),
+        compiler_params=pltpu.CompilerParams(vmem_limit_bytes=16 << 20),
         cost_estimate=pl.CostEstimate(
             flops=2 * 32 * session_head_state.size,
             bytes_accessed=2 * session_head_state.size,
             transcendentals=0,
         ),
         name="front",
-    )(
-        ids,
-        adapter_per_session,
-        adapter_storage_slot,
-        session_head_state,
-        convolved_activation,
-        gate_activations,
-        state_input_projection,
-        state_output_projection,
-        raw_step_sizes,
-        step_size_bias.reshape(1, heads),
-        log_decay_rate.reshape(1, heads),
-        skip_coefficient.reshape(1, heads),
-        gain,
-    )
+    )(session_head_state, adapter_down_weight, adapter_up_weight, *smalls)
     msgs = out[:n_msg]
-    gated, squares, drive, b_rows, keep, place = out[n_msg:]
+    gated, squares, drive, b_rows, keep, place, gain, held_state, down, up = out[n_msg:]
 
     def exchange(blocks):
         if split:
@@ -348,33 +375,32 @@
 
     pair = 2
     updated = pl.pallas_call(
-        functools.partial(state_kernel, sessions, heads, pair),
-        grid=(sessions // pair,),
+        functools.partial(state_kernel, pair),
         out_shape=shape(session_head_state.shape, BF16),
-        in_specs=[
-            pl.BlockSpec((rows, channels), lambda i: (0, 0)),
-            pl.BlockSpec((rows, LANES), lambda i: (0, 0)),
-            smem(),
-            pl.BlockSpec((pair, heads, HEAD_CHANNELS, state_size), lambda i: (i, 0, 0, 0)),
+        in_specs=[vmem(), vmem(), smem(), vmem()],
+        out_specs=pl.BlockSpec(memory_space=pltpu.HBM),
+        scratch_shapes=[
+            pltpu.VMEM(session_head_state.shape, BF16),
+            pltpu.SemaphoreType.DMA((sessions // pair,)),
         ],
-        out_specs=pl.BlockSpec((pair, heads, HEAD_CHANNELS, state_size), lambda i: (i, 0, 0, 0)),
-        scratch_shapes=[pltpu.VMEM((channels, 2 * rows), BF16)],
-        compiler_params=pltpu.CompilerParams(vmem_limit_bytes=16 << 20),
+        compiler_params=pltpu.CompilerParams(vmem_limit_bytes=12 << 20),
         cost_estimate=pl.CostEstimate(
             flops=8 * session_head_state.size,
             bytes_accessed=4 * session_head_state.size,
             transcendentals=0,
         ),
         name="state",
-    )(drive, b_rows, keep, session_head_state)
+    )(drive, b_rows, keep, held_state)
+    arrived = lax.optimization_barrier((arrived, updated))[0]
 
     partial, pick = pl.pallas_call(
         functools.partial(down_kernel, n_msg),
         out_shape=[shape((targets, 2 * RANK), F32), shape((targets, LANES), F32)],
         in_specs=[vmem()] * (n_msg + 2),
         out_specs=[vmem()] * 2,
+        compiler_params=pltpu.CompilerParams(vmem_limit_bytes=4 << 20),
         name="down",
-    )(*arrived, adapter_down_weight, squares)
+    )(*arrived, down, squares)
 
     if tensor_count in (2, 4):
         parts = [partial] + [
@@ -389,8 +415,9 @@
         out_shape=[shape((msg_rows, channels), F32)] * n_msg + [shape((rows, LANES), F32)],
         in_specs=[vmem()] * (len(parts) + 2),
         out_specs=[vmem()] * (n_msg + 1),
+        compiler_params=pltpu.CompilerParams(vmem_limit_bytes=4 << 20),
         name="up",
-    )(*parts, pick, adapter_up_weight)
+    )(*parts, pick, up)
     terms, inverse = out[:n_msg], out[n_msg]
     returned = exchange(terms)
 
@@ -399,6 +426,7 @@
         out_shape=shape((DECODE_STEPS, sessions, channels), BF16),
         in_specs=[vmem()] * 3,
         out_specs=vmem(),
+        compiler_params=pltpu.CompilerParams(vmem_limit_bytes=4 << 20),
         name="norm",
     )(gated, inverse, gain)
 
@@ -407,6 +435,7 @@
         out_shape=shape((DECODE_STEPS, sessions, channels), F32),
         in_specs=[vmem()] * (n_msg + 2),
         out_specs=vmem(),
+        compiler_params=pltpu.CompilerParams(vmem_limit_bytes=4 << 20),
         name="final",
     )(*returned, place, inverse)
     return (updated, normed, delta)

time: 55 us -> 42.4 us (0.77)
  Pallas kernels: 17.5 us -> 10.1 us
  local copies, waits for them, and re-layouts: 16.5 us -> 11.9 us
  waiting for transfers between devices: 7.68 us -> 6.98 us
    unnamed x52 -> x28, local copies, waits for them, and re-layouts: 15.8 us -> 11.9 us
    pallas_call x1, Pallas kernels: 5.6 us -> 3.27 us  [per_device(): pl.pallas_call(functools.partial(state_kernel, pair), out_shape=shape(ses...]
    pallas_call x1, Pallas kernels: 1.91 us -> 0.21 us  [per_device(): pl.pallas_call(functools.partial(up_kernel, len(parts), n_msg, sessions),...]
    pallas_call x1, Pallas kernels: 1.89 us -> 0.21 us  [per_device(): pl.pallas_call(functools.partial(down_kernel, n_msg), out_shape=[shape((t...]
    pallas_call x1, Pallas kernels: 1.63 us -> 0.71 us  [per_device(): pl.pallas_call(norm_kernel, out_shape=shape((DECODE_STEPS, sessions, chan...]
    pallas_call x1, Pallas kernels: 1.79 us -> 0.96 us  [per_device(): pl.pallas_call(functools.partial(final_kernel, n_msg), out_shape=shape((D...]
    reshape x1 -> x0, local copies, waits for them, and re-layouts: 0.69 us -> none  [per_device(): gain = group_norm_gain.reshape(1, channels)]
  transfers between devices with their start and end apart: 9 -> 9, of which waited for: 4 -> 4; matrix products, arithmetic and copies ran while one was open for 0% -> 0% of each run, Pallas kernels for 13% -> 10%
where the time goes in v2:
time: 42.4 us; the launch traced here: 41.8 us
  starting transfers between devices  12.1 us (29%)
  local copies, waits for them, and re-layouts  11.9 us (28%)
  Pallas kernels  10.1 us (24%)
  waiting for transfers between devices  6.98 us (16%)
  between operations  0.72 us (2%)
    unnamed x28, local copies, waits for them, and re-layouts  11.9 us
    ppermute x6, starting transfers between devices, exchange(): lax.ppermute(blocks[k], 'batch', [(i, i ^ k) for i in range(batch_count)])  10.1 us
    ppermute x6, waiting for transfers between devices, exchange(): lax.ppermute(blocks[k], 'batch', [(i, i ^ k) for i in range(batch_count)])  5.02 us
    pallas_call x1, Pallas kernels, per_device(): pl.pallas_call(functools.partial(front_kernel, dims), out_shape=[shape((m...  4.7 us
    pallas_call x1, Pallas kernels, per_device(): pl.pallas_call(functools.partial(state_kernel, pair), out_shape=shape(ses...  3.27 us
    ppermute x3, waiting for transfers between devices, per_device(): lax.ppermute(partial, 'tensor', [(i, i ^ k) for i in range(tensor_count)])  1.96 us
    ppermute x3, starting transfers between devices, per_device(): lax.ppermute(partial, 'tensor', [(i, i ^ k) for i in range(tensor_count)])  1.96 us
    pallas_call x1, Pallas kernels, per_device(): pl.pallas_call(functools.partial(final_kernel, n_msg), out_shape=shape((D...  0.96 us
  transfers between devices with their start and end apart: 9, of which 4 were waited for; matrix products, arithmetic and copies ran while one was open for 0% of the time, Pallas kernels for 10%

profile of v2, /device:TPU:0, one launch (start us, length us, event | category | flops | bytes accessed | tf_op | source)
XLA Modules:
  0.0 41.8 jit_solution(12602049741446612569)
XLA Ops:
  0.6 2.2 %copy-done = bf16[16,16,64,128]{3,2,1,0:T(8,128)(2,1)S(1)} copy-done((bf16[16,16,64,128]{3,2,1,0:T(8,128)(2,1)S(1)}, bf16[16,16,64,128]{3,2,1,0:T(8,128)(2,1)}, u32[]{:S(2)}) %copy-start) | copy-done | bytes 4194328
  2.8 0.9 %copy-done.1 = bf16[2,64,1024]{2,1,0:T(8,128)(2,1)S(1)} copy-done((bf16[2,64,1024]{2,1,0:T(8,128)(2,1)S(1)}, bf16[2,64,1024]{2,1,0:T(8,128)(2,1)}, u32[]{:S(2)}) %copy-start.1) | copy-done | bytes 262168
  3.8 0.9 %copy-done.2 = bf16[2,64,1024]{2,1,0:T(8,128)(2,1)S(1)} copy-done((bf16[2,64,1024]{2,1,0:T(8,128)(2,1)S(1)}, bf16[2,64,1024]{2,1,0:T(8,128)(2,1)}, u32[]{:S(2)}) %copy-start.2) | copy-done | bytes 262168
  4.7 0.8 %copy-done.3 = bf16[2,16,1024]{2,1,0:T(8,128)(2,1)S(1)} copy-done((bf16[2,16,1024]{2,1,0:T(8,128)(2,1)S(1)}, bf16[2,16,1024]{2,1,0:T(8,128)(2,1)}, u32[]{:S(2)}) %copy-start.3) | copy-done | bytes 65560
  5.6 0.8 %copy-done.4 = bf16[2,16,1024]{2,1,0:T(8,128)(2,1)S(1)} copy-done((bf16[2,16,1024]{2,1,0:T(8,128)(2,1)S(1)}, bf16[2,16,1024]{2,1,0:T(8,128)(2,1)}, u32[]{:S(2)}) %copy-start.4) | copy-done | bytes 65560
  6.4 0.8 %copy-done.5 = bf16[2,16,4,128]{3,2,1,0:T(4,128)(2,1)S(1)} copy-done((bf16[2,16,4,128]{3,2,1,0:T(4,128)(2,1)S(1)}, bf16[2,16,4,128]{3,2,1,0:T(4,128)(2,1)}, u32[]{:S(2)}) %copy-start.5) | copy-done | bytes 32792
  7.2 0.8 %copy-done.6 = bf16[2,16,4,128]{3,2,1,0:T(4,128)(2,1)S(1)} copy-done((bf16[2,16,4,128]{3,2,1,0:T(4,128)(2,1)S(1)}, bf16[2,16,4,128]{3,2,1,0:T(4,128)(2,1)}, u32[]{:S(2)}) %copy-start.6) | copy-done | bytes 32792
  7.9 0.7 %copy-done.7 = f32[2,16,16]{2,1,0:T(8,128)S(1)} copy-done((f32[2,16,16]{2,1,0:T(8,128)S(1)}, f32[2,16,16]{2,1,0:T(8,128)}, u32[]{:S(2)}) %copy-start.7) | copy-done | bytes 2072
  8.6 0.7 %copy-done.8 = bf16[1024]{0:T(1024)(128)(2,1)S(1)} copy-done((bf16[1024]{0:T(1024)(128)(2,1)S(1)}, bf16[1024]{0:T(1024)(128)(2,1)}, u32[]{:S(2)}) %copy-start.8) | copy-done | bytes 2072
  9.3 0.7 %copy-done.9 = s32[16]{0:T(128)S(1)} copy-done((s32[16]{0:T(128)S(1)}, s32[16]{0:T(128)}, u32[]{:S(2)}) %copy-start.9) | copy-done | bytes 88
  10.0 0.7 %copy-done.10 = s32[8]{0:T(128)S(1)} copy-done((s32[8]{0:T(128)S(1)}, s32[8]{0:T(128)}, u32[]{:S(2)}) %copy-start.10) | copy-done | bytes 56
  10.6 0.7 %copy-done.11 = f32[16]{0:T(128)S(1)} copy-done((f32[16]{0:T(128)S(1)}, f32[16]{0:T(128)}, u32[]{:S(2)}) %copy-start.11) | copy-done | bytes 88
  12.6 4.7 %front.1 = (bf16[8,1152]{1,0:T(8,128)(2,1)S(1)}, bf16[8,1152]{1,0:T(8,128)(2,1)S(1)}, bf16[8,1152]{1,0:T(8,128)(2,1)S(1)}, bf16[8,1152]{1,0:T(8,128)(2,1)S(1)}, ...) custom-call(bf16[16,16,64,128]{3,2,1,0:T(8,128)(2,1)S(1)} %copy-done, ...), custom_call_target="tpu_custom_call" | custom-call | flops 134217728 | bytes 4194304 | tf_op jit(solution)/shard_map/front/pallas_call | solution.py:326
  17.3 3.1 %collective-permute-start = (bf16[8,1152]{1,0:T(8,128)(2,1)S(1)}, bf16[8,1152]{1,0:T(8,128)(2,1)S(1)}, u32[]{:S(2)}, u32[]{:S(2)}) collective-permute-start(bf16[8,1152]{1,0:T(8,128)(2,1)S(1)} %get-tuple-element.34), channel_id=1, source_target_pairs={{0,4},{4,0},{8,12},{12,8},{1,5},{5,1},{9,13},{13,9},{2,6},{6,2},{1... | collective-permute-start | bytes 55304 | tf_op jit(solution)/shard_map/ppermute | solution.py:365
  20.4 2.6 %collective-permute-start.1 = (bf16[8,1152]{1,0:T(8,128)(2,1)S(1)}, bf16[8,1152]{1,0:T(8,128)(2,1)S(1)}, u32[]{:S(2)}, u32[]{:S(2)}) collective-permute-start(bf16[8,1152]{1,0:T(8,128)(2,1)S(1)} %get-tuple-element.35), channel_id=1, source_target_pairs={{0,8},{4,12},{8,0},{12,4},{1,9},{5,13},{9,1},{13,5},{2,10},{6,14},... | collective-permute-start | bytes 55304 | tf_op jit(solution)/shard_map/ppermute | solution.py:365
  23.0 3.3 %state.1 = bf16[16,16,64,128]{3,2,1,0:T(8,128)(2,1)} custom-call(f32[32,1024]{1,0:T(8,128)S(1)} %get-tuple-element.28.drive, f32[32,128]{1,0:T(8,128)S(1)} %get-tuple-element.29.b, f32[16,16]{1,0:T(8,128)S(1)} %get-tuple-element.30.keep, bf16[16,16,64,128]{3,2,1,0:T(8,128)(2,1)S(1)} %get-tuple-element.31.state), custom_call_target="tpu_custom_call" | custom-call | flops 16777216 | bytes 8388608 | tf_op jit(solution)/shard_map/state/pallas_call | solution.py:377
  26.3 2.3 %collective-permute-done.2.refs_3_ = bf16[8,1152]{1,0:T(8,128)(2,1)S(1)} collective-permute-done((bf16[8,1152]{1,0:T(8,128)(2,1)S(1)}, bf16[8,1152]{1,0:T(8,128)(2,1)S(1)}, u32[]{:S(2)}, u32[]{:S(2)}) %collective-permute-start.2) | collective-permute-done | bytes 18464 | tf_op jit(solution)/shard_map/ppermute | solution.py:365
  28.9 1.6 %collective-permute-start.4 = (f32[32,128]{1,0:T(8,128)S(1)}, f32[32,128]{1,0:T(8,128)S(1)}, u32[]{:S(2)}, u32[]{:S(2)}) collective-permute-start(f32[32,128]{1,0:T(8,128)S(1)} %get-tuple-element.43.refs_0_), channel_id=1, source_target_pairs={{0,2},{1,3},{2,0},{3,1},{4,6},{5,7},{6,4},{7,5},{8,10},{9,11},{10,... | collective-permute-start | bytes 49160 | tf_op jit(solution)/shard_map/ppermute | solution.py:407
  30.7 1.4 %collective-permute-done.5.refs_3_ = f32[32,128]{1,0:T(8,128)S(1)} collective-permute-done((f32[32,128]{1,0:T(8,128)S(1)}, f32[32,128]{1,0:T(8,128)S(1)}, u32[]{:S(2)}, u32[]{:S(2)}) %collective-permute-start.5) | collective-permute-done | bytes 16416 | tf_op jit(solution)/shard_map/ppermute | solution.py:407
  33.0 2.2 %collective-permute-start.7 = (f32[8,1024]{1,0:T(8,128)S(1)}, f32[8,1024]{1,0:T(8,128)S(1)}, u32[]{:S(2)}, u32[]{:S(2)}) collective-permute-start(f32[8,1024]{1,0:T(8,128)S(1)} %get-tuple-element.50), channel_id=1, source_target_pairs={{0,8},{4,12},{8,0},{12,4},{1,9},{5,13},{9,1},{13,5},{2,10},{6,14},... | collective-permute-start | bytes 98312 | tf_op jit(solution)/shard_map/ppermute | solution.py:365
  35.1 2.2 %collective-permute-start.8 = (f32[8,1024]{1,0:T(8,128)S(1)}, f32[8,1024]{1,0:T(8,128)S(1)}, u32[]{:S(2)}, u32[]{:S(2)}) collective-permute-start(f32[8,1024]{1,0:T(8,128)S(1)} %get-tuple-element.51), channel_id=1, source_target_pairs={{0,12},{4,8},{8,4},{12,0},{1,13},{5,9},{9,5},{13,1},{2,14},{6,10},... | collective-permute-start | bytes 98312 | tf_op jit(solution)/shard_map/ppermute | solution.py:365
  37.4 0.7 %norm.1 = bf16[2,16,1024]{2,1,0:T(8,128)(2,1)} custom-call(f32[32,1024]{1,0:T(8,128)S(1)} %get-tuple-element.32.gated, f32[32,128]{1,0:T(8,128)S(1)} %get-tuple-element.46.inverse.refs_5_, f32[1,1024]{1,0:T(1,128)S(1)} %get-tuple-element.47.gain), custom_call_target="tpu_custom_call" | custom-call | tf_op jit(solution)/shard_map/norm/pallas_call | solution.py:424
  38.1 2.8 %collective-permute-done.8.refs_3_ = f32[8,1024]{1,0:T(8,128)S(1)} collective-permute-done((f32[8,1024]{1,0:T(8,128)S(1)}, f32[8,1024]{1,0:T(8,128)S(1)}, u32[]{:S(2)}, u32[]{:S(2)}) %collective-permute-start.8) | collective-permute-done | bytes 32800 | tf_op jit(solution)/shard_map/ppermute | solution.py:365
  40.8 1.0 %final.1 = f32[2,16,1024]{2,1,0:T(8,128)} custom-call(f32[8,1024]{1,0:T(8,128)S(1)} %get-tuple-element.48.refs_0_, f32[8,1024]{1,0:T(8,128)S(1)} %collective-permute-done.6.refs_1_, f32[8,1024]{1,0:T(8,128)S(1)} %collective-permute-done.7.refs_2_, f32[8,1024]{1,0:T(8,128)S(1)} %collective-permute-done.8.refs_3_, f32[32,32]{1,0:T(8,128)S(1)} %get-tuple-element.52.refs_4_, ...), custom_call_target="tpu_custom_call" | custom-call | tf_op jit(solution)/shard_map/final/pallas_call | solution.py:433
  (28 shorter events, 2.8 us)
Async XLA Ops:
  0.6 2.2 %copy-start = (bf16[16,16,64,128]{3,2,1,0:T(8,128)(2,1)S(1)}, bf16[16,16,64,128]{3,2,1,0:T(8,128)(2,1)}, u32[]{:S(2)}) copy-start(bf16[16,16,64,128]{3,2,1,0:T(8,128)(2,1)} %refs_0_.1) | copy-start | bytes 12582916
  2.8 0.9 %copy-start.1 = (bf16[2,64,1024]{2,1,0:T(8,128)(2,1)S(1)}, bf16[2,64,1024]{2,1,0:T(8,128)(2,1)}, u32[]{:S(2)}) copy-start(bf16[2,64,1024]{2,1,0:T(8,128)(2,1)} %refs_1_.1) | copy-start | bytes 786436
  3.8 0.9 %copy-start.2 = (bf16[2,64,1024]{2,1,0:T(8,128)(2,1)S(1)}, bf16[2,64,1024]{2,1,0:T(8,128)(2,1)}, u32[]{:S(2)}) copy-start(bf16[2,64,1024]{2,1,0:T(8,128)(2,1)} %refs_2_.1) | copy-start | bytes 786436
  4.7 0.8 %copy-start.3 = (bf16[2,16,1024]{2,1,0:T(8,128)(2,1)S(1)}, bf16[2,16,1024]{2,1,0:T(8,128)(2,1)}, u32[]{:S(2)}) copy-start(bf16[2,16,1024]{2,1,0:T(8,128)(2,1)} %refs_5_.1) | copy-start | bytes 196612
  5.6 0.8 %copy-start.4 = (bf16[2,16,1024]{2,1,0:T(8,128)(2,1)S(1)}, bf16[2,16,1024]{2,1,0:T(8,128)(2,1)}, u32[]{:S(2)}) copy-start(bf16[2,16,1024]{2,1,0:T(8,128)(2,1)} %refs_6_.1) | copy-start | bytes 196612
  6.4 0.8 %copy-start.5 = (bf16[2,16,4,128]{3,2,1,0:T(4,128)(2,1)S(1)}, bf16[2,16,4,128]{3,2,1,0:T(4,128)(2,1)}, u32[]{:S(2)}) copy-start(bf16[2,16,4,128]{3,2,1,0:T(4,128)(2,1)} %refs_7_.1) | copy-start | bytes 98308
  7.2 0.8 %copy-start.6 = (bf16[2,16,4,128]{3,2,1,0:T(4,128)(2,1)S(1)}, bf16[2,16,4,128]{3,2,1,0:T(4,128)(2,1)}, u32[]{:S(2)}) copy-start(bf16[2,16,4,128]{3,2,1,0:T(4,128)(2,1)} %refs_8_.1) | copy-start | bytes 98308
  7.9 0.7 %copy-start.7 = (f32[2,16,16]{2,1,0:T(8,128)S(1)}, f32[2,16,16]{2,1,0:T(8,128)}, u32[]{:S(2)}) copy-start(f32[2,16,16]{2,1,0:T(8,128)} %refs_9_.1) | copy-start | bytes 6148
  8.6 0.7 %copy-start.8 = (bf16[1024]{0:T(1024)(128)(2,1)S(1)}, bf16[1024]{0:T(1024)(128)(2,1)}, u32[]{:S(2)}) copy-start(bf16[1024]{0:T(1024)(128)(2,1)} %param.23) | copy-start | bytes 6148
  9.3 0.7 %copy-start.9 = (s32[16]{0:T(128)S(1)}, s32[16]{0:T(128)}, u32[]{:S(2)}) copy-start(s32[16]{0:T(128)} %refs_3_.1) | copy-start | bytes 196
  10.0 0.7 %copy-start.10 = (s32[8]{0:T(128)S(1)}, s32[8]{0:T(128)}, u32[]{:S(2)}) copy-start(s32[8]{0:T(128)} %refs_4_.1) | copy-start | bytes 100
  10.6 0.7 %copy-start.11 = (f32[16]{0:T(128)S(1)}, f32[16]{0:T(128)}, u32[]{:S(2)}) copy-start(f32[16]{0:T(128)} %param.20) | copy-start | bytes 196
  11.3 0.7 %copy-start.12 = (f32[16]{0:T(128)S(1)}, f32[16]{0:T(128)}, u32[]{:S(2)}) copy-start(f32[16]{0:T(128)} %param.21) | copy-start | bytes 196
  11.9 0.7 %copy-start.13 = (f32[16]{0:T(128)S(1)}, f32[16]{0:T(128)}, u32[]{:S(2)}) copy-start(f32[16]{0:T(128)} %param.22) | copy-start | bytes 196
  17.3 9.0 %collective-permute-start = (bf16[8,1152]{1,0:T(8,128)(2,1)S(1)}, bf16[8,1152]{1,0:T(8,128)(2,1)S(1)}, u32[]{:S(2)}, u32[]{:S(2)}) collective-permute-start(bf16[8,1152]{1,0:T(8,128)(2,1)S(1)} %get-tuple-element.34), channel_id=1, source_target_pairs={{0,4},{4,0},{8,12},{12,8},{1,5},{5,1},{9,13},{13,9},{2,6},{6,2},{1... | collective-permute-start | bytes 55304 | tf_op jit(solution)/shard_map/ppermute | solution.py:365
  20.4 5.9 %collective-permute-start.1 = (bf16[8,1152]{1,0:T(8,128)(2,1)S(1)}, bf16[8,1152]{1,0:T(8,128)(2,1)S(1)}, u32[]{:S(2)}, u32[]{:S(2)}) collective-permute-start(bf16[8,1152]{1,0:T(8,128)(2,1)S(1)} %get-tuple-element.35), channel_id=1, source_target_pairs={{0,8},{4,12},{8,0},{12,4},{1,9},{5,13},{9,1},{13,5},{2,10},{6,14},... | collective-permute-start | bytes 55304 | tf_op jit(solution)/shard_map/ppermute | solution.py:365
  23.0 5.6 %collective-permute-start.2 = (bf16[8,1152]{1,0:T(8,128)(2,1)S(1)}, bf16[8,1152]{1,0:T(8,128)(2,1)S(1)}, u32[]{:S(2)}, u32[]{:S(2)}) collective-permute-start(bf16[8,1152]{1,0:T(8,128)(2,1)S(1)} %get-tuple-element.36), channel_id=1, source_target_pairs={{0,12},{4,8},{8,4},{12,0},{1,13},{5,9},{9,5},{13,1},{2,14},{6,10},... | collective-permute-start | bytes 55304 | tf_op jit(solution)/shard_map/ppermute | solution.py:365
  28.8 3.4 %collective-permute-start.5 = (f32[32,128]{1,0:T(8,128)S(1)}, f32[32,128]{1,0:T(8,128)S(1)}, u32[]{:S(2)}, u32[]{:S(2)}) collective-permute-start(f32[32,128]{1,0:T(8,128)S(1)} %get-tuple-element.43.refs_0_), channel_id=1, source_target_pairs={{0,3},{1,2},{2,1},{3,0},{4,7},{5,6},{6,5},{7,4},{8,11},{9,10},{10,... | collective-permute-start | bytes 49160 | tf_op jit(solution)/shard_map/ppermute | solution.py:407
  28.9 3.8 %collective-permute-start.4 = (f32[32,128]{1,0:T(8,128)S(1)}, f32[32,128]{1,0:T(8,128)S(1)}, u32[]{:S(2)}, u32[]{:S(2)}) collective-permute-start(f32[32,128]{1,0:T(8,128)S(1)} %get-tuple-element.43.refs_0_), channel_id=1, source_target_pairs={{0,2},{1,3},{2,0},{3,1},{4,6},{5,7},{6,4},{7,5},{8,10},{9,11},{10,... | collective-permute-start | bytes 49160 | tf_op jit(solution)/shard_map/ppermute | solution.py:407
  30.4 2.2 %collective-permute-start.3 = (f32[32,128]{1,0:T(8,128)S(1)}, f32[32,128]{1,0:T(8,128)S(1)}, u32[]{:S(2)}, u32[]{:S(2)}) collective-permute-start(f32[32,128]{1,0:T(8,128)S(1)} %get-tuple-element.43.refs_0_), channel_id=1, source_target_pairs={{0,1},{1,0},{2,3},{3,2},{4,5},{5,4},{6,7},{7,6},{8,9},{9,8},{10,11... | collective-permute-start | bytes 49160 | tf_op jit(solution)/shard_map/ppermute | solution.py:407
  32.9 5.2 %collective-permute-start.6 = (f32[8,1024]{1,0:T(8,128)S(1)}, f32[8,1024]{1,0:T(8,128)S(1)}, u32[]{:S(2)}, u32[]{:S(2)}) collective-permute-start(f32[8,1024]{1,0:T(8,128)S(1)} %get-tuple-element.49), channel_id=1, source_target_pairs={{0,4},{4,0},{8,12},{12,8},{1,5},{5,1},{9,13},{13,9},{2,6},{6,2},{1... | collective-permute-start | bytes 98312 | tf_op jit(solution)/shard_map/ppermute | solution.py:365
  33.0 5.1 %collective-permute-start.7 = (f32[8,1024]{1,0:T(8,128)S(1)}, f32[8,1024]{1,0:T(8,128)S(1)}, u32[]{:S(2)}, u32[]{:S(2)}) collective-permute-start(f32[8,1024]{1,0:T(8,128)S(1)} %get-tuple-element.50), channel_id=1, source_target_pairs={{0,8},{4,12},{8,0},{12,4},{1,9},{5,13},{9,1},{13,5},{2,10},{6,14},... | collective-permute-start | bytes 98312 | tf_op jit(solution)/shard_map/ppermute | solution.py:365
  35.1 5.7 %collective-permute-start.8 = (f32[8,1024]{1,0:T(8,128)S(1)}, f32[8,1024]{1,0:T(8,128)S(1)}, u32[]{:S(2)}, u32[]{:S(2)}) collective-permute-start(f32[8,1024]{1,0:T(8,128)S(1)} %get-tuple-element.51), channel_id=1, source_target_pairs={{0,12},{4,8},{8,4},{12,0},{1,13},{5,9},{9,5},{13,1},{2,14},{6,10},... | collective-permute-start | bytes 98312 | tf_op jit(solution)/shard_map/ppermute | solution.py:365

commit v3 on v2

--- a/solution.py
+++ b/solution.py
@@ -355,7 +355,7 @@
             transcendentals=0,
         ),
         name="front",
-    )(session_head_state, adapter_down_weight, adapter_up_weight, *smalls)
+    )(*[pltpu.with_memory_space_constraint(v, pltpu.HBM) for v in (session_head_state, adapter_down_weight, adapter_up_weight, *smalls)])
     msgs = out[:n_msg]
     gated, squares, drive, b_rows, keep, place, gain, held_state, down, up = out[n_msg:]
 

time: 42.4 us -> 31.2 us (0.74)
  local copies, waits for them, and re-layouts: 11.9 us -> 0 us
  Pallas kernels: 10.1 us -> 11.2 us
    unnamed x28 -> x0, local copies, waits for them, and re-layouts: 11.9 us -> none
    pallas_call x1, Pallas kernels: 4.7 us -> 5.87 us  [per_device(): pl.pallas_call(functools.partial(front_kernel, dims), out_shape=[shape((m...]
  transfers between devices with their start and end apart: 9 -> 9, of which waited for: 4 -> 4; matrix products, arithmetic and copies ran while one was open for 0% -> 0% of each run, Pallas kernels for 10% -> 13%
where the time goes in v3:
time: 31.2 us; the launch traced here: 31 us
  starting transfers between devices  12.1 us (39%)
  Pallas kernels  11.2 us (36%)
  waiting for transfers between devices  6.98 us (22%)
  between operations  0.7 us (2%)
    ppermute x6, starting transfers between devices, exchange(): lax.ppermute(blocks[k], 'batch', [(i, i ^ k) for i in range(batch_count)])  10.1 us
    pallas_call x1, Pallas kernels, per_device(): pl.pallas_call(functools.partial(front_kernel, dims), out_shape=[shape((m...  5.87 us
    ppermute x6, waiting for transfers between devices, exchange(): lax.ppermute(blocks[k], 'batch', [(i, i ^ k) for i in range(batch_count)])  5.03 us
    pallas_call x1, Pallas kernels, per_device(): pl.pallas_call(functools.partial(state_kernel, pair), out_shape=shape(ses...  3.27 us
    ppermute x3, waiting for transfers between devices, per_device(): lax.ppermute(partial, 'tensor', [(i, i ^ k) for i in range(tensor_count)])  1.96 us
    ppermute x3, starting transfers between devices, per_device(): lax.ppermute(partial, 'tensor', [(i, i ^ k) for i in range(tensor_count)])  1.96 us
    pallas_call x1, Pallas kernels, per_device(): pl.pallas_call(functools.partial(final_kernel, n_msg), out_shape=shape((D...  0.97 us
    pallas_call x1, Pallas kernels, per_device(): pl.pallas_call(norm_kernel, out_shape=shape((DECODE_STEPS, sessions, chan...  0.71 us
  transfers between devices with their start and end apart: 9, of which 4 were waited for; matrix products, arithmetic and copies ran while one was open for 0% of the time, Pallas kernels for 13%

profile of v3, /device:TPU:0, one launch (start us, length us, event | category | flops | bytes accessed | tf_op | source)
XLA Modules:
  0.0 31.0 jit_solution(2092555421632053577)
XLA Ops:
  0.6 5.9 %front.1 = (bf16[8,1152]{1,0:T(8,128)(2,1)S(1)}, bf16[8,1152]{1,0:T(8,128)(2,1)S(1)}, bf16[8,1152]{1,0:T(8,128)(2,1)S(1)}, bf16[8,1152]{1,0:T(8,128)(2,1)S(1)}, ...) custom-call(bf16[16,16,64,128]{3,2,1,0:T(8,128)(2,1)} %refs_0_.1, ...), custom_call_target="tpu_custom_call" | custom-call | flops 134217728 | bytes 4194304 | tf_op jit(solution)/shard_map/front/pallas_call | solution.py:326
  6.5 3.1 %collective-permute-start = (bf16[8,1152]{1,0:T(8,128)(2,1)S(1)}, bf16[8,1152]{1,0:T(8,128)(2,1)S(1)}, u32[]{:S(2)}, u32[]{:S(2)}) collective-permute-start(bf16[8,1152]{1,0:T(8,128)(2,1)S(1)} %get-tuple-element.34), channel_id=1, source_target_pairs={{0,4},{4,0},{8,12},{12,8},{1,5},{5,1},{9,13},{13,9},{2,6},{6,2},{1... | collective-permute-start | bytes 55304 | tf_op jit(solution)/shard_map/ppermute | solution.py:365
  9.6 2.6 %collective-permute-start.1 = (bf16[8,1152]{1,0:T(8,128)(2,1)S(1)}, bf16[8,1152]{1,0:T(8,128)(2,1)S(1)}, u32[]{:S(2)}, u32[]{:S(2)}) collective-permute-start(bf16[8,1152]{1,0:T(8,128)(2,1)S(1)} %get-tuple-element.35), channel_id=1, source_target_pairs={{0,8},{4,12},{8,0},{12,4},{1,9},{5,13},{9,1},{13,5},{2,10},{6,14},... | collective-permute-start | bytes 55304 | tf_op jit(solution)/shard_map/ppermute | solution.py:365
  12.2 0.0 collective-permute-start.2
  12.2 3.3 %state.1 = bf16[16,16,64,128]{3,2,1,0:T(8,128)(2,1)} custom-call(f32[32,1024]{1,0:T(8,128)S(1)} %get-tuple-element.28.drive, f32[32,128]{1,0:T(8,128)S(1)} %get-tuple-element.29.b, f32[16,16]{1,0:T(8,128)S(1)} %get-tuple-element.30.keep, bf16[16,16,64,128]{3,2,1,0:T(8,128)(2,1)S(1)} %get-tuple-element.31.state), custom_call_target="tpu_custom_call" | custom-call | flops 16777216 | bytes 8388608 | tf_op jit(solution)/shard_map/state/pallas_call | solution.py:377
  15.5 0.0 collective-permute-done.refs_1_
  15.5 0.0 collective-permute-done.1.refs_2_
  15.5 2.3 %collective-permute-done.2.refs_3_ = bf16[8,1152]{1,0:T(8,128)(2,1)S(1)} collective-permute-done((bf16[8,1152]{1,0:T(8,128)(2,1)S(1)}, bf16[8,1152]{1,0:T(8,128)(2,1)S(1)}, u32[]{:S(2)}, u32[]{:S(2)}) %collective-permute-start.2) | collective-permute-done | bytes 18464 | tf_op jit(solution)/shard_map/ppermute | solution.py:365
  17.8 0.2 down.1
  18.0 0.1 collective-permute-start.5
  18.1 1.6 %collective-permute-start.4 = (f32[32,128]{1,0:T(8,128)S(1)}, f32[32,128]{1,0:T(8,128)S(1)}, u32[]{:S(2)}, u32[]{:S(2)}) collective-permute-start(f32[32,128]{1,0:T(8,128)S(1)} %get-tuple-element.43.refs_0_), channel_id=1, source_target_pairs={{0,2},{1,3},{2,0},{3,1},{4,6},{5,7},{6,4},{7,5},{8,10},{9,11},{10,... | collective-permute-start | bytes 49160 | tf_op jit(solution)/shard_map/ppermute | solution.py:407
  19.6 0.3 collective-permute-start.3
  19.9 1.4 %collective-permute-done.5.refs_3_ = f32[32,128]{1,0:T(8,128)S(1)} collective-permute-done((f32[32,128]{1,0:T(8,128)S(1)}, f32[32,128]{1,0:T(8,128)S(1)}, u32[]{:S(2)}, u32[]{:S(2)}) %collective-permute-start.5) | collective-permute-done | bytes 16416 | tf_op jit(solution)/shard_map/ppermute | solution.py:407
  21.4 0.5 %collective-permute-done.4.refs_2_ = f32[32,128]{1,0:T(8,128)S(1)} collective-permute-done((f32[32,128]{1,0:T(8,128)S(1)}, f32[32,128]{1,0:T(8,128)S(1)}, u32[]{:S(2)}, u32[]{:S(2)}) %collective-permute-start.4) | collective-permute-done | bytes 16416 | tf_op jit(solution)/shard_map/ppermute | solution.py:407
  21.9 0.0 collective-permute-done.3.refs_1_
  21.9 0.2 up.1
  22.1 0.1 collective-permute-start.6
  22.2 2.2 %collective-permute-start.7 = (f32[8,1024]{1,0:T(8,128)S(1)}, f32[8,1024]{1,0:T(8,128)S(1)}, u32[]{:S(2)}, u32[]{:S(2)}) collective-permute-start(f32[8,1024]{1,0:T(8,128)S(1)} %get-tuple-element.50), channel_id=1, source_target_pairs={{0,8},{4,12},{8,0},{12,4},{1,9},{5,13},{9,1},{13,5},{2,10},{6,14},... | collective-permute-start | bytes 98312 | tf_op jit(solution)/shard_map/ppermute | solution.py:365
  24.3 2.2 %collective-permute-start.8 = (f32[8,1024]{1,0:T(8,128)S(1)}, f32[8,1024]{1,0:T(8,128)S(1)}, u32[]{:S(2)}, u32[]{:S(2)}) collective-permute-start(f32[8,1024]{1,0:T(8,128)S(1)} %get-tuple-element.51), channel_id=1, source_target_pairs={{0,12},{4,8},{8,4},{12,0},{1,13},{5,9},{9,5},{13,1},{2,14},{6,10},... | collective-permute-start | bytes 98312 | tf_op jit(solution)/shard_map/ppermute | solution.py:365
  26.6 0.7 %norm.1 = bf16[2,16,1024]{2,1,0:T(8,128)(2,1)} custom-call(f32[32,1024]{1,0:T(8,128)S(1)} %get-tuple-element.32.gated, f32[32,128]{1,0:T(8,128)S(1)} %get-tuple-element.46.inverse.refs_5_, f32[1,1024]{1,0:T(1,128)S(1)} %get-tuple-element.47.gain), custom_call_target="tpu_custom_call" | custom-call | tf_op jit(solution)/shard_map/norm/pallas_call | solution.py:424
  27.3 0.0 collective-permute-done.6.refs_1_
  27.3 0.0 collective-permute-done.7.refs_2_
  27.3 2.8 %collective-permute-done.8.refs_3_ = f32[8,1024]{1,0:T(8,128)S(1)} collective-permute-done((f32[8,1024]{1,0:T(8,128)S(1)}, f32[8,1024]{1,0:T(8,128)S(1)}, u32[]{:S(2)}, u32[]{:S(2)}) %collective-permute-start.8) | collective-permute-done | bytes 32800 | tf_op jit(solution)/shard_map/ppermute | solution.py:365
  30.1 1.0 %final.1 = f32[2,16,1024]{2,1,0:T(8,128)} custom-call(f32[8,1024]{1,0:T(8,128)S(1)} %get-tuple-element.48.refs_0_, f32[8,1024]{1,0:T(8,128)S(1)} %collective-permute-done.6.refs_1_, f32[8,1024]{1,0:T(8,128)S(1)} %collective-permute-done.7.refs_2_, f32[8,1024]{1,0:T(8,128)S(1)} %collective-permute-done.8.refs_3_, f32[32,32]{1,0:T(8,128)S(1)} %get-tuple-element.52.refs_4_, ...), custom_call_target="tpu_custom_call" | custom-call | tf_op jit(solution)/shard_map/final/pallas_call | solution.py:433
Async XLA Ops:
  6.5 9.0 %collective-permute-start = (bf16[8,1152]{1,0:T(8,128)(2,1)S(1)}, bf16[8,1152]{1,0:T(8,128)(2,1)S(1)}, u32[]{:S(2)}, u32[]{:S(2)}) collective-permute-start(bf16[8,1152]{1,0:T(8,128)(2,1)S(1)} %get-tuple-element.34), channel_id=1, source_target_pairs={{0,4},{4,0},{8,12},{12,8},{1,5},{5,1},{9,13},{13,9},{2,6},{6,2},{1... | collective-permute-start | bytes 55304 | tf_op jit(solution)/shard_map/ppermute | solution.py:365
  9.6 5.9 %collective-permute-start.1 = (bf16[8,1152]{1,0:T(8,128)(2,1)S(1)}, bf16[8,1152]{1,0:T(8,128)(2,1)S(1)}, u32[]{:S(2)}, u32[]{:S(2)}) collective-permute-start(bf16[8,1152]{1,0:T(8,128)(2,1)S(1)} %get-tuple-element.35), channel_id=1, source_target_pairs={{0,8},{4,12},{8,0},{12,4},{1,9},{5,13},{9,1},{13,5},{2,10},{6,14},... | collective-permute-start | bytes 55304 | tf_op jit(solution)/shard_map/ppermute | solution.py:365
  12.2 5.6 %collective-permute-start.2 = (bf16[8,1152]{1,0:T(8,128)(2,1)S(1)}, bf16[8,1152]{1,0:T(8,128)(2,1)S(1)}, u32[]{:S(2)}, u32[]{:S(2)}) collective-permute-start(bf16[8,1152]{1,0:T(8,128)(2,1)S(1)} %get-tuple-element.36), channel_id=1, source_target_pairs={{0,12},{4,8},{8,4},{12,0},{1,13},{5,9},{9,5},{13,1},{2,14},{6,10},... | collective-permute-start | bytes 55304 | tf_op jit(solution)/shard_map/ppermute | solution.py:365
  18.0 3.4 %collective-permute-start.5 = (f32[32,128]{1,0:T(8,128)S(1)}, f32[32,128]{1,0:T(8,128)S(1)}, u32[]{:S(2)}, u32[]{:S(2)}) collective-permute-start(f32[32,128]{1,0:T(8,128)S(1)} %get-tuple-element.43.refs_0_), channel_id=1, source_target_pairs={{0,3},{1,2},{2,1},{3,0},{4,7},{5,6},{6,5},{7,4},{8,11},{9,10},{10,... | collective-permute-start | bytes 49160 | tf_op jit(solution)/shard_map/ppermute | solution.py:407
  18.1 3.8 %collective-permute-start.4 = (f32[32,128]{1,0:T(8,128)S(1)}, f32[32,128]{1,0:T(8,128)S(1)}, u32[]{:S(2)}, u32[]{:S(2)}) collective-permute-start(f32[32,128]{1,0:T(8,128)S(1)} %get-tuple-element.43.refs_0_), channel_id=1, source_target_pairs={{0,2},{1,3},{2,0},{3,1},{4,6},{5,7},{6,4},{7,5},{8,10},{9,11},{10,... | collective-permute-start | bytes 49160 | tf_op jit(solution)/shard_map/ppermute | solution.py:407
  19.6 2.3 %collective-permute-start.3 = (f32[32,128]{1,0:T(8,128)S(1)}, f32[32,128]{1,0:T(8,128)S(1)}, u32[]{:S(2)}, u32[]{:S(2)}) collective-permute-start(f32[32,128]{1,0:T(8,128)S(1)} %get-tuple-element.43.refs_0_), channel_id=1, source_target_pairs={{0,1},{1,0},{2,3},{3,2},{4,5},{5,4},{6,7},{7,6},{8,9},{9,8},{10,11... | collective-permute-start | bytes 49160 | tf_op jit(solution)/shard_map/ppermute | solution.py:407
  22.1 5.2 %collective-permute-start.6 = (f32[8,1024]{1,0:T(8,128)S(1)}, f32[8,1024]{1,0:T(8,128)S(1)}, u32[]{:S(2)}, u32[]{:S(2)}) collective-permute-start(f32[8,1024]{1,0:T(8,128)S(1)} %get-tuple-element.49), channel_id=1, source_target_pairs={{0,4},{4,0},{8,12},{12,8},{1,5},{5,1},{9,13},{13,9},{2,6},{6,2},{1... | collective-permute-start | bytes 98312 | tf_op jit(solution)/shard_map/ppermute | solution.py:365
  22.2 5.1 %collective-permute-start.7 = (f32[8,1024]{1,0:T(8,128)S(1)}, f32[8,1024]{1,0:T(8,128)S(1)}, u32[]{:S(2)}, u32[]{:S(2)}) collective-permute-start(f32[8,1024]{1,0:T(8,128)S(1)} %get-tuple-element.50), channel_id=1, source_target_pairs={{0,8},{4,12},{8,0},{12,4},{1,9},{5,13},{9,1},{13,5},{2,10},{6,14},... | collective-permute-start | bytes 98312 | tf_op jit(solution)/shard_map/ppermute | solution.py:365
  24.3 5.7 %collective-permute-start.8 = (f32[8,1024]{1,0:T(8,128)S(1)}, f32[8,1024]{1,0:T(8,128)S(1)}, u32[]{:S(2)}, u32[]{:S(2)}) collective-permute-start(f32[8,1024]{1,0:T(8,128)S(1)} %get-tuple-element.51), channel_id=1, source_target_pairs={{0,12},{4,8},{8,4},{12,0},{1,13},{5,9},{9,5},{13,1},{2,14},{6,10},... | collective-permute-start | bytes 98312 | tf_op jit(solution)/shard_map/ppermute | solution.py:365

commit v4 on v3

--- a/solution.py
+++ b/solution.py
@@ -27,47 +27,116 @@
     return lax.broadcasted_iota(jnp.int32, shape, axis)
 
 
+def thirds(v):
+    high = v.astype(BF16)
+    rest = v - high.astype(F32)
+    middle = rest.astype(BF16)
+    return [high, middle, (rest - middle.astype(F32)).astype(BF16)]
+
+
 def front_kernel(dims, *refs):
     sessions, heads, batch_count, capacity, adapters_held, chunks, split = dims
     n_msg = batch_count if split else 1
-    inputs, refs = refs[:14], refs[14:]
+    inputs, refs = refs[:12], refs[12:]
     msgs, refs = refs[:n_msg], refs[n_msg:]
     gated_ref, square_ref, drive_ref, b_ref, keep_ref, place_ref, gain_ref = refs[:7]
-    held, down_out, up_out = refs[7:10]
-    local, (sems, small_sems, weight_sems, counts) = refs[10:21], refs[21:]
-    state, down, up = inputs[:3]
+    held = refs[7]
+    local, (sems, small_sems, counts) = refs[8:19], refs[19:]
+    state = inputs[0]
     channels = heads * HEAD_CHANNELS
     rows = DECODE_STEPS * sessions
-    part = heads // chunks
-    width = part * HEAD_CHANNELS
+    part = sessions // chunks
 
     loads = [
         pltpu.make_async_copy(source, target, small_sems.at[i])
-        for i, (source, target) in enumerate(zip(inputs[3:], local))
+        for i, (source, target) in enumerate(zip(inputs[1:], local))
     ]
     for load in loads:
         load.start()
     copies = []
     for i in range(chunks):
         window = pl.ds(i * part, part)
-        copy = pltpu.make_async_copy(state.at[:, window], held.at[:, window], sems.at[i])
+        copy = pltpu.make_async_copy(state.at[window], held.at[window], sems.at[i])
         copy.start()
         copies.append(copy)
-    weights = [
-        pltpu.make_async_copy(down, down_out, weight_sems.at[0]),
-        pltpu.make_async_copy(up, up_out, weight_sems.at[1]),
-    ]
-    for load in weights:
-        load.start()
     adapter, slot_of, x, z, b, c, raw, bias, rate, skip, gain_rows = local
     me = lax.axis_index("batch")
     group = lax.axis_index("tensor") * heads // (HEAD_COUNT // GROUPS)
     for load in loads:
         load.wait()
+    def pick_group(ref):
+        values = ref[...].astype(F32).reshape(rows, GROUPS, LANES)
+        return jnp.sum(jnp.where(iota(values.shape, 1) == group, values, 0.0), axis=1)
+
+    b_rows = pick_group(b)
+    c_rows = pick_group(c)
+    b_ref[...] = b_rows
+    row_session = iota((rows, LANES), 0) % sessions
+    c_blocks = jnp.concatenate(
+        [jnp.where(row_session == s, c_rows, 0.0).astype(BF16) for s in range(sessions)], axis=1
+    )
+    def read(i):
+        copies[i].wait()
+        lanes = slice(i * part * LANES, (i + 1) * part * LANES)
+        block = jnp.concatenate(
+            [held[i * part + s].reshape(channels, LANES) for s in range(part)], axis=1
+        )
+        return lax.dot_general(c_blocks[:, lanes], block, NT, preferred_element_type=F32)
+
+    reads = read(0)
+    b1, b2 = b_rows[:sessions], b_rows[sessions:]
+    c1, c2 = c_rows[:sessions], c_rows[sessions:]
+    bc11 = jnp.sum(b1 * c1, axis=1, keepdims=True)
+    bc12 = jnp.sum(b1 * c2, axis=1, keepdims=True)
+    bc22 = jnp.sum(b2 * c2, axis=1, keepdims=True)
+
+    def softplus(v):
+        return jnp.maximum(v, 0.0) + jnp.log1p(jnp.exp(-jnp.abs(v)))
+
+    step1 = softplus(raw[0] + bias[...])
+    step2 = softplus(raw[1] + bias[...])
+    speed = -jnp.exp(rate[...])
+    decay1 = jnp.exp(speed * step1)
+    decay2 = jnp.exp(speed * step2)
+    keep = decay1 * decay2
+    keep_ref[...] = keep
+    factors = jnp.concatenate(
+        [
+            decay1,
+            step1 * bc11 + skip[...],
+            keep,
+            decay2 * step1 * bc12,
+            step2 * bc22 + skip[...],
+            decay2 * step1,
+            step2,
+        ],
+        axis=0,
+    )
+    reads = reads + read(1)
     gain = jnp.concatenate(
         [gain_rows[i : i + 1].astype(F32) for i in range(channels // LANES)], axis=1
     )
     gain_ref[...] = gain
+    spread = (iota((heads, channels), 1) // HEAD_CHANNELS == iota((heads, channels), 0)).astype(F32)
+    wide = jnp.dot(
+        jnp.concatenate(thirds(factors), axis=1),
+        jnp.concatenate([spread] * 3, axis=0).astype(BF16),
+        preferred_element_type=F32,
+    )
+    wide = [wide[i * sessions : (i + 1) * sessions] for i in range(7)]
+    x1 = x[0].astype(F32)
+    x2 = x[1].astype(F32)
+    drive = jnp.concatenate([wide[5] * x1, wide[6] * x2], axis=0)
+    base1 = x1 * wide[1]
+    base2 = x1 * wide[3] + x2 * wide[4]
+    gates = jnp.concatenate([z[0].astype(F32), z[1].astype(F32)], axis=0)
+    gates = gates / (1.0 + jnp.exp(-gates))
+    base = jnp.concatenate([base1, base2], axis=0)
+    scale = jnp.concatenate([wide[0], wide[2]], axis=0)
+    reads = reads + read(2)
+    high = drive.astype(BF16)
+    low = (drive - high.astype(F32)).astype(BF16)
+    drive_ref[...] = jnp.concatenate([high, low], axis=0).T
     for i in range(batch_count):
         counts[i] = 0
     per_owner = DECODE_STEPS * capacity
@@ -92,115 +161,45 @@
     place_ref[...] = place
     place_bf = place.astype(BF16)
 
-    def pick_group(ref):
-        values = ref[...].astype(F32).reshape(rows, GROUPS, LANES)
-        return jnp.sum(jnp.where(iota(values.shape, 1) == group, values, 0.0), axis=1)
-
-    b_rows = pick_group(b)
-    c_rows = pick_group(c)
-    b_ref[...] = b_rows
-    b1, b2 = b_rows[:sessions], b_rows[sessions:]
-    c1, c2 = c_rows[:sessions], c_rows[sessions:]
-    bc11 = jnp.sum(b1 * c1, axis=1, keepdims=True)
-    bc12 = jnp.sum(b1 * c2, axis=1, keepdims=True)
-    bc22 = jnp.sum(b2 * c2, axis=1, keepdims=True)
-
-    def softplus(v):
-        return jnp.maximum(v, 0.0) + jnp.log1p(jnp.exp(-jnp.abs(v)))
-
-    step1 = softplus(raw[0] + bias[...])
-    step2 = softplus(raw[1] + bias[...])
-    speed = -jnp.exp(rate[...])
-    decay1 = jnp.exp(speed * step1)
-    decay2 = jnp.exp(speed * step2)
-    keep = decay1 * decay2
-    keep_ref[...] = keep
-    factors = jnp.concatenate(
-        [
-            decay1,
-            step1 * bc11 + skip[...],
-            keep,
-            decay2 * step1 * bc12,
-            step2 * bc22 + skip[...],
-            decay2 * step1,
-            step2,
-        ],
-        axis=0,
-    )
-    spread = (iota((heads, channels), 1) // HEAD_CHANNELS == iota((heads, channels), 0)).astype(F32)
-    wide = jnp.dot(factors, spread, precision=HIGHEST, preferred_element_type=F32)
-    wide = [wide[i * sessions : (i + 1) * sessions] for i in range(7)]
-    x1 = x[0].astype(F32)
-    x2 = x[1].astype(F32)
-    drive_ref[...] = jnp.concatenate([wide[5] * x1, wide[6] * x2], axis=0)
-    base1 = x1 * wide[1]
-    base2 = x1 * wide[3] + x2 * wide[4]
-    gates = jnp.concatenate([z[0].astype(F32), z[1].astype(F32)], axis=0)
-    gates = gates / (1.0 + jnp.exp(-gates))
-    base = jnp.concatenate([base1, base2], axis=0)
-    scale = jnp.concatenate([wide[0], wide[2]], axis=0)
-    row_session = iota((rows, LANES), 0) % sessions
-    c_blocks = jnp.concatenate(
-        [jnp.where(row_session == s, c_rows, 0.0).astype(BF16) for s in range(sessions)], axis=1
-    )
+    reads = reads + read(3)
+    gated = (scale * reads + base) * gates
+    gated_ref[...] = gated
     squares = jnp.zeros((rows, LANES), F32)
-    for i in range(chunks):
-        copies[i].wait()
-        lanes = slice(i * width, (i + 1) * width)
-        block = jnp.concatenate(
-            [
-                held[s, i * part : (i + 1) * part].reshape(width, LANES)
-                for s in range(sessions)
-            ],
-            axis=1,
-        )
-        reads = lax.dot_general(c_blocks, block, NT, preferred_element_type=F32)
-        gated = (scale[:, lanes] * reads + base[:, lanes]) * gates[:, lanes]
-        gated_ref[:, lanes] = gated
-        for j in range(width // LANES):
-            piece = gated[:, j * LANES : (j + 1) * LANES]
-            squares = squares + piece * piece
-        weighted = (gated * gain[:, lanes]).astype(BF16)
-        packed = jnp.dot(place_bf, weighted, preferred_element_type=F32)
-        for k in range(n_msg):
-            n = targets // n_msg
-            msgs[k][:, lanes] = packed[k * n : (k + 1) * n].astype(BF16)
+    for j in range(channels // LANES):
+        piece = gated[:, j * LANES : (j + 1) * LANES]
+        squares = squares + piece * piece
+    weighted = (gated * gain).astype(BF16)
+    packed = jnp.dot(place_bf, weighted, preferred_element_type=F32)
+    for k in range(n_msg):
+        n = targets // n_msg
+        msgs[k][:, :channels] = packed[k * n : (k + 1) * n].astype(BF16)
     for k in range(n_msg):
         n = targets // n_msg
         msgs[k][:, channels:] = pick[k * n : (k + 1) * n].astype(BF16)
     square_ref[...] = squares[:, :RANK] + squares[:, RANK:]
-    for load in weights:
-        load.wait()
-
-
-def state_kernel(pair, drive, b, keep, state, out, made, sems):
-    sessions, heads, _, _ = state.shape
-    rows = DECODE_STEPS * sessions
-    turned = drive[...].T
-    high = turned.astype(BF16)
-    low = (turned - high.astype(F32)).astype(BF16)
-    left = jnp.concatenate([high, low], axis=1)
+
+
+def state_kernel(pair, left, b, keep, state, out):
+    sessions, heads = state.shape[:2]
+    rows = b.shape[0]
     row_session = iota((rows, LANES), 0) % sessions
     b_rows = b[...]
-    copies = []
-    for i in range(sessions // pair):
+    for start in range(0, sessions, pair):
         right = jnp.concatenate(
-            [jnp.where(row_session == i * pair + q, b_rows, 0.0) for q in range(pair)], axis=1
+            [jnp.where(row_session == start + q, b_rows, 0.0) for q in range(pair)], axis=1
         )
         right = jnp.concatenate([right, right], axis=0).astype(BF16)
         for h in range(heads):
             piece = slice(h * HEAD_CHANNELS, (h + 1) * HEAD_CHANNELS)
             added = jnp.dot(left[piece], right, preferred_element_type=F32)
             for q in range(pair):
-                s = i * pair + q
-                kept = state[s, h].astype(F32) * keep[s, h]
-                made[s, h] = (kept + added[:, q * LANES : (q + 1) * LANES]).astype(BF16)
-        window = pl.ds(i * pair, pair)
-        copy = pltpu.make_async_copy(made.at[window], out.at[window], sems.at[i])
-        copy.start()
-        copies.append(copy)
-    for copy in copies:
-        copy.wait()
+                kept = state[start + q, h].astype(F32) * keep[start + q, h]
+                out[start + q, h] = (kept + added[:, q * LANES : (q + 1) * LANES]).astype(BF16)
+
+
+def norm_kernel(gated, inverse, gain, out):
+    normed = gated[...] * inverse[:, :1] * gain[...]
+    out[...] = normed.astype(BF16).reshape(out.shape)
 
 
 def down_kernel(n_msg, *refs):
@@ -252,18 +251,16 @@
     inverse[...] = jnp.broadcast_to(factor, inverse.shape)
 
 
-def norm_kernel(gated, inverse, gain, out):
-    rows, channels = gated.shape
-    normed = gated[...] * inverse[:, :1] * gain[...]
-    out[...] = normed.astype(BF16).reshape(out.shape)
-
-
 def final_kernel(n_msg, *refs):
     msgs = refs[:n_msg]
     place, inverse, out = refs[n_msg:]
-    terms = jnp.concatenate([m[...].astype(F32) for m in msgs], axis=0)
+    terms = jnp.concatenate([m[...] for m in msgs], axis=0)
+    one_hot = place[...].astype(BF16)
     mine = lax.dot_general(
-        place[...], terms, (((0,), (0,)), ((), ())), precision=HIGHEST, preferred_element_type=F32
+        jnp.concatenate([one_hot] * 3, axis=0),
+        jnp.concatenate(thirds(terms), axis=0),
+        (((0,), (0,)), ((), ())),
+        preferred_element_type=F32,
     )
     out[...] = (mine * inverse[:, :1]).reshape(out.shape)
 
@@ -329,23 +326,20 @@
         + [
             shape((rows, channels), F32),
             shape((rows, RANK), F32),
-            shape((rows, channels), F32),
+            shape((channels, 2 * rows), BF16),
             shape((rows, LANES), F32),
             shape((sessions, heads), F32),
             shape((targets, rows), F32),
             shape((1, channels), F32),
             shape(session_head_state.shape, BF16),
-            shape(adapter_down_weight.shape, BF16),
-            shape(adapter_up_weight.shape, BF16),
         ],
-        in_specs=[pl.BlockSpec(memory_space=pltpu.HBM)] * 14,
-        out_specs=[vmem()] * (n_msg + 10),
+        in_specs=[pl.BlockSpec(memory_space=pltpu.HBM)] * 12,
+        out_specs=[vmem()] * (n_msg + 8),
         scratch_shapes=[pltpu.SMEM(v.shape, v.dtype) for v in smalls[:2]]
         + [pltpu.VMEM(v.shape, v.dtype) for v in smalls[2:]]
         + [
             pltpu.SemaphoreType.DMA((chunks,)),
             pltpu.SemaphoreType.DMA((len(smalls),)),
-            pltpu.SemaphoreType.DMA((2,)),
             pltpu.SMEM((batch_count,), jnp.int32),
         ],
         compiler_params=pltpu.CompilerParams(vmem_limit_bytes=16 << 20),
@@ -355,9 +349,9 @@
             transcendentals=0,
         ),
         name="front",
-    )(*[pltpu.with_memory_space_constraint(v, pltpu.HBM) for v in (session_head_state, adapter_down_weight, adapter_up_weight, *smalls)])
+    )(*[pltpu.with_memory_space_constraint(v, pltpu.HBM) for v in (session_head_state, *smalls)])
     msgs = out[:n_msg]
-    gated, squares, drive, b_rows, keep, place, gain, held_state, down, up = out[n_msg:]
+    gated, squares, drive, b_rows, keep, place, gain, held_state = out[n_msg:]
 
     def exchange(blocks):
         if split:
@@ -376,14 +370,10 @@
     pair = 2
     updated = pl.pallas_call(
         functools.partial(state_kernel, pair),
-        out_shape=shape(session_head_state.shape, BF16),
+        out_shape=pltpu.VMEM(session_head_state.shape, BF16),
         in_specs=[vmem(), vmem(), smem(), vmem()],
-        out_specs=pl.BlockSpec(memory_space=pltpu.HBM),
-        scratch_shapes=[
-            pltpu.VMEM(session_head_state.shape, BF16),
-            pltpu.SemaphoreType.DMA((sessions // pair,)),
-        ],
-        compiler_params=pltpu.CompilerParams(vmem_limit_bytes=12 << 20),
+        out_specs=vmem(),
+        compiler_params=pltpu.CompilerParams(vmem_limit_bytes=4 << 20),
         cost_estimate=pl.CostEstimate(
             flops=8 * session_head_state.size,
             bytes_accessed=4 * session_head_state.size,
@@ -400,7 +390,7 @@
         out_specs=[vmem()] * 2,
         compiler_params=pltpu.CompilerParams(vmem_limit_bytes=4 << 20),
         name="down",
-    )(*arrived, down, squares)
+    )(*arrived, adapter_down_weight, squares)
 
     if tensor_count in (2, 4):
         parts = [partial] + [
@@ -417,7 +407,7 @@
         out_specs=[vmem()] * (n_msg + 1),
         compiler_params=pltpu.CompilerParams(vmem_limit_bytes=4 << 20),
         name="up",
-    )(*parts, pick, up)
+    )(*parts, pick, adapter_up_weight)
     terms, inverse = out[:n_msg], out[n_msg]
     returned = exchange(terms)
 

time: 31.2 us -> 28.2 us (0.904)
  Pallas kernels: 11.2 us -> 7.66 us
  local copies, waits for them, and re-layouts: 0 us -> 2.02 us
  waiting for transfers between devices: 6.98 us -> 5.6 us
    pallas_call x1, Pallas kernels: 5.87 us -> 3.77 us  [per_device(): pl.pallas_call(functools.partial(front_kernel, dims), out_shape=[shape((m...]
    unnamed x0 -> x5, local copies, waits for them, and re-layouts: none -> 2.02 us
    ppermute x6, waiting for transfers between devices: 5.03 us -> 3.64 us  [exchange(): lax.ppermute(blocks[k], 'batch', [(i, i ^ k) for i in range(batch_count)])]
    pallas_call x1, Pallas kernels: 3.27 us -> 1.9 us  [per_device(): pl.pallas_call(functools.partial(state_kernel, pair), out_shape=pltpu.VME...]
  transfers between devices with their start and end apart: 9 -> 9, of which waited for: 4 -> 4; matrix products, arithmetic and copies ran while one was open for 0% -> 7% of each run, Pallas kernels for 13% -> 9%
where the time goes in v4:
time: 28.2 us; the launch traced here: 28.1 us
  starting transfers between devices  12.1 us (43%)
  Pallas kernels  7.66 us (27%)
  waiting for transfers between devices  5.6 us (20%)
  local copies, waits for them, and re-layouts  2.02 us (7%)
  between operations  0.7 us (2%)
    ppermute x6, starting transfers between devices, exchange(): lax.ppermute(blocks[k], 'batch', [(i, i ^ k) for i in range(batch_count)])  10.1 us
    pallas_call x1, Pallas kernels, per_device(): pl.pallas_call(functools.partial(front_kernel, dims), out_shape=[shape((m...  3.77 us
    ppermute x6, waiting for transfers between devices, exchange(): lax.ppermute(blocks[k], 'batch', [(i, i ^ k) for i in range(batch_count)])  3.64 us
    unnamed x5, local copies, waits for them, and re-layouts  2.02 us
    ppermute x3, waiting for transfers between devices, per_device(): lax.ppermute(partial, 'tensor', [(i, i ^ k) for i in range(tensor_count)])  1.96 us
    ppermute x3, starting transfers between devices, per_device(): lax.ppermute(partial, 'tensor', [(i, i ^ k) for i in range(tensor_count)])  1.96 us
    pallas_call x1, Pallas kernels, per_device(): pl.pallas_call(functools.partial(state_kernel, pair), out_shape=pltpu.VME...  1.9 us
    pallas_call x1, Pallas kernels, per_device(): pl.pallas_call(functools.partial(final_kernel, n_msg), out_shape=shape((D...  0.85 us
  transfers between devices with their start and end apart: 9, of which 4 were waited for; matrix products, arithmetic and copies ran while one was open for 7% of the time, Pallas kernels for 9%

profile of v4, /device:TPU:0, one launch (start us, length us, event | category | flops | bytes accessed | tf_op | source)
XLA Modules:
  0.0 28.1 jit_solution(1138492330548040974)
XLA Ops:
  0.6 3.8 %front.1 = (bf16[8,1152]{1,0:T(8,128)(2,1)S(1)}, bf16[8,1152]{1,0:T(8,128)(2,1)S(1)}, bf16[8,1152]{1,0:T(8,128)(2,1)S(1)}, bf16[8,1152]{1,0:T(8,128)(2,1)S(1)}, ...) custom-call(bf16[16,16,64,128]{3,2,1,0:T(8,128)(2,1)} %refs_0_.1, ...), custom_call_target="tpu_custom_call" | custom-call | flops 134217728 | bytes 4194304 | tf_op jit(solution)/shard_map/front/pallas_call | solution.py:323
  4.4 3.1 %collective-permute-start = (bf16[8,1152]{1,0:T(8,128)(2,1)S(1)}, bf16[8,1152]{1,0:T(8,128)(2,1)S(1)}, u32[]{:S(2)}, u32[]{:S(2)}) collective-permute-start(bf16[8,1152]{1,0:T(8,128)(2,1)S(1)} %get-tuple-element.32), channel_id=1, source_target_pairs={{0,4},{4,0},{8,12},{12,8},{1,5},{5,1},{9,13},{13,9},{2,6},{6,2},{1... | collective-permute-start | bytes 55304 | tf_op jit(solution)/shard_map/ppermute | solution.py:359
  7.5 2.6 %collective-permute-start.1 = (bf16[8,1152]{1,0:T(8,128)(2,1)S(1)}, bf16[8,1152]{1,0:T(8,128)(2,1)S(1)}, u32[]{:S(2)}, u32[]{:S(2)}) collective-permute-start(bf16[8,1152]{1,0:T(8,128)(2,1)S(1)} %get-tuple-element.33), channel_id=1, source_target_pairs={{0,8},{4,12},{8,0},{12,4},{1,9},{5,13},{9,1},{13,5},{2,10},{6,14},... | collective-permute-start | bytes 55304 | tf_op jit(solution)/shard_map/ppermute | solution.py:359
  10.1 0.0 collective-permute-start.2
  10.1 1.9 %state.1 = bf16[16,16,64,128]{3,2,1,0:T(8,128)(2,1)S(1)} custom-call(bf16[1024,64]{1,0:T(8,128)(2,1)S(1)} %get-tuple-element.26.left, f32[32,128]{1,0:T(8,128)S(1)} %get-tuple-element.27.b, f32[16,16]{1,0:T(8,128)S(1)} %get-tuple-element.28.keep, bf16[16,16,64,128]{3,2,1,0:T(8,128)(2,1)S(1)} %get-tuple-element.29.state), custom_call_target="tpu_custom_call" | custom-call | flops 16777216 | bytes 8388608 | tf_op jit(solution)/shard_map/state/pallas_call | solution.py:371
  12.0 0.0 collective-permute-done.refs_1_
  12.0 0.3 %collective-permute-done.1.refs_2_ = bf16[8,1152]{1,0:T(8,128)(2,1)S(1)} collective-permute-done((bf16[8,1152]{1,0:T(8,128)(2,1)S(1)}, bf16[8,1152]{1,0:T(8,128)(2,1)S(1)}, u32[]{:S(2)}, u32[]{:S(2)}) %collective-permute-start.1) | collective-permute-done | bytes 18464 | tf_op jit(solution)/shard_map/ppermute | solution.py:359
  12.3 3.3 %collective-permute-done.2.refs_3_ = bf16[8,1152]{1,0:T(8,128)(2,1)S(1)} collective-permute-done((bf16[8,1152]{1,0:T(8,128)(2,1)S(1)}, bf16[8,1152]{1,0:T(8,128)(2,1)S(1)}, u32[]{:S(2)}, u32[]{:S(2)}) %collective-permute-start.2) | collective-permute-done | bytes 18464 | tf_op jit(solution)/shard_map/ppermute | solution.py:359
  15.7 0.2 down.1
  15.9 0.1 collective-permute-start.5
  16.0 1.6 %collective-permute-start.4 = (f32[32,128]{1,0:T(8,128)S(1)}, f32[32,128]{1,0:T(8,128)S(1)}, u32[]{:S(2)}, u32[]{:S(2)}) collective-permute-start(f32[32,128]{1,0:T(8,128)S(1)} %get-tuple-element.40.refs_0_), channel_id=1, source_target_pairs={{0,2},{1,3},{2,0},{3,1},{4,6},{5,7},{6,4},{7,5},{8,10},{9,11},{10,... | collective-permute-start | bytes 49160 | tf_op jit(solution)/shard_map/ppermute | solution.py:397
  17.5 0.3 %collective-permute-start.3 = (f32[32,128]{1,0:T(8,128)S(1)}, f32[32,128]{1,0:T(8,128)S(1)}, u32[]{:S(2)}, u32[]{:S(2)}) collective-permute-start(f32[32,128]{1,0:T(8,128)S(1)} %get-tuple-element.40.refs_0_), channel_id=1, source_target_pairs={{0,1},{1,0},{2,3},{3,2},{4,5},{5,4},{6,7},{7,6},{8,9},{9,8},{10,11... | collective-permute-start | bytes 49160 | tf_op jit(solution)/shard_map/ppermute | solution.py:397
  17.8 1.4 %collective-permute-done.5.refs_3_ = f32[32,128]{1,0:T(8,128)S(1)} collective-permute-done((f32[32,128]{1,0:T(8,128)S(1)}, f32[32,128]{1,0:T(8,128)S(1)}, u32[]{:S(2)}, u32[]{:S(2)}) %collective-permute-start.5) | collective-permute-done | bytes 16416 | tf_op jit(solution)/shard_map/ppermute | solution.py:397
  19.3 0.5 %collective-permute-done.4.refs_2_ = f32[32,128]{1,0:T(8,128)S(1)} collective-permute-done((f32[32,128]{1,0:T(8,128)S(1)}, f32[32,128]{1,0:T(8,128)S(1)}, u32[]{:S(2)}, u32[]{:S(2)}) %collective-permute-start.4) | collective-permute-done | bytes 16416 | tf_op jit(solution)/shard_map/ppermute | solution.py:397
  19.8 0.0 collective-permute-done.3.refs_1_
  19.8 0.2 up.1
  20.0 0.1 collective-permute-start.6
  20.1 0.8 %collective-permute-start.7 = (f32[8,1024]{1,0:T(8,128)S(1)}, f32[8,1024]{1,0:T(8,128)S(1)}, u32[]{:S(2)}, u32[]{:S(2)}) collective-permute-start(f32[8,1024]{1,0:T(8,128)S(1)} %get-tuple-element.46), channel_id=1, source_target_pairs={{0,8},{4,12},{8,0},{12,4},{1,9},{5,13},{9,1},{13,5},{2,10},{6,14},... | collective-permute-start | bytes 98312 | tf_op jit(solution)/shard_map/ppermute | solution.py:359
  20.9 3.6 %collective-permute-start.8 = (f32[8,1024]{1,0:T(8,128)S(1)}, f32[8,1024]{1,0:T(8,128)S(1)}, u32[]{:S(2)}, u32[]{:S(2)}) collective-permute-start(f32[8,1024]{1,0:T(8,128)S(1)} %get-tuple-element.47), channel_id=1, source_target_pairs={{0,12},{4,8},{8,4},{12,0},{1,13},{5,9},{9,5},{13,1},{2,14},{6,10},... | collective-permute-start | bytes 98312 | tf_op jit(solution)/shard_map/ppermute | solution.py:359
  24.5 2.0 %copy.17 = bf16[16,16,64,128]{3,2,1,0:T(8,128)(2,1)} copy(bf16[16,16,64,128]{3,2,1,0:T(8,128)(2,1)S(1)} %state.1) | data formatting | bytes 8388608
  26.5 0.7 %norm.1 = bf16[2,16,1024]{2,1,0:T(8,128)(2,1)} custom-call(f32[32,1024]{1,0:T(8,128)S(1)} %get-tuple-element.30.gated, f32[32,128]{1,0:T(8,128)S(1)} %get-tuple-element.42.inverse.refs_5_, f32[1,1024]{1,0:T(1,128)S(1)} %get-tuple-element.43.gain), custom_call_target="tpu_custom_call" | custom-call | tf_op jit(solution)/shard_map/norm/pallas_call | solution.py:414
  27.2 0.0 collective-permute-done.6.refs_1_
  27.2 0.0 collective-permute-done.8.refs_3_
  27.2 0.9 %final.1 = f32[2,16,1024]{2,1,0:T(8,128)} custom-call(f32[8,1024]{1,0:T(8,128)S(1)} %get-tuple-element.44.refs_0_, f32[8,1024]{1,0:T(8,128)S(1)} %collective-permute-done.6.refs_1_, f32[8,1024]{1,0:T(8,128)S(1)} %collective-permute-done.7.refs_2_, f32[8,1024]{1,0:T(8,128)S(1)} %collective-permute-done.8.refs_3_, f32[32,32]{1,0:T(8,128)S(1)} %get-tuple-element.48.refs_4_, ...), custom_call_target="tpu_custom_call" | custom-call | tf_op jit(solution)/shard_map/final/pallas_call | solution.py:423
  (5 shorter events, 0.0 us)
Async XLA Ops:
  4.4 7.6 %collective-permute-start = (bf16[8,1152]{1,0:T(8,128)(2,1)S(1)}, bf16[8,1152]{1,0:T(8,128)(2,1)S(1)}, u32[]{:S(2)}, u32[]{:S(2)}) collective-permute-start(bf16[8,1152]{1,0:T(8,128)(2,1)S(1)} %get-tuple-element.32), channel_id=1, source_target_pairs={{0,4},{4,0},{8,12},{12,8},{1,5},{5,1},{9,13},{13,9},{2,6},{6,2},{1... | collective-permute-start | bytes 55304 | tf_op jit(solution)/shard_map/ppermute | solution.py:359
  7.5 4.8 %collective-permute-start.1 = (bf16[8,1152]{1,0:T(8,128)(2,1)S(1)}, bf16[8,1152]{1,0:T(8,128)(2,1)S(1)}, u32[]{:S(2)}, u32[]{:S(2)}) collective-permute-start(bf16[8,1152]{1,0:T(8,128)(2,1)S(1)} %get-tuple-element.33), channel_id=1, source_target_pairs={{0,8},{4,12},{8,0},{12,4},{1,9},{5,13},{9,1},{13,5},{2,10},{6,14},... | collective-permute-start | bytes 55304 | tf_op jit(solution)/shard_map/ppermute | solution.py:359
  10.1 5.6 %collective-permute-start.2 = (bf16[8,1152]{1,0:T(8,128)(2,1)S(1)}, bf16[8,1152]{1,0:T(8,128)(2,1)S(1)}, u32[]{:S(2)}, u32[]{:S(2)}) collective-permute-start(bf16[8,1152]{1,0:T(8,128)(2,1)S(1)} %get-tuple-element.34), channel_id=1, source_target_pairs={{0,12},{4,8},{8,4},{12,0},{1,13},{5,9},{9,5},{13,1},{2,14},{6,10},... | collective-permute-start | bytes 55304 | tf_op jit(solution)/shard_map/ppermute | solution.py:359
  10.1 5.6 %copy-start = (bf16[2,64,1024]{2,1,0:T(8,128)(2,1)S(1)}, bf16[2,64,1024]{2,1,0:T(8,128)(2,1)}, u32[]{:S(2)}) copy-start(bf16[2,64,1024]{2,1,0:T(8,128)(2,1)} %refs_4_.3) | copy-start | bytes 786436
  10.1 9.7 %copy-start.1 = (bf16[2,64,1024]{2,1,0:T(8,128)(2,1)S(1)}, bf16[2,64,1024]{2,1,0:T(8,128)(2,1)}, u32[]{:S(2)}) copy-start(bf16[2,64,1024]{2,1,0:T(8,128)(2,1)} %refs_5_.3) | copy-start | bytes 786436
  15.9 3.4 %collective-permute-start.5 = (f32[32,128]{1,0:T(8,128)S(1)}, f32[32,128]{1,0:T(8,128)S(1)}, u32[]{:S(2)}, u32[]{:S(2)}) collective-permute-start(f32[32,128]{1,0:T(8,128)S(1)} %get-tuple-element.40.refs_0_), channel_id=1, source_target_pairs={{0,3},{1,2},{2,1},{3,0},{4,7},{5,6},{6,5},{7,4},{8,11},{9,10},{10,... | collective-permute-start | bytes 49160 | tf_op jit(solution)/shard_map/ppermute | solution.py:397
  16.0 3.8 %collective-permute-start.4 = (f32[32,128]{1,0:T(8,128)S(1)}, f32[32,128]{1,0:T(8,128)S(1)}, u32[]{:S(2)}, u32[]{:S(2)}) collective-permute-start(f32[32,128]{1,0:T(8,128)S(1)} %get-tuple-element.40.refs_0_), channel_id=1, source_target_pairs={{0,2},{1,3},{2,0},{3,1},{4,6},{5,7},{6,4},{7,5},{8,10},{9,11},{10,... | collective-permute-start | bytes 49160 | tf_op jit(solution)/shard_map/ppermute | solution.py:397
  17.5 2.3 %collective-permute-start.3 = (f32[32,128]{1,0:T(8,128)S(1)}, f32[32,128]{1,0:T(8,128)S(1)}, u32[]{:S(2)}, u32[]{:S(2)}) collective-permute-start(f32[32,128]{1,0:T(8,128)S(1)} %get-tuple-element.40.refs_0_), channel_id=1, source_target_pairs={{0,1},{1,0},{2,3},{3,2},{4,5},{5,4},{6,7},{7,6},{8,9},{9,8},{10,11... | collective-permute-start | bytes 49160 | tf_op jit(solution)/shard_map/ppermute | solution.py:397
  20.0 7.2 %collective-permute-start.6 = (f32[8,1024]{1,0:T(8,128)S(1)}, f32[8,1024]{1,0:T(8,128)S(1)}, u32[]{:S(2)}, u32[]{:S(2)}) collective-permute-start(f32[8,1024]{1,0:T(8,128)S(1)} %get-tuple-element.45), channel_id=1, source_target_pairs={{0,4},{4,0},{8,12},{12,8},{1,5},{5,1},{9,13},{13,9},{2,6},{6,2},{1... | collective-permute-start | bytes 98312 | tf_op jit(solution)/shard_map/ppermute | solution.py:359
  20.1 7.1 %collective-permute-start.7 = (f32[8,1024]{1,0:T(8,128)S(1)}, f32[8,1024]{1,0:T(8,128)S(1)}, u32[]{:S(2)}, u32[]{:S(2)}) collective-permute-start(f32[8,1024]{1,0:T(8,128)S(1)} %get-tuple-element.46), channel_id=1, source_target_pairs={{0,8},{4,12},{8,0},{12,4},{1,9},{5,13},{9,1},{13,5},{2,10},{6,14},... | collective-permute-start | bytes 98312 | tf_op jit(solution)/shard_map/ppermute | solution.py:359
  20.9 6.3 %collective-permute-start.8 = (f32[8,1024]{1,0:T(8,128)S(1)}, f32[8,1024]{1,0:T(8,128)S(1)}, u32[]{:S(2)}, u32[]{:S(2)}) collective-permute-start(f32[8,1024]{1,0:T(8,128)S(1)} %get-tuple-element.47), channel_id=1, source_target_pairs={{0,12},{4,8},{8,4},{12,0},{1,13},{5,9},{9,5},{13,1},{2,14},{6,10},... | collective-permute-start | bytes 98312 | tf_op jit(solution)/shard_map/ppermute | solution.py:359

commit v5 on v4

--- a/solution.py
+++ b/solution.py
@@ -13,6 +13,7 @@
 DECODE_STEPS = 2
 RANK = 64
 LANES = 128
+PAIR = 2
 
 adapter_scale = 2.0
 norm_eps = 1e-05
@@ -35,7 +36,7 @@
 
 
 def front_kernel(dims, *refs):
-    sessions, heads, batch_count, capacity, adapters_held, chunks, split = dims
+    sessions, heads, batch_count, capacity, adapters_held, chunks, depth, split = dims
     n_msg = batch_count if split else 1
     inputs, refs = refs[:12], refs[12:]
     msgs, refs = refs[:n_msg], refs[n_msg:]
@@ -57,8 +58,9 @@
     for i in range(chunks):
         window = pl.ds(i * part, part)
         copy = pltpu.make_async_copy(state.at[window], held.at[window], sems.at[i])
+        copies.append(copy)
+    for copy in copies[:depth]:
         copy.start()
-        copies.append(copy)
     adapter, slot_of, x, z, b, c, raw, bias, rate, skip, gain_rows = local
     me = lax.axis_index("batch")
     group = lax.axis_index("tensor") * heads // (HEAD_COUNT // GROUPS)
@@ -77,13 +79,15 @@
     )
     def read(i):
         copies[i].wait()
+        if i + depth < chunks:
+            copies[i + depth].start()
         lanes = slice(i * part * LANES, (i + 1) * part * LANES)
         block = jnp.concatenate(
             [held[i * part + s].reshape(channels, LANES) for s in range(part)], axis=1
         )
         return lax.dot_general(c_blocks[:, lanes], block, NT, preferred_element_type=F32)
 
-    reads = read(0)
+    reads = read(0) + read(1)
     b1, b2 = b_rows[:sessions], b_rows[sessions:]
     c1, c2 = c_rows[:sessions], c_rows[sessions:]
     bc11 = jnp.sum(b1 * c1, axis=1, keepdims=True)
@@ -112,7 +116,7 @@
         ],
         axis=0,
     )
-    reads = reads + read(1)
+    reads = reads + read(2) + read(3)
     gain = jnp.concatenate(
         [gain_rows[i : i + 1].astype(F32) for i in range(channels // LANES)], axis=1
     )
@@ -133,7 +137,7 @@
     gates = gates / (1.0 + jnp.exp(-gates))
     base = jnp.concatenate([base1, base2], axis=0)
     scale = jnp.concatenate([wide[0], wide[2]], axis=0)
-    reads = reads + read(2)
+    reads = reads + read(4) + read(5)
     high = drive.astype(BF16)
     low = (drive - high.astype(F32)).astype(BF16)
     drive_ref[...] = jnp.concatenate([high, low], axis=0).T
@@ -161,7 +165,7 @@
     place_ref[...] = place
     place_bf = place.astype(BF16)
 
-    reads = reads + read(3)
+    reads = reads + read(6) + read(7)
     gated = (scale * reads + base) * gates
     gated_ref[...] = gated
     squares = jnp.zeros((rows, LANES), F32)
@@ -179,31 +183,49 @@
     square_ref[...] = squares[:, :RANK] + squares[:, RANK:]
 
 
-def state_kernel(pair, left, b, keep, state, out):
-    sessions, heads = state.shape[:2]
+def advance_state(first, count, left, b, keep, state, made):
+    heads = state.shape[1]
     rows = b.shape[0]
-    row_session = iota((rows, LANES), 0) % sessions
+    row_session = iota((rows, LANES), 0) % (rows // DECODE_STEPS)
     b_rows = b[...]
-    for start in range(0, sessions, pair):
+    kept_all = keep[...]
+    for start in range(0, count, PAIR):
         right = jnp.concatenate(
-            [jnp.where(row_session == start + q, b_rows, 0.0) for q in range(pair)], axis=1
+            [
+                jnp.where(row_session == first + start + q, b_rows, 0.0)
+                for q in range(PAIR)
+            ],
+            axis=1,
         )
         right = jnp.concatenate([right, right], axis=0).astype(BF16)
         for h in range(heads):
             piece = slice(h * HEAD_CHANNELS, (h + 1) * HEAD_CHANNELS)
             added = jnp.dot(left[piece], right, preferred_element_type=F32)
-            for q in range(pair):
-                kept = state[start + q, h].astype(F32) * keep[start + q, h]
-                out[start + q, h] = (kept + added[:, q * LANES : (q + 1) * LANES]).astype(BF16)
-
-
-def norm_kernel(gated, inverse, gain, out):
-    normed = gated[...] * inverse[:, :1] * gain[...]
-    out[...] = normed.astype(BF16).reshape(out.shape)
-
-
-def down_kernel(n_msg, *refs):
-    msgs = refs[:n_msg]
+            for q in range(PAIR):
+                s = first + start + q
+                kept = state[s, h].astype(F32) * kept_all[s : s + 1, h : h + 1]
+                new = kept + added[:, q * LANES : (q + 1) * LANES]
+                made[start + q, h] = new.astype(BF16)
+
+
+def state_kernel(first, left, b, keep, state, made):
+    advance_state(first, made.shape[0], left, b, keep, state, made)
+
+
+def close_kernel(gated, inverse, gain, made, normed, out, rows, sems):
+    store_state = pltpu.make_async_copy(made, out, sems.at[0])
+    store_state.start()
+    scaled = gated[...] * inverse[:, :1] * gain[...]
+    rows[...] = scaled.astype(BF16).reshape(rows.shape)
+    store_rows = pltpu.make_async_copy(rows, normed, sems.at[1])
+    store_rows.start()
+    store_state.wait()
+    store_rows.wait()
+
+
+def down_kernel(order, *refs):
+    n_msg = len(order)
+    msgs = [refs[order.index(k)] for k in range(n_msg)]
     down, squares, out, pick_ref = refs[n_msg:]
     held, rank, channels = down.shape
     rows = jnp.concatenate([m[...].astype(F32) for m in msgs], axis=0)
@@ -251,8 +273,9 @@
     inverse[...] = jnp.broadcast_to(factor, inverse.shape)
 
 
-def final_kernel(n_msg, *refs):
-    msgs = refs[:n_msg]
+def final_kernel(order, *refs):
+    n_msg = len(order)
+    msgs = [refs[order.index(k)] for k in range(n_msg)]
     place, inverse, out = refs[n_msg:]
     terms = jnp.concatenate([m[...] for m in msgs], axis=0)
     one_hot = place[...].astype(BF16)
@@ -304,9 +327,10 @@
     per_owner = DECODE_STEPS * capacity
     targets = batch_count * per_owner
     n_msg = batch_count if split else 1
-    chunks = 4
+    chunks = 8
+    depth = 5
     msg_rows = targets // n_msg
-    dims = (sessions, heads, batch_count, capacity, adapters_held, chunks, split)
+    dims = (sessions, heads, batch_count, capacity, adapters_held, chunks, depth, split)
     smalls = (
         adapter_per_session,
         adapter_storage_slot,
@@ -351,7 +375,7 @@
         name="front",
     )(*[pltpu.with_memory_space_constraint(v, pltpu.HBM) for v in (session_head_state, *smalls)])
     msgs = out[:n_msg]
-    gated, squares, drive, b_rows, keep, place, gain, held_state = out[n_msg:]
+    gated, squares, left, b_rows, keep, place, gain, held_state = out[n_msg:]
 
     def exchange(blocks):
         if split:
@@ -365,26 +389,32 @@
         block = lax.all_to_all(block, "batch", split_axis=0, concat_axis=0, tiled=True)
         return [block.reshape(targets, -1)]
 
+    order = [0] + list(range(n_msg - 1, 0, -1))
     arrived = exchange(msgs)
-
-    pair = 2
-    updated = pl.pallas_call(
-        functools.partial(state_kernel, pair),
-        out_shape=pltpu.VMEM(session_head_state.shape, BF16),
-        in_specs=[vmem(), vmem(), smem(), vmem()],
+    arrived = [arrived[k] for k in order]
+
+    in_hbm = pl.BlockSpec(memory_space=pltpu.HBM)
+    one_state = session_head_state.shape[1:]
+    middle = sessions
+    small = pltpu.CompilerParams(vmem_limit_bytes=4 << 20)
+
+    def cost(count):
+        elements = count * heads * HEAD_CHANNELS * state_size
+        return pl.CostEstimate(flops=8 * elements, bytes_accessed=4 * elements, transcendentals=0)
+
+    made = pl.pallas_call(
+        functools.partial(state_kernel, 0),
+        out_shape=pltpu.VMEM((middle,) + one_state, BF16),
+        in_specs=[vmem()] * 4,
         out_specs=vmem(),
-        compiler_params=pltpu.CompilerParams(vmem_limit_bytes=4 << 20),
-        cost_estimate=pl.CostEstimate(
-            flops=8 * session_head_state.size,
-            bytes_accessed=4 * session_head_state.size,
-            transcendentals=0,
-        ),
+        compiler_params=small,
+        cost_estimate=cost(middle),
         name="state",
-    )(drive, b_rows, keep, held_state)
-    arrived = lax.optimization_barrier((arrived, updated))[0]
+    )(left, b_rows, keep, held_state)
+    arrived, made = lax.optimization_barrier((arrived, made))
 
     partial, pick = pl.pallas_call(
-        functools.partial(down_kernel, n_msg),
+        functools.partial(down_kernel, order),
         out_shape=[shape((targets, 2 * RANK), F32), shape((targets, LANES), F32)],
         in_specs=[vmem()] * (n_msg + 2),
         out_specs=[vmem()] * 2,
@@ -410,18 +440,27 @@
     )(*parts, pick, adapter_up_weight)
     terms, inverse = out[:n_msg], out[n_msg]
     returned = exchange(terms)
-
-    normed = pl.pallas_call(
-        norm_kernel,
-        out_shape=shape((DECODE_STEPS, sessions, channels), BF16),
-        in_specs=[vmem()] * 3,
-        out_specs=vmem(),
-        compiler_params=pltpu.CompilerParams(vmem_limit_bytes=4 << 20),
-        name="norm",
-    )(gated, inverse, gain)
+    returned = [returned[k] for k in order]
+
+    normed, updated = pl.pallas_call(
+        close_kernel,
+        out_shape=[
+            pltpu.HBM((DECODE_STEPS, sessions, channels), BF16),
+            pltpu.HBM(session_head_state.shape, BF16),
+        ],
+        in_specs=[vmem()] * 4,
+        out_specs=[in_hbm, in_hbm],
+        scratch_shapes=[
+            pltpu.VMEM((DECODE_STEPS, sessions, channels), BF16),
+            pltpu.SemaphoreType.DMA((2,)),
+        ],
+        compiler_params=small,
+        cost_estimate=cost(sessions),
+        name="close",
+    )(gated, inverse, gain, made)
 
     delta = pl.pallas_call(
-        functools.partial(final_kernel, n_msg),
+        functools.partial(final_kernel, order),
         out_shape=shape((DECODE_STEPS, sessions, channels), F32),
         in_specs=[vmem()] * (n_msg + 2),
         out_specs=vmem(),

time: 28.2 us -> 26.3 us (0.933)
  local copies, waits for them, and re-layouts: 2.02 us -> 0.01 us
  waiting for transfers between devices: 5.6 us -> 5.13 us
  Pallas kernels: 7.66 us -> 8.1 us
    unnamed x5 -> x4, local copies, waits for them, and re-layouts: 2.02 us -> 0.01 us
    pallas_call x4, Pallas kernels: 3.67 us -> 4.34 us  [the longest x1 2.03 us: per_device(): pl.pallas_call(close_kernel, out_shape=[pltpu.HBM((DECODE_STEPS, sessions...]
    ppermute x6, waiting for transfers between devices: 3.64 us -> 3.17 us  [exchange(): lax.ppermute(blocks[k], 'batch', [(i, i ^ k) for i in range(batch_count)])]
  transfers between devices with their start and end apart: 9 -> 9, of which waited for: 4 -> 5; matrix products, arithmetic and copies ran while one was open for 7% -> 0% of each run, Pallas kernels for 9% -> 13%
where the time goes in v5:
time: 26.3 us; the launch traced here: 26.1 us
  starting transfers between devices  12.2 us (46%)
  Pallas kernels  8.1 us (31%)
  waiting for transfers between devices  5.13 us (20%)
  between operations  0.7 us (3%)
    ppermute x6, starting transfers between devices, exchange(): lax.ppermute(blocks[k], 'batch', [(i, i ^ k) for i in range(batch_count)])  10.2 us
    pallas_call x1, Pallas kernels, per_device(): pl.pallas_call(functools.partial(front_kernel, dims), out_shape=[shape((m...  3.54 us
    ppermute x6, waiting for transfers between devices, exchange(): lax.ppermute(blocks[k], 'batch', [(i, i ^ k) for i in range(batch_count)])  3.17 us
    pallas_call x1, Pallas kernels, per_device(): pl.pallas_call(close_kernel, out_shape=[pltpu.HBM((DECODE_STEPS, sessions...  2.03 us
    ppermute x3, waiting for transfers between devices, per_device(): lax.ppermute(partial, 'tensor', [(i, i ^ k) for i in range(tensor_count)])  1.96 us
    ppermute x3, starting transfers between devices, per_device(): lax.ppermute(partial, 'tensor', [(i, i ^ k) for i in range(tensor_count)])  1.96 us
    pallas_call x1, Pallas kernels, per_device(): pl.pallas_call(functools.partial(state_kernel, 0), out_shape=pltpu.VMEM((...  1.25 us
    pallas_call x1, Pallas kernels, per_device(): pl.pallas_call(functools.partial(final_kernel, order), out_shape=shape((D...  0.86 us
  transfers between devices with their start and end apart: 9, of which 5 were waited for; matrix products, arithmetic and copies ran while one was open for 0% of the time, Pallas kernels for 13%

profile of v5, /device:TPU:0, one launch (start us, length us, event | category | flops | bytes accessed | tf_op | source)
XLA Modules:
  0.0 26.1 jit_solution(16374396525983659758)
XLA Ops:
  0.6 3.5 %front.1 = (bf16[8,1152]{1,0:T(8,128)(2,1)S(1)}, bf16[8,1152]{1,0:T(8,128)(2,1)S(1)}, bf16[8,1152]{1,0:T(8,128)(2,1)S(1)}, bf16[8,1152]{1,0:T(8,128)(2,1)S(1)}, ...) custom-call(bf16[16,16,64,128]{3,2,1,0:T(8,128)(2,1)} %refs_0_.1, ...), custom_call_target="tpu_custom_call" | custom-call | flops 134217728 | bytes 4194304 | tf_op jit(solution)/shard_map/front/pallas_call | solution.py:347
  4.2 5.1 %collective-permute-start = (bf16[8,1152]{1,0:T(8,128)(2,1)S(1)}, bf16[8,1152]{1,0:T(8,128)(2,1)S(1)}, u32[]{:S(2)}, u32[]{:S(2)}) collective-permute-start(bf16[8,1152]{1,0:T(8,128)(2,1)S(1)} %get-tuple-element.31), channel_id=1, source_target_pairs={{0,12},{4,8},{8,4},{12,0},{1,13},{5,9},{9,5},{13,1},{2,14},{6,10},... | collective-permute-start | bytes 55304 | tf_op jit(solution)/shard_map/ppermute | solution.py:383
  9.3 0.0 collective-permute-start.1
  9.3 0.6 %collective-permute-start.2 = (bf16[8,1152]{1,0:T(8,128)(2,1)S(1)}, bf16[8,1152]{1,0:T(8,128)(2,1)S(1)}, u32[]{:S(2)}, u32[]{:S(2)}) collective-permute-start(bf16[8,1152]{1,0:T(8,128)(2,1)S(1)} %get-tuple-element.33), channel_id=1, source_target_pairs={{0,4},{4,0},{8,12},{12,8},{1,5},{5,1},{9,13},{13,9},{2,6},{6,2},{1... | collective-permute-start | bytes 55304 | tf_op jit(solution)/shard_map/ppermute | solution.py:383
  9.9 1.2 %state.1.made = bf16[16,16,64,128]{3,2,1,0:T(8,128)(2,1)S(1)} custom-call(bf16[1024,64]{1,0:T(8,128)(2,1)S(1)} %get-tuple-element.34.left, f32[32,128]{1,0:T(8,128)S(1)} %get-tuple-element.35.b, f32[16,16]{1,0:T(8,128)S(1)} %get-tuple-element.36.keep, bf16[16,16,64,128]{3,2,1,0:T(8,128)(2,1)S(1)} %get-tuple-element.37.state), custom_call_target="tpu_custom_call" | custom-call | flops 16777216 | bytes 8388608 | tf_op jit(solution)/shard_map/state/pallas_call | solution.py:405
  11.2 0.0 collective-permute-done.refs_1_
  11.2 2.7 %collective-permute-done.1.refs_2_ = bf16[8,1152]{1,0:T(8,128)(2,1)S(1)} collective-permute-done((bf16[8,1152]{1,0:T(8,128)(2,1)S(1)}, bf16[8,1152]{1,0:T(8,128)(2,1)S(1)}, u32[]{:S(2)}, u32[]{:S(2)}) %collective-permute-start.1) | collective-permute-done | bytes 18464 | tf_op jit(solution)/shard_map/ppermute | solution.py:383
  14.0 0.0 collective-permute-done.2.refs_3_
  14.0 0.2 down.1
  14.2 0.1 collective-permute-start.5
  14.3 1.6 %collective-permute-start.4 = (f32[32,128]{1,0:T(8,128)S(1)}, f32[32,128]{1,0:T(8,128)S(1)}, u32[]{:S(2)}, u32[]{:S(2)}) collective-permute-start(f32[32,128]{1,0:T(8,128)S(1)} %get-tuple-element.43.refs_0_), channel_id=1, source_target_pairs={{0,2},{1,3},{2,0},{3,1},{4,6},{5,7},{6,4},{7,5},{8,10},{9,11},{10,... | collective-permute-start | bytes 49160 | tf_op jit(solution)/shard_map/ppermute | solution.py:427
  15.8 0.3 %collective-permute-start.3 = (f32[32,128]{1,0:T(8,128)S(1)}, f32[32,128]{1,0:T(8,128)S(1)}, u32[]{:S(2)}, u32[]{:S(2)}) collective-permute-start(f32[32,128]{1,0:T(8,128)S(1)} %get-tuple-element.43.refs_0_), channel_id=1, source_target_pairs={{0,1},{1,0},{2,3},{3,2},{4,5},{5,4},{6,7},{7,6},{8,9},{9,8},{10,11... | collective-permute-start | bytes 49160 | tf_op jit(solution)/shard_map/ppermute | solution.py:427
  16.1 1.4 %collective-permute-done.5.refs_3_ = f32[32,128]{1,0:T(8,128)S(1)} collective-permute-done((f32[32,128]{1,0:T(8,128)S(1)}, f32[32,128]{1,0:T(8,128)S(1)}, u32[]{:S(2)}, u32[]{:S(2)}) %collective-permute-start.5) | collective-permute-done | bytes 16416 | tf_op jit(solution)/shard_map/ppermute | solution.py:427
  17.6 0.5 %collective-permute-done.4.refs_2_ = f32[32,128]{1,0:T(8,128)S(1)} collective-permute-done((f32[32,128]{1,0:T(8,128)S(1)}, f32[32,128]{1,0:T(8,128)S(1)}, u32[]{:S(2)}, u32[]{:S(2)}) %collective-permute-start.4) | collective-permute-done | bytes 16416 | tf_op jit(solution)/shard_map/ppermute | solution.py:427
  18.1 0.0 collective-permute-done.3.refs_1_
  18.1 0.2 up.1
  18.3 1.5 %collective-permute-start.6 = (f32[8,1024]{1,0:T(8,128)S(1)}, f32[8,1024]{1,0:T(8,128)S(1)}, u32[]{:S(2)}, u32[]{:S(2)}) collective-permute-start(f32[8,1024]{1,0:T(8,128)S(1)} %get-tuple-element.51), channel_id=1, source_target_pairs={{0,12},{4,8},{8,4},{12,0},{1,13},{5,9},{9,5},{13,1},{2,14},{6,10},... | collective-permute-start | bytes 98312 | tf_op jit(solution)/shard_map/ppermute | solution.py:383
  19.9 0.6 %collective-permute-start.7 = (f32[8,1024]{1,0:T(8,128)S(1)}, f32[8,1024]{1,0:T(8,128)S(1)}, u32[]{:S(2)}, u32[]{:S(2)}) collective-permute-start(f32[8,1024]{1,0:T(8,128)S(1)} %get-tuple-element.52), channel_id=1, source_target_pairs={{0,8},{4,12},{8,0},{12,4},{1,9},{5,13},{9,1},{13,5},{2,10},{6,14},... | collective-permute-start | bytes 98312 | tf_op jit(solution)/shard_map/ppermute | solution.py:383
  20.5 2.3 %collective-permute-start.8 = (f32[8,1024]{1,0:T(8,128)S(1)}, f32[8,1024]{1,0:T(8,128)S(1)}, u32[]{:S(2)}, u32[]{:S(2)}) collective-permute-start(f32[8,1024]{1,0:T(8,128)S(1)} %get-tuple-element.53), channel_id=1, source_target_pairs={{0,4},{4,0},{8,12},{12,8},{1,5},{5,1},{9,13},{13,9},{2,6},{6,2},{1... | collective-permute-start | bytes 98312 | tf_op jit(solution)/shard_map/ppermute | solution.py:383
  22.8 2.0 %close.1 = (bf16[2,16,1024]{2,1,0:T(8,128)(2,1)}, bf16[16,16,64,128]{3,2,1,0:T(8,128)(2,1)}) custom-call(f32[32,1024]{1,0:T(8,128)S(1)} %get-tuple-element.29.gated, f32[32,128]{1,0:T(8,128)S(1)} %get-tuple-element.45.inverse.refs_5_, f32[1,1024]{1,0:T(1,128)S(1)} %get-tuple-element.46.gain, bf16[16,16,64,128]{3,2,1,0:T(8,128)(2,1)S(1)} %state.1.made), custom_call_target="tpu_custom_call" | custom-call | flops 16777216 | bytes 8388608 | tf_op jit(solution)/shard_map/close/pallas_call | solution.py:445
  24.8 0.0 collective-permute-done.6.refs_1_
  24.8 0.1 collective-permute-done.7.refs_2_
  24.9 0.3 %collective-permute-done.8.refs_3_ = f32[8,1024]{1,0:T(8,128)S(1)} collective-permute-done((f32[8,1024]{1,0:T(8,128)S(1)}, f32[8,1024]{1,0:T(8,128)S(1)}, u32[]{:S(2)}, u32[]{:S(2)}) %collective-permute-start.8) | collective-permute-done | bytes 32800 | tf_op jit(solution)/shard_map/ppermute | solution.py:383
  25.3 0.9 %final.1 = f32[2,16,1024]{2,1,0:T(8,128)} custom-call(f32[8,1024]{1,0:T(8,128)S(1)} %get-tuple-element.50.refs_0_, f32[8,1024]{1,0:T(8,128)S(1)} %collective-permute-done.6.refs_1_, f32[8,1024]{1,0:T(8,128)S(1)} %collective-permute-done.7.refs_2_, f32[8,1024]{1,0:T(8,128)S(1)} %collective-permute-done.8.refs_3_, f32[32,32]{1,0:T(8,128)S(1)} %get-tuple-element.54.refs_4_, ...), custom_call_target="tpu_custom_call" | custom-call | tf_op jit(solution)/shard_map/final/pallas_call | solution.py:462
  (4 shorter events, 0.0 us)
Async XLA Ops:
  4.2 7.0 %collective-permute-start = (bf16[8,1152]{1,0:T(8,128)(2,1)S(1)}, bf16[8,1152]{1,0:T(8,128)(2,1)S(1)}, u32[]{:S(2)}, u32[]{:S(2)}) collective-permute-start(bf16[8,1152]{1,0:T(8,128)(2,1)S(1)} %get-tuple-element.31), channel_id=1, source_target_pairs={{0,12},{4,8},{8,4},{12,0},{1,13},{5,9},{9,5},{13,1},{2,14},{6,10},... | collective-permute-start | bytes 55304 | tf_op jit(solution)/shard_map/ppermute | solution.py:383
  9.3 4.7 %collective-permute-start.1 = (bf16[8,1152]{1,0:T(8,128)(2,1)S(1)}, bf16[8,1152]{1,0:T(8,128)(2,1)S(1)}, u32[]{:S(2)}, u32[]{:S(2)}) collective-permute-start(bf16[8,1152]{1,0:T(8,128)(2,1)S(1)} %get-tuple-element.32), channel_id=1, source_target_pairs={{0,8},{4,12},{8,0},{12,4},{1,9},{5,13},{9,1},{13,5},{2,10},{6,14},... | collective-permute-start | bytes 55304 | tf_op jit(solution)/shard_map/ppermute | solution.py:383
  9.3 4.7 %collective-permute-start.2 = (bf16[8,1152]{1,0:T(8,128)(2,1)S(1)}, bf16[8,1152]{1,0:T(8,128)(2,1)S(1)}, u32[]{:S(2)}, u32[]{:S(2)}) collective-permute-start(bf16[8,1152]{1,0:T(8,128)(2,1)S(1)} %get-tuple-element.33), channel_id=1, source_target_pairs={{0,4},{4,0},{8,12},{12,8},{1,5},{5,1},{9,13},{13,9},{2,6},{6,2},{1... | collective-permute-start | bytes 55304 | tf_op jit(solution)/shard_map/ppermute | solution.py:383
  9.9 4.0 %copy-start = (bf16[2,64,1024]{2,1,0:T(8,128)(2,1)S(1)}, bf16[2,64,1024]{2,1,0:T(8,128)(2,1)}, u32[]{:S(2)}) copy-start(bf16[2,64,1024]{2,1,0:T(8,128)(2,1)} %refs_4_.3) | copy-start | bytes 786436
  9.9 8.2 %copy-start.1 = (bf16[2,64,1024]{2,1,0:T(8,128)(2,1)S(1)}, bf16[2,64,1024]{2,1,0:T(8,128)(2,1)}, u32[]{:S(2)}) copy-start(bf16[2,64,1024]{2,1,0:T(8,128)(2,1)} %refs_5_.3) | copy-start | bytes 786436
  14.2 3.4 %collective-permute-start.5 = (f32[32,128]{1,0:T(8,128)S(1)}, f32[32,128]{1,0:T(8,128)S(1)}, u32[]{:S(2)}, u32[]{:S(2)}) collective-permute-start(f32[32,128]{1,0:T(8,128)S(1)} %get-tuple-element.43.refs_0_), channel_id=1, source_target_pairs={{0,3},{1,2},{2,1},{3,0},{4,7},{5,6},{6,5},{7,4},{8,11},{9,10},{10,... | collective-permute-start | bytes 49160 | tf_op jit(solution)/shard_map/ppermute | solution.py:427
  14.3 3.8 %collective-permute-start.4 = (f32[32,128]{1,0:T(8,128)S(1)}, f32[32,128]{1,0:T(8,128)S(1)}, u32[]{:S(2)}, u32[]{:S(2)}) collective-permute-start(f32[32,128]{1,0:T(8,128)S(1)} %get-tuple-element.43.refs_0_), channel_id=1, source_target_pairs={{0,2},{1,3},{2,0},{3,1},{4,6},{5,7},{6,4},{7,5},{8,10},{9,11},{10,... | collective-permute-start | bytes 49160 | tf_op jit(solution)/shard_map/ppermute | solution.py:427
  15.8 2.3 %collective-permute-start.3 = (f32[32,128]{1,0:T(8,128)S(1)}, f32[32,128]{1,0:T(8,128)S(1)}, u32[]{:S(2)}, u32[]{:S(2)}) collective-permute-start(f32[32,128]{1,0:T(8,128)S(1)} %get-tuple-element.43.refs_0_), channel_id=1, source_target_pairs={{0,1},{1,0},{2,3},{3,2},{4,5},{5,4},{6,7},{7,6},{8,9},{9,8},{10,11... | collective-permute-start | bytes 49160 | tf_op jit(solution)/shard_map/ppermute | solution.py:427
  18.3 6.5 %collective-permute-start.6 = (f32[8,1024]{1,0:T(8,128)S(1)}, f32[8,1024]{1,0:T(8,128)S(1)}, u32[]{:S(2)}, u32[]{:S(2)}) collective-permute-start(f32[8,1024]{1,0:T(8,128)S(1)} %get-tuple-element.51), channel_id=1, source_target_pairs={{0,12},{4,8},{8,4},{12,0},{1,13},{5,9},{9,5},{13,1},{2,14},{6,10},... | collective-permute-start | bytes 98312 | tf_op jit(solution)/shard_map/ppermute | solution.py:383
  19.9 5.1 %collective-permute-start.7 = (f32[8,1024]{1,0:T(8,128)S(1)}, f32[8,1024]{1,0:T(8,128)S(1)}, u32[]{:S(2)}, u32[]{:S(2)}) collective-permute-start(f32[8,1024]{1,0:T(8,128)S(1)} %get-tuple-element.52), channel_id=1, source_target_pairs={{0,8},{4,12},{8,0},{12,4},{1,9},{5,13},{9,1},{13,5},{2,10},{6,14},... | collective-permute-start | bytes 98312 | tf_op jit(solution)/shard_map/ppermute | solution.py:383
  20.5 4.8 %collective-permute-start.8 = (f32[8,1024]{1,0:T(8,128)S(1)}, f32[8,1024]{1,0:T(8,128)S(1)}, u32[]{:S(2)}, u32[]{:S(2)}) collective-permute-start(f32[8,1024]{1,0:T(8,128)S(1)} %get-tuple-element.53), channel_id=1, source_target_pairs={{0,4},{4,0},{8,12},{12,8},{1,5},{5,1},{9,13},{13,9},{2,6},{6,2},{1... | collective-permute-start | bytes 98312 | tf_op jit(solution)/shard_map/ppermute | solution.py:383

commit v6 on v5

--- a/solution.py
+++ b/solution.py
@@ -162,7 +162,7 @@
         place = jnp.where(hit, 1.0, place)
         mine = (lane_to >= first) & (lane_to < first + DECODE_STEPS)
         pick = jnp.where(mine, which, pick)
-    place_ref[...] = place
+    place_ref[...] = place.T.astype(BF16)
     place_bf = place.astype(BF16)
 
     reads = reads + read(6) + read(7)
@@ -266,7 +266,7 @@
     )
     n = terms.shape[0] // n_msg
     for k in range(n_msg):
-        outs[k][...] = terms[k * n : (k + 1) * n]
+        outs[k][...] = terms[k * n : (k + 1) * n].astype(BF16)
     rows = DECODE_STEPS * sessions
     sums = jnp.sum(total[:rows, rank:], axis=1, keepdims=True)
     factor = lax.rsqrt(sums / (HEAD_COUNT * HEAD_CHANNELS) + norm_eps)
@@ -277,14 +277,8 @@
     n_msg = len(order)
     msgs = [refs[order.index(k)] for k in range(n_msg)]
     place, inverse, out = refs[n_msg:]
-    terms = jnp.concatenate([m[...] for m in msgs], axis=0)
-    one_hot = place[...].astype(BF16)
-    mine = lax.dot_general(
-        jnp.concatenate([one_hot] * 3, axis=0),
-        jnp.concatenate(thirds(terms), axis=0),
-        (((0,), (0,)), ((), ())),
-        preferred_element_type=F32,
-    )
+    terms = jnp.concatenate([m[...].astype(F32) for m in msgs], axis=0)
+    mine = jnp.dot(place[...], terms.astype(BF16), preferred_element_type=F32)
     out[...] = (mine * inverse[:, :1]).reshape(out.shape)
 
 
@@ -353,7 +347,7 @@
             shape((channels, 2 * rows), BF16),
             shape((rows, LANES), F32),
             shape((sessions, heads), F32),
-            shape((targets, rows), F32),
+            shape((rows, targets), BF16),
             shape((1, channels), F32),
             shape(session_head_state.shape, BF16),
         ],
@@ -432,7 +426,7 @@
 
     out = pl.pallas_call(
         functools.partial(up_kernel, len(parts), n_msg, sessions),
-        out_shape=[shape((msg_rows, channels), F32)] * n_msg + [shape((rows, LANES), F32)],
+        out_shape=[shape((msg_rows, channels), BF16)] * n_msg + [shape((rows, LANES), F32)],
         in_specs=[vmem()] * (len(parts) + 2),
         out_specs=[vmem()] * (n_msg + 1),
         compiler_params=pltpu.CompilerParams(vmem_limit_bytes=4 << 20),

time: 26.3 us -> 25.9 us (0.985)
  waiting for transfers between devices: 5.13 us -> 4.68 us
    ppermute x6, waiting for transfers between devices: 3.17 us -> 2.73 us  [exchange(): lax.ppermute(blocks[k], 'batch', [(i, i ^ k) for i in range(batch_count)])]
  transfers between devices with their start and end apart: 9 -> 9, of which waited for: 5 -> 3; matrix products, arithmetic and copies ran while one was open for 0% -> 0% of each run, Pallas kernels for 13% -> 13%
where the time goes in v6:
time: 25.9 us; the launch traced here: 25.7 us
  starting transfers between devices  12.2 us (47%)
  Pallas kernels  8.13 us (31%)
  waiting for transfers between devices  4.68 us (18%)
  between operations  0.72 us (3%)
    ppermute x6, starting transfers between devices, exchange(): lax.ppermute(blocks[k], 'batch', [(i, i ^ k) for i in range(batch_count)])  10.2 us
    pallas_call x1, Pallas kernels, per_device(): pl.pallas_call(functools.partial(front_kernel, dims), out_shape=[shape((m...  3.59 us
    ppermute x6, waiting for transfers between devices, exchange(): lax.ppermute(blocks[k], 'batch', [(i, i ^ k) for i in range(batch_count)])  2.73 us
    pallas_call x1, Pallas kernels, per_device(): pl.pallas_call(close_kernel, out_shape=[pltpu.HBM((DECODE_STEPS, sessions...  2.03 us
    ppermute x3, waiting for transfers between devices, per_device(): lax.ppermute(partial, 'tensor', [(i, i ^ k) for i in range(tensor_count)])  1.96 us
    ppermute x3, starting transfers between devices, per_device(): lax.ppermute(partial, 'tensor', [(i, i ^ k) for i in range(tensor_count)])  1.96 us
    pallas_call x1, Pallas kernels, per_device(): pl.pallas_call(functools.partial(state_kernel, 0), out_shape=pltpu.VMEM((...  1.28 us
    pallas_call x1, Pallas kernels, per_device(): pl.pallas_call(functools.partial(final_kernel, order), out_shape=shape((D...  0.8 us
  transfers between devices with their start and end apart: 9, of which 3 were waited for; matrix products, arithmetic and copies ran while one was open for 0% of the time, Pallas kernels for 13%

profile of v6, /device:TPU:0, one launch (start us, length us, event | category | flops | bytes accessed | tf_op | source)
XLA Modules:
  0.0 25.7 jit_solution(2120539308900974088)
XLA Ops:
  0.6 3.6 %front.1 = (bf16[8,1152]{1,0:T(8,128)(2,1)S(1)}, bf16[8,1152]{1,0:T(8,128)(2,1)S(1)}, bf16[8,1152]{1,0:T(8,128)(2,1)S(1)}, bf16[8,1152]{1,0:T(8,128)(2,1)S(1)}, ...) custom-call(bf16[16,16,64,128]{3,2,1,0:T(8,128)(2,1)} %refs_0_.1, ...), custom_call_target="tpu_custom_call" | custom-call | flops 134217728 | bytes 4194304 | tf_op jit(solution)/shard_map/front/pallas_call | solution.py:341
  4.2 5.1 %collective-permute-start = (bf16[8,1152]{1,0:T(8,128)(2,1)S(1)}, bf16[8,1152]{1,0:T(8,128)(2,1)S(1)}, u32[]{:S(2)}, u32[]{:S(2)}) collective-permute-start(bf16[8,1152]{1,0:T(8,128)(2,1)S(1)} %get-tuple-element.31), channel_id=1, source_target_pairs={{0,12},{4,8},{8,4},{12,0},{1,13},{5,9},{9,5},{13,1},{2,14},{6,10},... | collective-permute-start | bytes 55304 | tf_op jit(solution)/shard_map/ppermute | solution.py:377
  9.3 0.0 collective-permute-start.1
  9.3 0.6 %collective-permute-start.2 = (bf16[8,1152]{1,0:T(8,128)(2,1)S(1)}, bf16[8,1152]{1,0:T(8,128)(2,1)S(1)}, u32[]{:S(2)}, u32[]{:S(2)}) collective-permute-start(bf16[8,1152]{1,0:T(8,128)(2,1)S(1)} %get-tuple-element.33), channel_id=1, source_target_pairs={{0,4},{4,0},{8,12},{12,8},{1,5},{5,1},{9,13},{13,9},{2,6},{6,2},{1... | collective-permute-start | bytes 55304 | tf_op jit(solution)/shard_map/ppermute | solution.py:377
  10.0 1.3 %state.1.made = bf16[16,16,64,128]{3,2,1,0:T(8,128)(2,1)S(1)} custom-call(bf16[1024,64]{1,0:T(8,128)(2,1)S(1)} %get-tuple-element.34.left, f32[32,128]{1,0:T(8,128)S(1)} %get-tuple-element.35.b, f32[16,16]{1,0:T(8,128)S(1)} %get-tuple-element.36.keep, bf16[16,16,64,128]{3,2,1,0:T(8,128)(2,1)S(1)} %get-tuple-element.37.state), custom_call_target="tpu_custom_call" | custom-call | flops 16777216 | bytes 8388608 | tf_op jit(solution)/shard_map/state/pallas_call | solution.py:399
  11.3 0.0 collective-permute-done.refs_1_
  11.3 2.7 %collective-permute-done.1.refs_2_ = bf16[8,1152]{1,0:T(8,128)(2,1)S(1)} collective-permute-done((bf16[8,1152]{1,0:T(8,128)(2,1)S(1)}, bf16[8,1152]{1,0:T(8,128)(2,1)S(1)}, u32[]{:S(2)}, u32[]{:S(2)}) %collective-permute-start.1) | collective-permute-done | bytes 18464 | tf_op jit(solution)/shard_map/ppermute | solution.py:377
  14.0 0.0 collective-permute-done.2.refs_3_
  14.0 0.2 down.1
  14.2 0.1 collective-permute-start.5
  14.3 1.6 %collective-permute-start.4 = (f32[32,128]{1,0:T(8,128)S(1)}, f32[32,128]{1,0:T(8,128)S(1)}, u32[]{:S(2)}, u32[]{:S(2)}) collective-permute-start(f32[32,128]{1,0:T(8,128)S(1)} %get-tuple-element.43.refs_0_), channel_id=1, source_target_pairs={{0,2},{1,3},{2,0},{3,1},{4,6},{5,7},{6,4},{7,5},{8,10},{9,11},{10,... | collective-permute-start | bytes 49160 | tf_op jit(solution)/shard_map/ppermute | solution.py:421
  15.9 0.3 %collective-permute-start.3 = (f32[32,128]{1,0:T(8,128)S(1)}, f32[32,128]{1,0:T(8,128)S(1)}, u32[]{:S(2)}, u32[]{:S(2)}) collective-permute-start(f32[32,128]{1,0:T(8,128)S(1)} %get-tuple-element.43.refs_0_), channel_id=1, source_target_pairs={{0,1},{1,0},{2,3},{3,2},{4,5},{5,4},{6,7},{7,6},{8,9},{9,8},{10,11... | collective-permute-start | bytes 49160 | tf_op jit(solution)/shard_map/ppermute | solution.py:421
  16.2 1.4 %collective-permute-done.5.refs_3_ = f32[32,128]{1,0:T(8,128)S(1)} collective-permute-done((f32[32,128]{1,0:T(8,128)S(1)}, f32[32,128]{1,0:T(8,128)S(1)}, u32[]{:S(2)}, u32[]{:S(2)}) %collective-permute-start.5) | collective-permute-done | bytes 16416 | tf_op jit(solution)/shard_map/ppermute | solution.py:421
  17.6 0.5 %collective-permute-done.4.refs_2_ = f32[32,128]{1,0:T(8,128)S(1)} collective-permute-done((f32[32,128]{1,0:T(8,128)S(1)}, f32[32,128]{1,0:T(8,128)S(1)}, u32[]{:S(2)}, u32[]{:S(2)}) %collective-permute-start.4) | collective-permute-done | bytes 16416 | tf_op jit(solution)/shard_map/ppermute | solution.py:421
  18.1 0.0 collective-permute-done.3.refs_1_
  18.2 0.2 up.1
  18.4 1.5 %collective-permute-start.6 = (bf16[8,1024]{1,0:T(8,128)(2,1)S(1)}, bf16[8,1024]{1,0:T(8,128)(2,1)S(1)}, u32[]{:S(2)}, u32[]{:S(2)}) collective-permute-start(bf16[8,1024]{1,0:T(8,128)(2,1)S(1)} %get-tuple-element.51), channel_id=1, source_target_pairs={{0,12},{4,8},{8,4},{12,0},{1,13},{5,9},{9,5},{13,1},{2,14},{6,10},... | collective-permute-start | bytes 49160 | tf_op jit(solution)/shard_map/ppermute | solution.py:377
  19.9 0.6 %collective-permute-start.7 = (bf16[8,1024]{1,0:T(8,128)(2,1)S(1)}, bf16[8,1024]{1,0:T(8,128)(2,1)S(1)}, u32[]{:S(2)}, u32[]{:S(2)}) collective-permute-start(bf16[8,1024]{1,0:T(8,128)(2,1)S(1)} %get-tuple-element.52), channel_id=1, source_target_pairs={{0,8},{4,12},{8,0},{12,4},{1,9},{5,13},{9,1},{13,5},{2,10},{6,14},... | collective-permute-start | bytes 49160 | tf_op jit(solution)/shard_map/ppermute | solution.py:377
  20.5 2.3 %collective-permute-start.8 = (bf16[8,1024]{1,0:T(8,128)(2,1)S(1)}, bf16[8,1024]{1,0:T(8,128)(2,1)S(1)}, u32[]{:S(2)}, u32[]{:S(2)}) collective-permute-start(bf16[8,1024]{1,0:T(8,128)(2,1)S(1)} %get-tuple-element.53), channel_id=1, source_target_pairs={{0,4},{4,0},{8,12},{12,8},{1,5},{5,1},{9,13},{13,9},{2,6},{6,2},{1... | collective-permute-start | bytes 49160 | tf_op jit(solution)/shard_map/ppermute | solution.py:377
  22.8 2.0 %close.1 = (bf16[2,16,1024]{2,1,0:T(8,128)(2,1)}, bf16[16,16,64,128]{3,2,1,0:T(8,128)(2,1)}) custom-call(f32[32,1024]{1,0:T(8,128)S(1)} %get-tuple-element.29.gated, f32[32,128]{1,0:T(8,128)S(1)} %get-tuple-element.45.inverse.refs_5_, f32[1,1024]{1,0:T(1,128)S(1)} %get-tuple-element.46.gain, bf16[16,16,64,128]{3,2,1,0:T(8,128)(2,1)S(1)} %state.1.made), custom_call_target="tpu_custom_call" | custom-call | flops 16777216 | bytes 8388608 | tf_op jit(solution)/shard_map/close/pallas_call | solution.py:439
  24.9 0.0 collective-permute-done.6.refs_1_
  24.9 0.0 collective-permute-done.7.refs_2_
  24.9 0.0 collective-permute-done.8.refs_3_
  24.9 0.8 %final.1 = f32[2,16,1024]{2,1,0:T(8,128)} custom-call(bf16[8,1024]{1,0:T(8,128)(2,1)S(1)} %get-tuple-element.50.refs_0_, bf16[8,1024]{1,0:T(8,128)(2,1)S(1)} %collective-permute-done.6.refs_1_, bf16[8,1024]{1,0:T(8,128)(2,1)S(1)} %collective-permute-done.7.refs_2_, bf16[8,1024]{1,0:T(8,128)(2,1)S(1)} %collective-permute-done.8.refs_3_, ...), custom_call_target="tpu_custom_call" | custom-call | tf_op jit(solution)/shard_map/final/pallas_call | solution.py:456
  (4 shorter events, 0.0 us)
Async XLA Ops:
  4.2 7.1 %collective-permute-start = (bf16[8,1152]{1,0:T(8,128)(2,1)S(1)}, bf16[8,1152]{1,0:T(8,128)(2,1)S(1)}, u32[]{:S(2)}, u32[]{:S(2)}) collective-permute-start(bf16[8,1152]{1,0:T(8,128)(2,1)S(1)} %get-tuple-element.31), channel_id=1, source_target_pairs={{0,12},{4,8},{8,4},{12,0},{1,13},{5,9},{9,5},{13,1},{2,14},{6,10},... | collective-permute-start | bytes 55304 | tf_op jit(solution)/shard_map/ppermute | solution.py:377
  9.3 4.7 %collective-permute-start.1 = (bf16[8,1152]{1,0:T(8,128)(2,1)S(1)}, bf16[8,1152]{1,0:T(8,128)(2,1)S(1)}, u32[]{:S(2)}, u32[]{:S(2)}) collective-permute-start(bf16[8,1152]{1,0:T(8,128)(2,1)S(1)} %get-tuple-element.32), channel_id=1, source_target_pairs={{0,8},{4,12},{8,0},{12,4},{1,9},{5,13},{9,1},{13,5},{2,10},{6,14},... | collective-permute-start | bytes 55304 | tf_op jit(solution)/shard_map/ppermute | solution.py:377
  9.3 4.7 %collective-permute-start.2 = (bf16[8,1152]{1,0:T(8,128)(2,1)S(1)}, bf16[8,1152]{1,0:T(8,128)(2,1)S(1)}, u32[]{:S(2)}, u32[]{:S(2)}) collective-permute-start(bf16[8,1152]{1,0:T(8,128)(2,1)S(1)} %get-tuple-element.33), channel_id=1, source_target_pairs={{0,4},{4,0},{8,12},{12,8},{1,5},{5,1},{9,13},{13,9},{2,6},{6,2},{1... | collective-permute-start | bytes 55304 | tf_op jit(solution)/shard_map/ppermute | solution.py:377
  10.0 4.0 %copy-start = (bf16[2,64,1024]{2,1,0:T(8,128)(2,1)S(1)}, bf16[2,64,1024]{2,1,0:T(8,128)(2,1)}, u32[]{:S(2)}) copy-start(bf16[2,64,1024]{2,1,0:T(8,128)(2,1)} %refs_4_.3) | copy-start | bytes 786436
  10.0 8.2 %copy-start.1 = (bf16[2,64,1024]{2,1,0:T(8,128)(2,1)S(1)}, bf16[2,64,1024]{2,1,0:T(8,128)(2,1)}, u32[]{:S(2)}) copy-start(bf16[2,64,1024]{2,1,0:T(8,128)(2,1)} %refs_5_.3) | copy-start | bytes 786436
  14.2 3.4 %collective-permute-start.5 = (f32[32,128]{1,0:T(8,128)S(1)}, f32[32,128]{1,0:T(8,128)S(1)}, u32[]{:S(2)}, u32[]{:S(2)}) collective-permute-start(f32[32,128]{1,0:T(8,128)S(1)} %get-tuple-element.43.refs_0_), channel_id=1, source_target_pairs={{0,3},{1,2},{2,1},{3,0},{4,7},{5,6},{6,5},{7,4},{8,11},{9,10},{10,... | collective-permute-start | bytes 49160 | tf_op jit(solution)/shard_map/ppermute | solution.py:421
  14.3 3.8 %collective-permute-start.4 = (f32[32,128]{1,0:T(8,128)S(1)}, f32[32,128]{1,0:T(8,128)S(1)}, u32[]{:S(2)}, u32[]{:S(2)}) collective-permute-start(f32[32,128]{1,0:T(8,128)S(1)} %get-tuple-element.43.refs_0_), channel_id=1, source_target_pairs={{0,2},{1,3},{2,0},{3,1},{4,6},{5,7},{6,4},{7,5},{8,10},{9,11},{10,... | collective-permute-start | bytes 49160 | tf_op jit(solution)/shard_map/ppermute | solution.py:421
  15.9 2.2 %collective-permute-start.3 = (f32[32,128]{1,0:T(8,128)S(1)}, f32[32,128]{1,0:T(8,128)S(1)}, u32[]{:S(2)}, u32[]{:S(2)}) collective-permute-start(f32[32,128]{1,0:T(8,128)S(1)} %get-tuple-element.43.refs_0_), channel_id=1, source_target_pairs={{0,1},{1,0},{2,3},{3,2},{4,5},{5,4},{6,7},{7,6},{8,9},{9,8},{10,11... | collective-permute-start | bytes 49160 | tf_op jit(solution)/shard_map/ppermute | solution.py:421
  18.4 6.5 %collective-permute-start.6 = (bf16[8,1024]{1,0:T(8,128)(2,1)S(1)}, bf16[8,1024]{1,0:T(8,128)(2,1)S(1)}, u32[]{:S(2)}, u32[]{:S(2)}) collective-permute-start(bf16[8,1024]{1,0:T(8,128)(2,1)S(1)} %get-tuple-element.51), channel_id=1, source_target_pairs={{0,12},{4,8},{8,4},{12,0},{1,13},{5,9},{9,5},{13,1},{2,14},{6,10},... | collective-permute-start | bytes 49160 | tf_op jit(solution)/shard_map/ppermute | solution.py:377
  19.9 5.0 %collective-permute-start.7 = (bf16[8,1024]{1,0:T(8,128)(2,1)S(1)}, bf16[8,1024]{1,0:T(8,128)(2,1)S(1)}, u32[]{:S(2)}, u32[]{:S(2)}) collective-permute-start(bf16[8,1024]{1,0:T(8,128)(2,1)S(1)} %get-tuple-element.52), channel_id=1, source_target_pairs={{0,8},{4,12},{8,0},{12,4},{1,9},{5,13},{9,1},{13,5},{2,10},{6,14},... | collective-permute-start | bytes 49160 | tf_op jit(solution)/shard_map/ppermute | solution.py:377
  20.5 4.4 %collective-permute-start.8 = (bf16[8,1024]{1,0:T(8,128)(2,1)S(1)}, bf16[8,1024]{1,0:T(8,128)(2,1)S(1)}, u32[]{:S(2)}, u32[]{:S(2)}) collective-permute-start(bf16[8,1024]{1,0:T(8,128)(2,1)S(1)} %get-tuple-element.53), channel_id=1, source_target_pairs={{0,4},{4,0},{8,12},{12,8},{1,5},{5,1},{9,13},{13,9},{2,6},{6,2},{1... | collective-permute-start | bytes 49160 | tf_op jit(solution)/shard_map/ppermute | solution.py:377

commit v7 on v6

--- a/solution.py
+++ b/solution.py
@@ -52,7 +52,8 @@
         pltpu.make_async_copy(source, target, small_sems.at[i])
         for i, (source, target) in enumerate(zip(inputs[1:], local))
     ]
-    for load in loads:
+    first, later = loads[4:10], loads[:4] + loads[10:]
+    for load in first:
         load.start()
     copies = []
     for i in range(chunks):
@@ -61,10 +62,12 @@
         copies.append(copy)
     for copy in copies[:depth]:
         copy.start()
+    for load in later:
+        load.start()
     adapter, slot_of, x, z, b, c, raw, bias, rate, skip, gain_rows = local
     me = lax.axis_index("batch")
     group = lax.axis_index("tensor") * heads // (HEAD_COUNT // GROUPS)
-    for load in loads:
+    for load in first[:2]:
         load.wait()
     def pick_group(ref):
         values = ref[...].astype(F32).reshape(rows, GROUPS, LANES)
@@ -88,6 +91,8 @@
         return lax.dot_general(c_blocks[:, lanes], block, NT, preferred_element_type=F32)
 
     reads = read(0) + read(1)
+    for load in first[2:] + later:
+        load.wait()
     b1, b2 = b_rows[:sessions], b_rows[sessions:]
     c1, c2 = c_rows[:sessions], c_rows[sessions:]
     bc11 = jnp.sum(b1 * c1, axis=1, keepdims=True)
@@ -260,10 +265,15 @@
     ranks = total[:, :rank]
     left = jnp.concatenate(
         [jnp.where(pick[:, :rank] == j, ranks, 0.0) for j in range(held)], axis=1
-    ).astype(BF16)
-    terms = adapter_scale * jnp.dot(
-        left, up[...].reshape(held * rank, channels), preferred_element_type=F32
-    )
+    )
+    high = left.astype(BF16)
+    weights = up[...].reshape(held * rank, channels)
+    both = jnp.dot(
+        jnp.concatenate([left, left - high.astype(F32)], axis=0).astype(BF16),
+        weights,
+        preferred_element_type=F32,
+    )
+    terms = adapter_scale * (both[: left.shape[0]] + both[left.shape[0] :])
     n = terms.shape[0] // n_msg
     for k in range(n_msg):
         outs[k][...] = terms[k * n : (k + 1) * n].astype(BF16)

time: 25.9 us -> 25.8 us (level)
  no operation moved by 1% of the time
where the time goes in v7:
time: 25.8 us; the launch traced here: 25.6 us
  starting transfers between devices  12.2 us (47%)
  Pallas kernels  7.99 us (31%)
  waiting for transfers between devices  4.68 us (18%)
  between operations  0.72 us (3%)
    ppermute x6, starting transfers between devices, exchange(): lax.ppermute(blocks[k], 'batch', [(i, i ^ k) for i in range(batch_count)])  10.2 us
    pallas_call x1, Pallas kernels, per_device(): pl.pallas_call(functools.partial(front_kernel, dims), out_shape=[shape((m...  3.44 us
    ppermute x6, waiting for transfers between devices, exchange(): lax.ppermute(blocks[k], 'batch', [(i, i ^ k) for i in range(batch_count)])  2.72 us
    pallas_call x1, Pallas kernels, per_device(): pl.pallas_call(close_kernel, out_shape=[pltpu.HBM((DECODE_STEPS, sessions...  2.03 us
    ppermute x3, waiting for transfers between devices, per_device(): lax.ppermute(partial, 'tensor', [(i, i ^ k) for i in range(tensor_count)])  1.96 us
    ppermute x3, starting transfers between devices, per_device(): lax.ppermute(partial, 'tensor', [(i, i ^ k) for i in range(tensor_count)])  1.96 us
    pallas_call x1, Pallas kernels, per_device(): pl.pallas_call(functools.partial(state_kernel, 0), out_shape=pltpu.VMEM((...  1.28 us
    pallas_call x1, Pallas kernels, per_device(): pl.pallas_call(functools.partial(final_kernel, order), out_shape=shape((D...  0.8 us
  transfers between devices with their start and end apart: 9, of which 3 were waited for; matrix products, arithmetic and copies ran while one was open for 0% of the time, Pallas kernels for 13%

profile of v7, /device:TPU:0, one launch (start us, length us, event | category | flops | bytes accessed | tf_op | source)
XLA Modules:
  0.0 25.6 jit_solution(1661086685781866427)
XLA Ops:
  0.6 3.4 %front.1 = (bf16[8,1152]{1,0:T(8,128)(2,1)S(1)}, bf16[8,1152]{1,0:T(8,128)(2,1)S(1)}, bf16[8,1152]{1,0:T(8,128)(2,1)S(1)}, bf16[8,1152]{1,0:T(8,128)(2,1)S(1)}, ...) custom-call(bf16[16,16,64,128]{3,2,1,0:T(8,128)(2,1)} %refs_0_.1, ...), custom_call_target="tpu_custom_call" | custom-call | flops 134217728 | bytes 4194304 | tf_op jit(solution)/shard_map/front/pallas_call | solution.py:351
  4.1 5.1 %collective-permute-start = (bf16[8,1152]{1,0:T(8,128)(2,1)S(1)}, bf16[8,1152]{1,0:T(8,128)(2,1)S(1)}, u32[]{:S(2)}, u32[]{:S(2)}) collective-permute-start(bf16[8,1152]{1,0:T(8,128)(2,1)S(1)} %get-tuple-element.31), channel_id=1, source_target_pairs={{0,12},{4,8},{8,4},{12,0},{1,13},{5,9},{9,5},{13,1},{2,14},{6,10},... | collective-permute-start | bytes 55304 | tf_op jit(solution)/shard_map/ppermute | solution.py:387
  9.2 0.0 collective-permute-start.1
  9.2 0.6 %collective-permute-start.2 = (bf16[8,1152]{1,0:T(8,128)(2,1)S(1)}, bf16[8,1152]{1,0:T(8,128)(2,1)S(1)}, u32[]{:S(2)}, u32[]{:S(2)}) collective-permute-start(bf16[8,1152]{1,0:T(8,128)(2,1)S(1)} %get-tuple-element.33), channel_id=1, source_target_pairs={{0,4},{4,0},{8,12},{12,8},{1,5},{5,1},{9,13},{13,9},{2,6},{6,2},{1... | collective-permute-start | bytes 55304 | tf_op jit(solution)/shard_map/ppermute | solution.py:387
  9.8 1.3 %state.1.made = bf16[16,16,64,128]{3,2,1,0:T(8,128)(2,1)S(1)} custom-call(bf16[1024,64]{1,0:T(8,128)(2,1)S(1)} %get-tuple-element.34.left, f32[32,128]{1,0:T(8,128)S(1)} %get-tuple-element.35.b, f32[16,16]{1,0:T(8,128)S(1)} %get-tuple-element.36.keep, bf16[16,16,64,128]{3,2,1,0:T(8,128)(2,1)S(1)} %get-tuple-element.37.state), custom_call_target="tpu_custom_call" | custom-call | flops 16777216 | bytes 8388608 | tf_op jit(solution)/shard_map/state/pallas_call | solution.py:409
  11.1 0.0 collective-permute-done.refs_1_
  11.2 2.7 %collective-permute-done.1.refs_2_ = bf16[8,1152]{1,0:T(8,128)(2,1)S(1)} collective-permute-done((bf16[8,1152]{1,0:T(8,128)(2,1)S(1)}, bf16[8,1152]{1,0:T(8,128)(2,1)S(1)}, u32[]{:S(2)}, u32[]{:S(2)}) %collective-permute-start.1) | collective-permute-done | bytes 18464 | tf_op jit(solution)/shard_map/ppermute | solution.py:387
  13.9 0.0 collective-permute-done.2.refs_3_
  13.9 0.2 down.1
  14.1 0.1 collective-permute-start.5
  14.2 1.6 %collective-permute-start.4 = (f32[32,128]{1,0:T(8,128)S(1)}, f32[32,128]{1,0:T(8,128)S(1)}, u32[]{:S(2)}, u32[]{:S(2)}) collective-permute-start(f32[32,128]{1,0:T(8,128)S(1)} %get-tuple-element.43.refs_0_), channel_id=1, source_target_pairs={{0,2},{1,3},{2,0},{3,1},{4,6},{5,7},{6,4},{7,5},{8,10},{9,11},{10,... | collective-permute-start | bytes 49160 | tf_op jit(solution)/shard_map/ppermute | solution.py:431
  15.8 0.3 %collective-permute-start.3 = (f32[32,128]{1,0:T(8,128)S(1)}, f32[32,128]{1,0:T(8,128)S(1)}, u32[]{:S(2)}, u32[]{:S(2)}) collective-permute-start(f32[32,128]{1,0:T(8,128)S(1)} %get-tuple-element.43.refs_0_), channel_id=1, source_target_pairs={{0,1},{1,0},{2,3},{3,2},{4,5},{5,4},{6,7},{7,6},{8,9},{9,8},{10,11... | collective-permute-start | bytes 49160 | tf_op jit(solution)/shard_map/ppermute | solution.py:431
  16.0 1.4 %collective-permute-done.5.refs_3_ = f32[32,128]{1,0:T(8,128)S(1)} collective-permute-done((f32[32,128]{1,0:T(8,128)S(1)}, f32[32,128]{1,0:T(8,128)S(1)}, u32[]{:S(2)}, u32[]{:S(2)}) %collective-permute-start.5) | collective-permute-done | bytes 16416 | tf_op jit(solution)/shard_map/ppermute | solution.py:431
  17.5 0.5 %collective-permute-done.4.refs_2_ = f32[32,128]{1,0:T(8,128)S(1)} collective-permute-done((f32[32,128]{1,0:T(8,128)S(1)}, f32[32,128]{1,0:T(8,128)S(1)}, u32[]{:S(2)}, u32[]{:S(2)}) %collective-permute-start.4) | collective-permute-done | bytes 16416 | tf_op jit(solution)/shard_map/ppermute | solution.py:431
  18.0 0.0 collective-permute-done.3.refs_1_
  18.0 0.2 up.1
  18.2 1.5 %collective-permute-start.6 = (bf16[8,1024]{1,0:T(8,128)(2,1)S(1)}, bf16[8,1024]{1,0:T(8,128)(2,1)S(1)}, u32[]{:S(2)}, u32[]{:S(2)}) collective-permute-start(bf16[8,1024]{1,0:T(8,128)(2,1)S(1)} %get-tuple-element.51), channel_id=1, source_target_pairs={{0,12},{4,8},{8,4},{12,0},{1,13},{5,9},{9,5},{13,1},{2,14},{6,10},... | collective-permute-start | bytes 49160 | tf_op jit(solution)/shard_map/ppermute | solution.py:387
  19.8 0.6 %collective-permute-start.7 = (bf16[8,1024]{1,0:T(8,128)(2,1)S(1)}, bf16[8,1024]{1,0:T(8,128)(2,1)S(1)}, u32[]{:S(2)}, u32[]{:S(2)}) collective-permute-start(bf16[8,1024]{1,0:T(8,128)(2,1)S(1)} %get-tuple-element.52), channel_id=1, source_target_pairs={{0,8},{4,12},{8,0},{12,4},{1,9},{5,13},{9,1},{13,5},{2,10},{6,14},... | collective-permute-start | bytes 49160 | tf_op jit(solution)/shard_map/ppermute | solution.py:387
  20.4 2.3 %collective-permute-start.8 = (bf16[8,1024]{1,0:T(8,128)(2,1)S(1)}, bf16[8,1024]{1,0:T(8,128)(2,1)S(1)}, u32[]{:S(2)}, u32[]{:S(2)}) collective-permute-start(bf16[8,1024]{1,0:T(8,128)(2,1)S(1)} %get-tuple-element.53), channel_id=1, source_target_pairs={{0,4},{4,0},{8,12},{12,8},{1,5},{5,1},{9,13},{13,9},{2,6},{6,2},{1... | collective-permute-start | bytes 49160 | tf_op jit(solution)/shard_map/ppermute | solution.py:387
  22.7 2.0 %close.1 = (bf16[2,16,1024]{2,1,0:T(8,128)(2,1)}, bf16[16,16,64,128]{3,2,1,0:T(8,128)(2,1)}) custom-call(f32[32,1024]{1,0:T(8,128)S(1)} %get-tuple-element.29.gated, f32[32,128]{1,0:T(8,128)S(1)} %get-tuple-element.45.inverse.refs_5_, f32[1,1024]{1,0:T(1,128)S(1)} %get-tuple-element.46.gain, bf16[16,16,64,128]{3,2,1,0:T(8,128)(2,1)S(1)} %state.1.made), custom_call_target="tpu_custom_call" | custom-call | flops 16777216 | bytes 8388608 | tf_op jit(solution)/shard_map/close/pallas_call | solution.py:449
  24.7 0.0 collective-permute-done.6.refs_1_
  24.8 0.0 collective-permute-done.7.refs_2_
  24.8 0.0 collective-permute-done.8.refs_3_
  24.8 0.8 %final.1 = f32[2,16,1024]{2,1,0:T(8,128)} custom-call(bf16[8,1024]{1,0:T(8,128)(2,1)S(1)} %get-tuple-element.50.refs_0_, bf16[8,1024]{1,0:T(8,128)(2,1)S(1)} %collective-permute-done.6.refs_1_, bf16[8,1024]{1,0:T(8,128)(2,1)S(1)} %collective-permute-done.7.refs_2_, bf16[8,1024]{1,0:T(8,128)(2,1)S(1)} %collective-permute-done.8.refs_3_, ...), custom_call_target="tpu_custom_call" | custom-call | tf_op jit(solution)/shard_map/final/pallas_call | solution.py:466
  (4 shorter events, 0.0 us)
Async XLA Ops:
  4.1 7.1 %collective-permute-start = (bf16[8,1152]{1,0:T(8,128)(2,1)S(1)}, bf16[8,1152]{1,0:T(8,128)(2,1)S(1)}, u32[]{:S(2)}, u32[]{:S(2)}) collective-permute-start(bf16[8,1152]{1,0:T(8,128)(2,1)S(1)} %get-tuple-element.31), channel_id=1, source_target_pairs={{0,12},{4,8},{8,4},{12,0},{1,13},{5,9},{9,5},{13,1},{2,14},{6,10},... | collective-permute-start | bytes 55304 | tf_op jit(solution)/shard_map/ppermute | solution.py:387
  9.2 4.7 %collective-permute-start.1 = (bf16[8,1152]{1,0:T(8,128)(2,1)S(1)}, bf16[8,1152]{1,0:T(8,128)(2,1)S(1)}, u32[]{:S(2)}, u32[]{:S(2)}) collective-permute-start(bf16[8,1152]{1,0:T(8,128)(2,1)S(1)} %get-tuple-element.32), channel_id=1, source_target_pairs={{0,8},{4,12},{8,0},{12,4},{1,9},{5,13},{9,1},{13,5},{2,10},{6,14},... | collective-permute-start | bytes 55304 | tf_op jit(solution)/shard_map/ppermute | solution.py:387
  9.2 4.7 %collective-permute-start.2 = (bf16[8,1152]{1,0:T(8,128)(2,1)S(1)}, bf16[8,1152]{1,0:T(8,128)(2,1)S(1)}, u32[]{:S(2)}, u32[]{:S(2)}) collective-permute-start(bf16[8,1152]{1,0:T(8,128)(2,1)S(1)} %get-tuple-element.33), channel_id=1, source_target_pairs={{0,4},{4,0},{8,12},{12,8},{1,5},{5,1},{9,13},{13,9},{2,6},{6,2},{1... | collective-permute-start | bytes 55304 | tf_op jit(solution)/shard_map/ppermute | solution.py:387
  9.8 4.0 %copy-start = (bf16[2,64,1024]{2,1,0:T(8,128)(2,1)S(1)}, bf16[2,64,1024]{2,1,0:T(8,128)(2,1)}, u32[]{:S(2)}) copy-start(bf16[2,64,1024]{2,1,0:T(8,128)(2,1)} %refs_4_.3) | copy-start | bytes 786436
  9.8 8.2 %copy-start.1 = (bf16[2,64,1024]{2,1,0:T(8,128)(2,1)S(1)}, bf16[2,64,1024]{2,1,0:T(8,128)(2,1)}, u32[]{:S(2)}) copy-start(bf16[2,64,1024]{2,1,0:T(8,128)(2,1)} %refs_5_.3) | copy-start | bytes 786436
  14.1 3.4 %collective-permute-start.5 = (f32[32,128]{1,0:T(8,128)S(1)}, f32[32,128]{1,0:T(8,128)S(1)}, u32[]{:S(2)}, u32[]{:S(2)}) collective-permute-start(f32[32,128]{1,0:T(8,128)S(1)} %get-tuple-element.43.refs_0_), channel_id=1, source_target_pairs={{0,3},{1,2},{2,1},{3,0},{4,7},{5,6},{6,5},{7,4},{8,11},{9,10},{10,... | collective-permute-start | bytes 49160 | tf_op jit(solution)/shard_map/ppermute | solution.py:431
  14.2 3.8 %collective-permute-start.4 = (f32[32,128]{1,0:T(8,128)S(1)}, f32[32,128]{1,0:T(8,128)S(1)}, u32[]{:S(2)}, u32[]{:S(2)}) collective-permute-start(f32[32,128]{1,0:T(8,128)S(1)} %get-tuple-element.43.refs_0_), channel_id=1, source_target_pairs={{0,2},{1,3},{2,0},{3,1},{4,6},{5,7},{6,4},{7,5},{8,10},{9,11},{10,... | collective-permute-start | bytes 49160 | tf_op jit(solution)/shard_map/ppermute | solution.py:431
  15.8 2.3 %collective-permute-start.3 = (f32[32,128]{1,0:T(8,128)S(1)}, f32[32,128]{1,0:T(8,128)S(1)}, u32[]{:S(2)}, u32[]{:S(2)}) collective-permute-start(f32[32,128]{1,0:T(8,128)S(1)} %get-tuple-element.43.refs_0_), channel_id=1, source_target_pairs={{0,1},{1,0},{2,3},{3,2},{4,5},{5,4},{6,7},{7,6},{8,9},{9,8},{10,11... | collective-permute-start | bytes 49160 | tf_op jit(solution)/shard_map/ppermute | solution.py:431
  18.2 6.5 %collective-permute-start.6 = (bf16[8,1024]{1,0:T(8,128)(2,1)S(1)}, bf16[8,1024]{1,0:T(8,128)(2,1)S(1)}, u32[]{:S(2)}, u32[]{:S(2)}) collective-permute-start(bf16[8,1024]{1,0:T(8,128)(2,1)S(1)} %get-tuple-element.51), channel_id=1, source_target_pairs={{0,12},{4,8},{8,4},{12,0},{1,13},{5,9},{9,5},{13,1},{2,14},{6,10},... | collective-permute-start | bytes 49160 | tf_op jit(solution)/shard_map/ppermute | solution.py:387
  19.8 5.0 %collective-permute-start.7 = (bf16[8,1024]{1,0:T(8,128)(2,1)S(1)}, bf16[8,1024]{1,0:T(8,128)(2,1)S(1)}, u32[]{:S(2)}, u32[]{:S(2)}) collective-permute-start(bf16[8,1024]{1,0:T(8,128)(2,1)S(1)} %get-tuple-element.52), channel_id=1, source_target_pairs={{0,8},{4,12},{8,0},{12,4},{1,9},{5,13},{9,1},{13,5},{2,10},{6,14},... | collective-permute-start | bytes 49160 | tf_op jit(solution)/shard_map/ppermute | solution.py:387
  20.4 4.4 %collective-permute-start.8 = (bf16[8,1024]{1,0:T(8,128)(2,1)S(1)}, bf16[8,1024]{1,0:T(8,128)(2,1)S(1)}, u32[]{:S(2)}, u32[]{:S(2)}) collective-permute-start(bf16[8,1024]{1,0:T(8,128)(2,1)S(1)} %get-tuple-element.53), channel_id=1, source_target_pairs={{0,4},{4,0},{8,12},{12,8},{1,5},{5,1},{9,13},{13,9},{2,6},{6,2},{1... | collective-permute-start | bytes 49160 | tf_op jit(solution)/shard_map/ppermute | solution.py:387

commit v8 on v7

--- a/solution.py
+++ b/solution.py
@@ -88,7 +88,19 @@
         block = jnp.concatenate(
             [held[i * part + s].reshape(channels, LANES) for s in range(part)], axis=1
         )
-        return lax.dot_general(c_blocks[:, lanes], block, NT, preferred_element_type=F32)
+        quarter = channels // 4
+        return jnp.concatenate(
+            [
+                lax.dot_general(
+                    c_blocks[:, lanes],
+                    block[q * quarter : (q + 1) * quarter],
+                    NT,
+                    preferred_element_type=F32,
+                )
+                for q in range(4)
+            ],
+            axis=1,
+        )
 
     reads = read(0) + read(1)
     for load in first[2:] + later:

time: 25.8 us -> 25.7 us (level)
  no operation moved by 1% of the time
where the time goes in v8:
time: 25.7 us; the launch traced here: 25.6 us
  starting transfers between devices  12.2 us (47%)
  Pallas kernels  7.96 us (31%)
  waiting for transfers between devices  4.68 us (18%)
  between operations  0.72 us (3%)
    ppermute x6, starting transfers between devices, exchange(): lax.ppermute(blocks[k], 'batch', [(i, i ^ k) for i in range(batch_count)])  10.2 us
    pallas_call x1, Pallas kernels, per_device(): pl.pallas_call(functools.partial(front_kernel, dims), out_shape=[shape((m...  3.41 us
    ppermute x6, waiting for transfers between devices, exchange(): lax.ppermute(blocks[k], 'batch', [(i, i ^ k) for i in range(batch_count)])  2.72 us
    pallas_call x1, Pallas kernels, per_device(): pl.pallas_call(close_kernel, out_shape=[pltpu.HBM((DECODE_STEPS, sessions...  2.03 us
    ppermute x3, waiting for transfers between devices, per_device(): lax.ppermute(partial, 'tensor', [(i, i ^ k) for i in range(tensor_count)])  1.96 us
    ppermute x3, starting transfers between devices, per_device(): lax.ppermute(partial, 'tensor', [(i, i ^ k) for i in range(tensor_count)])  1.96 us
    pallas_call x1, Pallas kernels, per_device(): pl.pallas_call(functools.partial(state_kernel, 0), out_shape=pltpu.VMEM((...  1.29 us
    pallas_call x1, Pallas kernels, per_device(): pl.pallas_call(functools.partial(final_kernel, order), out_shape=shape((D...  0.8 us
  transfers between devices with their start and end apart: 9, of which 3 were waited for; matrix products, arithmetic and copies ran while one was open for 0% of the time, Pallas kernels for 13%

profile of v8, /device:TPU:0, one launch (start us, length us, event | category | flops | bytes accessed | tf_op | source)
XLA Modules:
  0.0 25.6 jit_solution(11408757264927783396)
XLA Ops:
  0.6 3.4 %front.1 = (bf16[8,1152]{1,0:T(8,128)(2,1)S(1)}, bf16[8,1152]{1,0:T(8,128)(2,1)S(1)}, bf16[8,1152]{1,0:T(8,128)(2,1)S(1)}, bf16[8,1152]{1,0:T(8,128)(2,1)S(1)}, ...) custom-call(bf16[16,16,64,128]{3,2,1,0:T(8,128)(2,1)} %refs_0_.1, ...), custom_call_target="tpu_custom_call" | custom-call | flops 134217728 | bytes 4194304 | tf_op jit(solution)/shard_map/front/pallas_call | solution.py:363
  4.1 5.1 %collective-permute-start = (bf16[8,1152]{1,0:T(8,128)(2,1)S(1)}, bf16[8,1152]{1,0:T(8,128)(2,1)S(1)}, u32[]{:S(2)}, u32[]{:S(2)}) collective-permute-start(bf16[8,1152]{1,0:T(8,128)(2,1)S(1)} %get-tuple-element.31), channel_id=1, source_target_pairs={{0,12},{4,8},{8,4},{12,0},{1,13},{5,9},{9,5},{13,1},{2,14},{6,10},... | collective-permute-start | bytes 55304 | tf_op jit(solution)/shard_map/ppermute | solution.py:399
  9.2 0.0 collective-permute-start.1
  9.2 0.6 %collective-permute-start.2 = (bf16[8,1152]{1,0:T(8,128)(2,1)S(1)}, bf16[8,1152]{1,0:T(8,128)(2,1)S(1)}, u32[]{:S(2)}, u32[]{:S(2)}) collective-permute-start(bf16[8,1152]{1,0:T(8,128)(2,1)S(1)} %get-tuple-element.33), channel_id=1, source_target_pairs={{0,4},{4,0},{8,12},{12,8},{1,5},{5,1},{9,13},{13,9},{2,6},{6,2},{1... | collective-permute-start | bytes 55304 | tf_op jit(solution)/shard_map/ppermute | solution.py:399
  9.8 1.3 %state.1.made = bf16[16,16,64,128]{3,2,1,0:T(8,128)(2,1)S(1)} custom-call(bf16[1024,64]{1,0:T(8,128)(2,1)S(1)} %get-tuple-element.34.left, f32[32,128]{1,0:T(8,128)S(1)} %get-tuple-element.35.b, f32[16,16]{1,0:T(8,128)S(1)} %get-tuple-element.36.keep, bf16[16,16,64,128]{3,2,1,0:T(8,128)(2,1)S(1)} %get-tuple-element.37.state), custom_call_target="tpu_custom_call" | custom-call | flops 16777216 | bytes 8388608 | tf_op jit(solution)/shard_map/state/pallas_call | solution.py:421
  11.1 0.0 collective-permute-done.refs_1_
  11.1 2.7 %collective-permute-done.1.refs_2_ = bf16[8,1152]{1,0:T(8,128)(2,1)S(1)} collective-permute-done((bf16[8,1152]{1,0:T(8,128)(2,1)S(1)}, bf16[8,1152]{1,0:T(8,128)(2,1)S(1)}, u32[]{:S(2)}, u32[]{:S(2)}) %collective-permute-start.1) | collective-permute-done | bytes 18464 | tf_op jit(solution)/shard_map/ppermute | solution.py:399
  13.8 0.0 collective-permute-done.2.refs_3_
  13.8 0.2 down.1
  14.1 0.1 collective-permute-start.5
  14.2 1.6 %collective-permute-start.4 = (f32[32,128]{1,0:T(8,128)S(1)}, f32[32,128]{1,0:T(8,128)S(1)}, u32[]{:S(2)}, u32[]{:S(2)}) collective-permute-start(f32[32,128]{1,0:T(8,128)S(1)} %get-tuple-element.43.refs_0_), channel_id=1, source_target_pairs={{0,2},{1,3},{2,0},{3,1},{4,6},{5,7},{6,4},{7,5},{8,10},{9,11},{10,... | collective-permute-start | bytes 49160 | tf_op jit(solution)/shard_map/ppermute | solution.py:443
  15.7 0.3 %collective-permute-start.3 = (f32[32,128]{1,0:T(8,128)S(1)}, f32[32,128]{1,0:T(8,128)S(1)}, u32[]{:S(2)}, u32[]{:S(2)}) collective-permute-start(f32[32,128]{1,0:T(8,128)S(1)} %get-tuple-element.43.refs_0_), channel_id=1, source_target_pairs={{0,1},{1,0},{2,3},{3,2},{4,5},{5,4},{6,7},{7,6},{8,9},{9,8},{10,11... | collective-permute-start | bytes 49160 | tf_op jit(solution)/shard_map/ppermute | solution.py:443
  16.0 1.4 %collective-permute-done.5.refs_3_ = f32[32,128]{1,0:T(8,128)S(1)} collective-permute-done((f32[32,128]{1,0:T(8,128)S(1)}, f32[32,128]{1,0:T(8,128)S(1)}, u32[]{:S(2)}, u32[]{:S(2)}) %collective-permute-start.5) | collective-permute-done | bytes 16416 | tf_op jit(solution)/shard_map/ppermute | solution.py:443
  17.4 0.5 %collective-permute-done.4.refs_2_ = f32[32,128]{1,0:T(8,128)S(1)} collective-permute-done((f32[32,128]{1,0:T(8,128)S(1)}, f32[32,128]{1,0:T(8,128)S(1)}, u32[]{:S(2)}, u32[]{:S(2)}) %collective-permute-start.4) | collective-permute-done | bytes 16416 | tf_op jit(solution)/shard_map/ppermute | solution.py:443
  18.0 0.0 collective-permute-done.3.refs_1_
  18.0 0.2 up.1
  18.2 1.5 %collective-permute-start.6 = (bf16[8,1024]{1,0:T(8,128)(2,1)S(1)}, bf16[8,1024]{1,0:T(8,128)(2,1)S(1)}, u32[]{:S(2)}, u32[]{:S(2)}) collective-permute-start(bf16[8,1024]{1,0:T(8,128)(2,1)S(1)} %get-tuple-element.51), channel_id=1, source_target_pairs={{0,12},{4,8},{8,4},{12,0},{1,13},{5,9},{9,5},{13,1},{2,14},{6,10},... | collective-permute-start | bytes 49160 | tf_op jit(solution)/shard_map/ppermute | solution.py:399
  19.7 0.6 %collective-permute-start.7 = (bf16[8,1024]{1,0:T(8,128)(2,1)S(1)}, bf16[8,1024]{1,0:T(8,128)(2,1)S(1)}, u32[]{:S(2)}, u32[]{:S(2)}) collective-permute-start(bf16[8,1024]{1,0:T(8,128)(2,1)S(1)} %get-tuple-element.52), channel_id=1, source_target_pairs={{0,8},{4,12},{8,0},{12,4},{1,9},{5,13},{9,1},{13,5},{2,10},{6,14},... | collective-permute-start | bytes 49160 | tf_op jit(solution)/shard_map/ppermute | solution.py:399
  20.4 2.3 %collective-permute-start.8 = (bf16[8,1024]{1,0:T(8,128)(2,1)S(1)}, bf16[8,1024]{1,0:T(8,128)(2,1)S(1)}, u32[]{:S(2)}, u32[]{:S(2)}) collective-permute-start(bf16[8,1024]{1,0:T(8,128)(2,1)S(1)} %get-tuple-element.53), channel_id=1, source_target_pairs={{0,4},{4,0},{8,12},{12,8},{1,5},{5,1},{9,13},{13,9},{2,6},{6,2},{1... | collective-permute-start | bytes 49160 | tf_op jit(solution)/shard_map/ppermute | solution.py:399
  22.7 2.0 %close.1 = (bf16[2,16,1024]{2,1,0:T(8,128)(2,1)}, bf16[16,16,64,128]{3,2,1,0:T(8,128)(2,1)}) custom-call(f32[32,1024]{1,0:T(8,128)S(1)} %get-tuple-element.29.gated, f32[32,128]{1,0:T(8,128)S(1)} %get-tuple-element.45.inverse.refs_5_, f32[1,1024]{1,0:T(1,128)S(1)} %get-tuple-element.46.gain, bf16[16,16,64,128]{3,2,1,0:T(8,128)(2,1)S(1)} %state.1.made), custom_call_target="tpu_custom_call" | custom-call | flops 16777216 | bytes 8388608 | tf_op jit(solution)/shard_map/close/pallas_call | solution.py:461
  24.7 0.0 collective-permute-done.6.refs_1_
  24.7 0.0 collective-permute-done.7.refs_2_
  24.7 0.0 collective-permute-done.8.refs_3_
  24.7 0.8 %final.1 = f32[2,16,1024]{2,1,0:T(8,128)} custom-call(bf16[8,1024]{1,0:T(8,128)(2,1)S(1)} %get-tuple-element.50.refs_0_, bf16[8,1024]{1,0:T(8,128)(2,1)S(1)} %collective-permute-done.6.refs_1_, bf16[8,1024]{1,0:T(8,128)(2,1)S(1)} %collective-permute-done.7.refs_2_, bf16[8,1024]{1,0:T(8,128)(2,1)S(1)} %collective-permute-done.8.refs_3_, ...), custom_call_target="tpu_custom_call" | custom-call | tf_op jit(solution)/shard_map/final/pallas_call | solution.py:478
  (4 shorter events, 0.0 us)
Async XLA Ops:
  4.1 7.1 %collective-permute-start = (bf16[8,1152]{1,0:T(8,128)(2,1)S(1)}, bf16[8,1152]{1,0:T(8,128)(2,1)S(1)}, u32[]{:S(2)}, u32[]{:S(2)}) collective-permute-start(bf16[8,1152]{1,0:T(8,128)(2,1)S(1)} %get-tuple-element.31), channel_id=1, source_target_pairs={{0,12},{4,8},{8,4},{12,0},{1,13},{5,9},{9,5},{13,1},{2,14},{6,10},... | collective-permute-start | bytes 55304 | tf_op jit(solution)/shard_map/ppermute | solution.py:399
  9.2 4.7 %collective-permute-start.1 = (bf16[8,1152]{1,0:T(8,128)(2,1)S(1)}, bf16[8,1152]{1,0:T(8,128)(2,1)S(1)}, u32[]{:S(2)}, u32[]{:S(2)}) collective-permute-start(bf16[8,1152]{1,0:T(8,128)(2,1)S(1)} %get-tuple-element.32), channel_id=1, source_target_pairs={{0,8},{4,12},{8,0},{12,4},{1,9},{5,13},{9,1},{13,5},{2,10},{6,14},... | collective-permute-start | bytes 55304 | tf_op jit(solution)/shard_map/ppermute | solution.py:399
  9.2 4.7 %collective-permute-start.2 = (bf16[8,1152]{1,0:T(8,128)(2,1)S(1)}, bf16[8,1152]{1,0:T(8,128)(2,1)S(1)}, u32[]{:S(2)}, u32[]{:S(2)}) collective-permute-start(bf16[8,1152]{1,0:T(8,128)(2,1)S(1)} %get-tuple-element.33), channel_id=1, source_target_pairs={{0,4},{4,0},{8,12},{12,8},{1,5},{5,1},{9,13},{13,9},{2,6},{6,2},{1... | collective-permute-start | bytes 55304 | tf_op jit(solution)/shard_map/ppermute | solution.py:399
  9.8 4.0 %copy-start = (bf16[2,64,1024]{2,1,0:T(8,128)(2,1)S(1)}, bf16[2,64,1024]{2,1,0:T(8,128)(2,1)}, u32[]{:S(2)}) copy-start(bf16[2,64,1024]{2,1,0:T(8,128)(2,1)} %refs_4_.3) | copy-start | bytes 786436
  9.8 8.2 %copy-start.1 = (bf16[2,64,1024]{2,1,0:T(8,128)(2,1)S(1)}, bf16[2,64,1024]{2,1,0:T(8,128)(2,1)}, u32[]{:S(2)}) copy-start(bf16[2,64,1024]{2,1,0:T(8,128)(2,1)} %refs_5_.3) | copy-start | bytes 786436
  14.1 3.4 %collective-permute-start.5 = (f32[32,128]{1,0:T(8,128)S(1)}, f32[32,128]{1,0:T(8,128)S(1)}, u32[]{:S(2)}, u32[]{:S(2)}) collective-permute-start(f32[32,128]{1,0:T(8,128)S(1)} %get-tuple-element.43.refs_0_), channel_id=1, source_target_pairs={{0,3},{1,2},{2,1},{3,0},{4,7},{5,6},{6,5},{7,4},{8,11},{9,10},{10,... | collective-permute-start | bytes 49160 | tf_op jit(solution)/shard_map/ppermute | solution.py:443
  14.2 3.8 %collective-permute-start.4 = (f32[32,128]{1,0:T(8,128)S(1)}, f32[32,128]{1,0:T(8,128)S(1)}, u32[]{:S(2)}, u32[]{:S(2)}) collective-permute-start(f32[32,128]{1,0:T(8,128)S(1)} %get-tuple-element.43.refs_0_), channel_id=1, source_target_pairs={{0,2},{1,3},{2,0},{3,1},{4,6},{5,7},{6,4},{7,5},{8,10},{9,11},{10,... | collective-permute-start | bytes 49160 | tf_op jit(solution)/shard_map/ppermute | solution.py:443
  15.7 2.2 %collective-permute-start.3 = (f32[32,128]{1,0:T(8,128)S(1)}, f32[32,128]{1,0:T(8,128)S(1)}, u32[]{:S(2)}, u32[]{:S(2)}) collective-permute-start(f32[32,128]{1,0:T(8,128)S(1)} %get-tuple-element.43.refs_0_), channel_id=1, source_target_pairs={{0,1},{1,0},{2,3},{3,2},{4,5},{5,4},{6,7},{7,6},{8,9},{9,8},{10,11... | collective-permute-start | bytes 49160 | tf_op jit(solution)/shard_map/ppermute | solution.py:443
  18.2 6.5 %collective-permute-start.6 = (bf16[8,1024]{1,0:T(8,128)(2,1)S(1)}, bf16[8,1024]{1,0:T(8,128)(2,1)S(1)}, u32[]{:S(2)}, u32[]{:S(2)}) collective-permute-start(bf16[8,1024]{1,0:T(8,128)(2,1)S(1)} %get-tuple-element.51), channel_id=1, source_target_pairs={{0,12},{4,8},{8,4},{12,0},{1,13},{5,9},{9,5},{13,1},{2,14},{6,10},... | collective-permute-start | bytes 49160 | tf_op jit(solution)/shard_map/ppermute | solution.py:399
  19.7 5.0 %collective-permute-start.7 = (bf16[8,1024]{1,0:T(8,128)(2,1)S(1)}, bf16[8,1024]{1,0:T(8,128)(2,1)S(1)}, u32[]{:S(2)}, u32[]{:S(2)}) collective-permute-start(bf16[8,1024]{1,0:T(8,128)(2,1)S(1)} %get-tuple-element.52), channel_id=1, source_target_pairs={{0,8},{4,12},{8,0},{12,4},{1,9},{5,13},{9,1},{13,5},{2,10},{6,14},... | collective-permute-start | bytes 49160 | tf_op jit(solution)/shard_map/ppermute | solution.py:399
  20.4 4.4 %collective-permute-start.8 = (bf16[8,1024]{1,0:T(8,128)(2,1)S(1)}, bf16[8,1024]{1,0:T(8,128)(2,1)S(1)}, u32[]{:S(2)}, u32[]{:S(2)}) collective-permute-start(bf16[8,1024]{1,0:T(8,128)(2,1)S(1)} %get-tuple-element.53), channel_id=1, source_target_pairs={{0,4},{4,0},{8,12},{12,8},{1,5},{5,1},{9,13},{13,9},{2,6},{6,2},{1... | collective-permute-start | bytes 49160 | tf_op jit(solution)/shard_map/ppermute | solution.py:399
